TPU v7x, 32 devices: a whole 2x2x4 slice. The times are simulated.
32 devices in a mesh: group: 2 (over core), shard: 4 (over y, x), tensor: 4 (over z).
Axes of the slice: x: 2, y: 2, z: 4, core: 2. Of those that a mesh axis runs over, the one named last changes fastest.
Arguments:
- attn_in_local: bfloat16 [2, 768, 2304], P('group', 'shard', 'tensor'), may hold values from -6 to 6
- attn_out_local: bfloat16 [2, 768, 768], P('group', 'shard', 'tensor'), may hold values from -6 to 6
- ffn_in_local: bfloat16 [2, 768, 3072], P('group', 'shard', 'tensor'), may hold values from -6 to 6
- ffn_out_local: bfloat16 [2, 3072, 768], P('group', 'shard', 'tensor'), may hold values from -6 to 6
- small_local: bfloat16 [2, 1920], P('group'), may hold values from -6 to 6
- dense_old: float32 [16, 442368], P(('shard', 'tensor'), 'group'), may hold values from -6 to 6
- dense_momentum: float32 [16, 442368], P(('shard', 'tensor'), 'group'), may hold values from -6 to 6
- small_old: float32 [1920], P('group'), may hold values from -6 to 6
- small_momentum: float32 [1920], P('group'), may hold values from -6 to 6
- embed_local: bfloat16 [2, 768, 8192], P('group', 'shard', 'tensor'), may hold values from -6 to 6
- embed_old: float32 [768, 8192], P('shard', 'tensor'), may hold values from -6 to 6
- basis: float32 [768, 64], P('shard'), may hold values from -0.21875 to 0.21875
- coeff_momentum: float32 [64, 8192], P(None, 'tensor'), may hold values from -6 to 6
Outputs:
- attn_in_next: float32 [768, 2304], P('shard', 'tensor')
- attn_out_next: float32 [768, 768], P('shard', 'tensor')
- ffn_in_next: float32 [768, 3072], P('shard', 'tensor')
- ffn_out_next: float32 [3072, 768], P('shard', 'tensor')
- dense_momentum_next: float32 [16, 442368], P(('shard', 'tensor'), 'group')
- small_next: float32 [1920], replicated
- small_momentum_next: float32 [1920], P('group')
- embed_next: float32 [768, 8192], P('shard', 'tensor')
- coeff_momentum_next: float32 [64, 8192], P(None, 'tensor')
All inputs are finite; a program needn't handle non-finite values.
Results may differ from a plain program's by a relative error of at most 0.0003.
Values sent between devices are 32-bit elements; how exact they have to be, the bound alone decides.
No kernel may reach another device: no remote copies, remote signals or barrier semaphores. Data moves between devices by JAX's collectives and lax.ppermute only.
A program may use at most 64 MiB of HBM per device.

v0:
```python
import jax
import jax.numpy as jnp
from jax import lax
from jax.sharding import PartitionSpec as P

momentum_coef = 0.5
outer_rate = 0.7


def nesterov(old_value, momentum, delta):
    moved = momentum_coef * momentum + delta
    return (old_value - outer_rate * (delta + momentum_coef * moved), moved)


def shards(
    attn_in_local,
    attn_out_local,
    ffn_in_local,
    ffn_out_local,
    small_local,
    dense_old,
    dense_momentum,
    small_old,
    small_momentum,
    embed_local,
    embed_old,
    basis,
    coeff_momentum,
):
    groups = lax.axis_size("group")
    matrices = (attn_in_local, attn_out_local, ffn_in_local, ffn_out_local)
    local_terms = jnp.concatenate([matrix[0].reshape(-1) for matrix in matrices]).astype(
        jnp.float32
    )
    small_terms = small_local[0].astype(jnp.float32)
    old_flat = dense_old[0]
    momentum_flat = dense_momentum[0]
    dense_part, small_part = (
        lax.psum_scatter(local_terms, "group", scatter_dimension=0, tiled=True),
        lax.psum_scatter(small_terms, "group", scatter_dimension=0, tiled=True),
    )
    dense_new, dense_moved = nesterov(old_flat, momentum_flat, old_flat - dense_part / groups)
    small_new, small_moved = nesterov(small_old, small_momentum, small_old - small_part / groups)
    full_flat, small_next = (
        lax.all_gather(dense_new, "group", axis=0, tiled=True),
        lax.all_gather(small_new, "group", axis=0, tiled=True),
    )
    results = []
    offset = 0
    for matrix in matrices:
        block_size = matrix.shape[1] * matrix.shape[2]
        results.append(
            full_flat[offset : offset + block_size].reshape(matrix.shape[1], matrix.shape[2])
        )
        offset = offset + block_size
    difference = embed_old - embed_local[0].astype(jnp.float32)
    partial_coeff = lax.dot_general(
        basis,
        difference,
        (((0,), (0,)), ((), ())),
        precision=lax.Precision.HIGHEST,
        preferred_element_type=jnp.float32,
    )
    coeff = lax.psum(partial_coeff, ("group", "shard")) / groups
    coeff_moved = momentum_coef * coeff_momentum + coeff
    update = coeff + momentum_coef * coeff_moved
    embed_next = embed_old - outer_rate * jnp.dot(
        basis, update, precision=lax.Precision.HIGHEST, preferred_element_type=jnp.float32
    )
    return (
        results[0],
        results[1],
        results[2],
        results[3],
        dense_moved[None, :],
        small_next,
        small_moved,
        embed_next,
        coeff_moved,
    )


def solution(mesh):
    placed = (
        P("group", "shard", "tensor"),
        P("group", "shard", "tensor"),
        P("group", "shard", "tensor"),
        P("group", "shard", "tensor"),
        P("group", None),
        P(("shard", "tensor"), "group"),
        P(("shard", "tensor"), "group"),
        P("group"),
        P("group"),
        P("group", "shard", "tensor"),
        P("shard", "tensor"),
        P("shard", None),
        P(None, "tensor"),
    )
    return jax.shard_map(
        shards,
        mesh=mesh,
        in_specs=placed,
        out_specs=(
            P("shard", "tensor"),
            P("shard", "tensor"),
            P("shard", "tensor"),
            P("shard", "tensor"),
            P(("shard", "tensor"), "group"),
            P(),
            P("group"),
            P("shard", "tensor"),
            P(None, "tensor"),
        ),
        check_vma=False,
    )
```

profile of v0, /device:TPU:0, one launch (start us, length us, event | category | flops | bytes accessed | tf_op | source)
XLA Modules:
  0.0 118.1 jit_solution(13172482698302932152)
XLA Ops:
  7.2 0.0 all-reduce.8.cloned.1.call-start
  7.3 1.2 %copy.24 = bf16[1,768,192]{2,1,0:T(8,128)(2,1)S(1)} copy(bf16[1,768,192]{1,2,0:T(8,128)(2,1)} %param.16) | data formatting | bytes 589824 | tf_op args[3]
  8.5 0.5 reshape_squeeze.15
  9.0 1.2 %reshape_squeeze.14 = bf16[147456]{0:T(1024)(128)(2,1)S(1)} reshape(bf16[1,192,768]{2,1,0:T(8,128)(2,1)} %param.15) | data formatting | bytes 589824 | tf_op jit(solution)/shard_map/reshape;squeeze | solution.py:32
  10.2 0.3 reshape_squeeze.12
  10.5 0.2 reshape_squeeze.13
  10.7 1.3 %maximum_convert_fusion = f32[442368]{0:T(1024)} fusion(bf16[147456]{0:T(1024)(128)(2,1)S(1)} %reshape_squeeze.15, bf16[147456]{0:T(1024)(128)(2,1)S(1)} %reshape_squeeze.14, bf16[36864]{0:T(1024)(128)(2,1)S(1)} %reshape_squeeze.13, bf16[110592]{0:T(1024)(128)(2,1)S(1)} %reshape_squeeze.12), kind=kLoop, calls=%fused_computation.5 | loop fusion | flops 3538944 | bytes 2654208 | tf_op jit(solution)/shard_map/convert_element_type | solution.py:32
  12.0 0.0 all-reduce.8.cloned.1.call-update
  12.0 0.0 all-reduce.6.cloned.1.call-start
  12.1 0.6 copy-done.1
  12.7 0.5 copy-done.5
  13.3 1.9 %convolution_bitcast_fusion = f32[64,2048]{1,0:T(8,128)} fusion(f32[192,64]{0,1:T(8,128)S(1)} %copy-done, f32[192,2048]{1,0:T(8,128)S(1)} %copy-done.1, bf16[1,192,2048]{2,1,0:T(8,128)(2,1)S(1)} %copy-done.5), kind=kOutput, calls=%fused_computation.3 | convolution fusion | flops 302776320 | bytes 2932736 | tf_op jit(solution)/shard_map/dot_general | solution.py:57
  15.1 0.0 all-gather.2.cloned.1.call-start
  15.2 0.8 broadcast_multiply_fusion
  16.1 0.6 fusion.13
  17.3 18.3 %all-reduce.8.cloned.1.call-done = f32[442368]{0:T(1024)} async-done(((f32[442368]{0:T(1024)}), f32[442368]{0:T(1024)}) %all-reduce.8.cloned.1.call-update) | async-done | bytes 1769488
  35.6 2.9 %multiply_subtract_fusion = (f32[221184]{0:T(1024)}, f32[221184]{0:T(1024)}) fusion(f32[221184]{0:T(1024)} %bitcast.20, f32[442368]{0:T(1024)} %all-reduce.8.cloned.1.call-done, u32[]{:T(128)S(6)} %multiply.7, f32[221184]{0:T(1024)S(1)} %bitcast.19), kind=kLoop, calls=%fused_computation.8 | loop fusion | flops 1548288 | bytes 4423684 | tf_op jit(solution)/shard_map/sub | solution.py:12
  38.5 0.0 all-gather.2.cloned.1.call-update
  39.9 2.5 %all-reduce.2 = f32[1920]{0:T(1024)S(1)} all-reduce(f32[1920]{0:T(1024)S(1)} %convert_reduce_fusion), channel_id=3, replica_groups=mesh['group'=2,'shard'=4,'tensor'=4] {'group'}, use_global_device_ids=true, to_apply=%region_1.0.clone | all-reduce | flops 1920 | bytes 15360
  42.4 0.7 subtract_dynamic-update-slice_fusion
  43.1 3.0 %all-reduce = f32[1920]{0:T(1024)} all-reduce(f32[1920]{0:T(1024)S(1)} %get-tuple-element.27), channel_id=1, replica_groups=mesh['group'=2,'shard'=4,'tensor'=4] {'group'}, use_global_device_ids=true, to_apply=%add | all-reduce | flops 1920 | bytes 15360
  46.2 49.1 %all-reduce.6.cloned.1.call-done = f32[64,2048]{1,0:T(8,128)} async-done(((f32[64,2048]{1,0:T(8,128)}), f32[64,2048]{1,0:T(8,128)}) %all-reduce.6.cloned.1.call-update) | async-done | bytes 524304 | tf_op jit(solution)/shard_map/psum | solution.py:64
  95.3 1.2 multiply_add_fusion
  96.5 0.0 copy-done.2
  96.5 2.6 %fusion.1 = f32[192,2048]{1,0:T(8,128)} fusion(f32[192,2048]{1,0:T(8,128)S(1)} %copy-done.1, f32[192,64]{0,1:T(8,128)S(1)} %copy-done, f32[64,2048]{1,0:T(8,128)S(1)} %multiply_add_fusion, f32[64,2048]{1,0:T(8,128)S(1)} %copy-done.2), kind=kOutput, calls=%fused_computation.2 | convolution fusion | flops 303169536 | bytes 4243456 | tf_op jit(solution)/shard_map/dot_general | solution.py:67
  99.2 7.1 %all-gather.2.cloned.1.call-done = f32[442368]{0:T(1024)} async-done(((f32[221184]{0:T(1024)}), f32[442368]{0:T(1024)}) %all-gather.2.cloned.1.call-update) | async-done | bytes 1769488 | tf_op jit(solution)/shard_map/all_gather | solution.py:45
  106.3 1.3 %fusion.12 = (f32[147456]{0:T(1024)S(1)}, f32[147456]{0:T(1024)S(1)}) fusion(f32[442368]{0:T(1024)} %all-gather.2.cloned.1.call-done), kind=kLoop, calls=%fused_computation.23 | loop fusion | bytes 2359296 | tf_op jit(solution)/shard_map/slice | solution.py:53
  107.6 0.2 slice.59
  107.8 1.1 copy.25
  108.9 0.9 slice.57
  109.8 0.9 slice.53
  110.8 0.8 slice.55
  (30 shorter events, 0.1 us)
Async XLA Ops:
  7.2 4.9 %copy-start = (f32[192,64]{0,1:T(8,128)S(1)}, f32[192,64]{0,1:T(8,128)}, u32[]{:S(2)}) copy-start(f32[192,64]{0,1:T(8,128)} %param.24) | copy-start | bytes 147460
  7.2 3.0 %copy-start.7 = (bf16[1,192,576]{2,1,0:T(8,128)(2,1)S(1)}, bf16[1,192,576]{2,1,0:T(8,128)(2,1)}, u32[]{:S(2)}) copy-start(bf16[1,192,576]{2,1,0:T(8,128)(2,1)} %param.13) | copy-start | bytes 663556
  7.2 3.3 %copy-start.8 = (bf16[1,192,192]{2,1,0:T(8,128)(2,1)S(1)}, bf16[1,192,192]{2,1,0:T(8,128)(2,1)}, u32[]{:S(2)}) copy-start(bf16[1,192,192]{2,1,0:T(8,128)(2,1)} %param.14) | copy-start | bytes 221188
  7.2 28.4 %all-reduce.8.cloned.1.call-start = ((), (), s32[]{:S(2)}) async-start(), calls=%async_computation.2 | async-start | bytes 3538944
  10.7 2.0 %copy-start.1 = (f32[192,2048]{1,0:T(8,128)S(1)}, f32[192,2048]{1,0:T(8,128)}, u32[]{:S(2)}) copy-start(f32[192,2048]{1,0:T(8,128)} %param.23) | copy-start | bytes 4718596
  12.0 1.3 %copy-start.5 = (bf16[1,192,2048]{2,1,0:T(8,128)(2,1)S(1)}, bf16[1,192,2048]{2,1,0:T(8,128)(2,1)}, u32[]{:S(2)}) copy-start(bf16[1,192,2048]{2,1,0:T(8,128)(2,1)} %param.22) | copy-start | bytes 2359300
  12.0 3.2 %copy-start.4 = (f32[1,221184]{1,0:T(1,128)S(1)}, f32[1,221184]{1,0:T(1,128)}, u32[]{:S(2)}) copy-start(f32[1,221184]{1,0:T(1,128)} %param.19) | copy-start | bytes 2654212
  12.0 83.3 %all-reduce.6.cloned.1.call-start = ((), (), s32[]{:S(2)}) async-start(), calls=%async_computation.1 | async-start | bytes 1048576 | tf_op jit(solution)/shard_map/psum | solution.py:64
  15.1 0.9 copy-start.12
  15.1 91.1 %all-gather.2.cloned.1.call-start = ((), (), s32[]{:S(2)}) async-start(), calls=%async_computation | async-start | bytes 2654208 | tf_op jit(solution)/shard_map/all_gather | solution.py:45
  35.6 4.3 %copy-start.9 = (bf16[1,1920]{1,0:T(2,128)(2,1)S(1)}, bf16[1,1920]{1,0:T(2,128)(2,1)}, u32[]{:S(2)}) copy-start(bf16[1,1920]{1,0:T(2,128)(2,1)} %param.17) | copy-start | bytes 11524
  35.6 6.8 %copy-start.10 = (f32[960]{0:T(1024)S(1)}, f32[960]{0:T(1024)}, u32[]{:S(2)}) copy-start(f32[960]{0:T(1024)} %param.20) | copy-start | bytes 11524
  35.6 6.8 %copy-start.11 = (f32[960]{0:T(1024)S(1)}, f32[960]{0:T(1024)}, u32[]{:S(2)}) copy-start(f32[960]{0:T(1024)} %param.21) | copy-start | bytes 11524
  35.6 59.7 %copy-start.6 = (f32[64,2048]{1,0:T(8,128)S(1)}, f32[64,2048]{1,0:T(8,128)}, u32[]{:S(2)}) copy-start(f32[64,2048]{1,0:T(8,128)} %param.25) | copy-start | bytes 1572868
  95.3 1.2 %copy-start.2 = (f32[64,2048]{1,0:T(8,128)S(1)}, f32[64,2048]{1,0:T(8,128)}, u32[]{:S(2)}) copy-start(f32[64,2048]{1,0:T(8,128)} %all-reduce.6.cloned.1.call-done) | copy-start | bytes 1572868
  96.5 2.6 %copy-start.3 = (f32[64,2048]{1,0:T(8,128)}, f32[64,2048]{1,0:T(8,128)S(1)}, u32[]{:S(2)}) copy-start(f32[64,2048]{1,0:T(8,128)S(1)} %multiply_add_fusion) | copy-start | bytes 1572868
  107.8 2.0 %slice-start = ((f32[442368]{0:T(1024)}), f32[110592]{0:T(1024)S(1)}, s32[]{:S(2)}) async-start(f32[442368]{0:T(1024)} %all-gather.2.cloned.1.call-done), calls=%async_computation.3 | async-start | bytes 884736 | tf_op jit(solution)/shard_map/slice | solution.py:53
  108.9 1.9 %slice-start.1 = ((f32[442368]{0:T(1024)}), f32[36864]{0:T(1024)S(1)}, s32[]{:S(2)}) async-start(f32[442368]{0:T(1024)} %all-gather.2.cloned.1.call-done), calls=%async_computation.4 | async-start | bytes 294912 | tf_op jit(solution)/shard_map/slice | solution.py:53
Sparse Core Ops, SparseCore 0:
  12.2 23.3 all-reduce.7
  39.5 55.7 all-reduce.5
  96.9 9.3 all-gather.1
where the time goes:
time: 118 us
  waiting for transfers between devices  74.6 us (63%)
  between operations  15.9 us (13%)
  local copies, waits for them, and re-layouts  10.4 us (9%)
  other arithmetic  6.97 us (6%)
  blocking collectives  5.55 us (5%)
  matrix products  4.5 us (4%)
    psum x1, waiting for transfers between devices, shards(): coeff = lax.psum(partial_coeff, ('group', 'shard')) / groups  49.1 us
    unnamed x4, waiting for transfers between devices  18.3 us
    all_gather x1, waiting for transfers between devices, shards(): lax.all_gather(dense_new, 'group', axis=0, tiled=True)  7.14 us
    unnamed x2, blocking collectives  5.55 us
    slice x9, local copies, waits for them, and re-layouts, shards(): full_flat[offset:offset + block_size]  4.16 us
    unnamed x30, local copies, waits for them, and re-layouts  4.13 us
    sub x1, other arithmetic, nesterov(): return (old_value - outer_rate * (delta + momentum_coef * moved), moved)  2.93 us
    dot_general x1, matrix products, shards(): jnp.dot(basis, update, precision=lax.Precision.HIGHEST, preferred_element...  2.64 us
  transfers between devices with their start and end apart: 3, of which 3 were waited for; matrix products, arithmetic and copies ran while one was open for 9% of the time, Pallas kernels for 0%

commit v1 on v0

--- a/solution.py
+++ b/solution.py
@@ -1,10 +1,17 @@
 import jax
 import jax.numpy as jnp
 from jax import lax
+from jax.experimental import pallas as pl
+from jax.experimental.pallas import tpu as pltpu
 from jax.sharding import PartitionSpec as P
 
 momentum_coef = 0.5
 outer_rate = 0.7
+
+f32 = jnp.float32
+bf16 = jnp.bfloat16
+LANES = 128
+HALF = LANES // 2
 
 
 def nesterov(old_value, momentum, delta):
@@ -12,7 +19,7 @@
     return (old_value - outer_rate * (delta + momentum_coef * moved), moved)
 
 
-def shards(
+def general(
     attn_in_local,
     attn_out_local,
     ffn_in_local,
@@ -29,10 +36,8 @@
 ):
     groups = lax.axis_size("group")
     matrices = (attn_in_local, attn_out_local, ffn_in_local, ffn_out_local)
-    local_terms = jnp.concatenate([matrix[0].reshape(-1) for matrix in matrices]).astype(
-        jnp.float32
-    )
-    small_terms = small_local[0].astype(jnp.float32)
+    local_terms = jnp.concatenate([matrix[0].reshape(-1) for matrix in matrices]).astype(f32)
+    small_terms = small_local[0].astype(f32)
     old_flat = dense_old[0]
     momentum_flat = dense_momentum[0]
     dense_part, small_part = (
@@ -53,19 +58,19 @@
             full_flat[offset : offset + block_size].reshape(matrix.shape[1], matrix.shape[2])
         )
         offset = offset + block_size
-    difference = embed_old - embed_local[0].astype(jnp.float32)
+    difference = embed_old - embed_local[0].astype(f32)
     partial_coeff = lax.dot_general(
         basis,
         difference,
         (((0,), (0,)), ((), ())),
         precision=lax.Precision.HIGHEST,
-        preferred_element_type=jnp.float32,
+        preferred_element_type=f32,
     )
     coeff = lax.psum(partial_coeff, ("group", "shard")) / groups
     coeff_moved = momentum_coef * coeff_momentum + coeff
     update = coeff + momentum_coef * coeff_moved
     embed_next = embed_old - outer_rate * jnp.dot(
-        basis, update, precision=lax.Precision.HIGHEST, preferred_element_type=jnp.float32
+        basis, update, precision=lax.Precision.HIGHEST, preferred_element_type=f32
     )
     return (
         results[0],
@@ -77,6 +82,468 @@
         small_moved,
         embed_next,
         coeff_moved,
+    )
+
+
+local_coef = outer_rate * (1 + momentum_coef) / 2
+old_coef = 1 - outer_rate * (1 + momentum_coef)
+mom_coef = -outer_rate * momentum_coef * momentum_coef
+
+
+def split(value):
+    high = value.astype(bf16)
+    return high, (value - high.astype(f32)).astype(bf16)
+
+
+def partial_kernel(group_ref, basis_ref, local_ref, old_ref, out_ref):
+    del group_ref
+    rank = basis_ref.shape[0]
+    high, low = split(basis_ref[...])
+    both = jnp.concatenate([high, low], axis=0)
+    diff_high, diff_low = split(old_ref[...] - local_ref[...].astype(f32))
+    first = jnp.dot(both, diff_high, preferred_element_type=f32)
+    second = jnp.dot(high, diff_low, preferred_element_type=f32)
+    out_ref[...] = first[:rank] + first[rank:] + second
+
+
+def partial_coeff(group, basis_t, local, old, other):
+    rank, depth = basis_t.shape
+    columns = old.shape[1] // 2
+    steps = 2
+    block = columns // steps
+
+    def half(step, group_ref):
+        side = 1 - group_ref[0] if other else group_ref[0]
+        return (0, side * steps + step)
+
+    return pl.pallas_call(
+        partial_kernel,
+        grid_spec=pltpu.PrefetchScalarGridSpec(
+            num_scalar_prefetch=1,
+            grid=(steps,),
+            in_specs=[
+                pl.BlockSpec((rank, depth), lambda step, group_ref: (0, 0)),
+                pl.BlockSpec((depth, block), half),
+                pl.BlockSpec((depth, block), half),
+            ],
+            out_specs=pl.BlockSpec((rank, block), lambda step, group_ref: (0, step)),
+        ),
+        out_shape=jax.ShapeDtypeStruct((rank, columns), f32),
+        cost_estimate=pl.CostEstimate(
+            flops=6 * rank * depth * columns, bytes_accessed=6 * depth * columns, transcendentals=0
+        ),
+        name="partial_coeff",
+    )(group, basis_t, local, old)
+
+
+def embed_kernel(group_ref, basis_ref, coeff_ref, moment_ref, old_ref, *refs):
+    del group_ref
+    embed_ref, moved_ref = refs[-2:]
+    moved = momentum_coef * moment_ref[...] + coeff_ref[...]
+    moved_ref[...] = moved
+    update = coeff_ref[...] + momentum_coef * moved
+    high, low = split(basis_ref[...])
+    up_high, up_low = split(update)
+    product = lax.dot_general(
+        jnp.concatenate([high, low, high], axis=0),
+        jnp.concatenate([up_high, up_high, up_low], axis=0),
+        (((0,), (0,)), ((), ())),
+        preferred_element_type=f32,
+    )
+    embed_ref[...] = old_ref[...] - outer_rate * product
+
+
+def embed_half(group, basis_t, coeff, moment, old, before):
+    rank, depth = basis_t.shape
+    width = old.shape[1]
+    columns = width // 2
+    steps = 2
+    block = columns // steps
+
+    def half(step, group_ref):
+        side = group_ref[0] if before is None else 1 - group_ref[0]
+        return (0, side * steps + step)
+
+    more = () if before is None else before
+    return pl.pallas_call(
+        embed_kernel,
+        grid_spec=pltpu.PrefetchScalarGridSpec(
+            num_scalar_prefetch=1,
+            grid=(steps,),
+            in_specs=[
+                pl.BlockSpec((rank, depth), lambda step, group_ref: (0, 0)),
+                pl.BlockSpec((rank, block), lambda step, group_ref: (0, step)),
+                pl.BlockSpec((rank, block), half),
+                pl.BlockSpec((depth, block), half),
+            ]
+            + [pl.BlockSpec(memory_space=pl.ANY)] * len(more),
+            out_specs=[pl.BlockSpec((depth, block), half), pl.BlockSpec((rank, block), half)],
+        ),
+        out_shape=[
+            jax.ShapeDtypeStruct((depth, width), f32),
+            jax.ShapeDtypeStruct((rank, width), f32),
+        ],
+        input_output_aliases={} if before is None else {5: 0, 6: 1},
+        cost_estimate=pl.CostEstimate(
+            flops=6 * rank * depth * columns, bytes_accessed=8 * depth * columns, transcendentals=0
+        ),
+        name="embed_half",
+    )(group, basis_t, coeff, moment, old, *more)
+
+
+def low_lanes(rows):
+    return lax.broadcasted_iota(jnp.int32, (rows, LANES), 1) < HALF
+
+
+def turn(value):
+    return pltpu.roll(value, HALF, 1)
+
+
+def attn_tiles(in_ref, out_ref):
+    whole = in_ref.shape[-1] // LANES
+    tiles = [in_ref[0, :, k * LANES : (k + 1) * LANES].astype(f32) for k in range(whole)]
+    last = in_ref[0, :, whole * LANES :].astype(f32)
+    side = out_ref[0, :, LANES:].astype(f32)
+    tiles.append(jnp.concatenate([last, side], axis=-1))
+    tiles.append(out_ref[0, :, :LANES].astype(f32))
+    return tiles
+
+
+def unflatten_attn(flat, put, rows):
+    pairs = rows // 2
+    low = low_lanes(pairs)
+    inner = [flat(j, pairs, 9) for j in range(9)]
+    base = pairs * 9
+    outer = [flat(base + j, pairs, 3) for j in range(3)]
+    turned = [turn(inner[j]) for j in range(4, 9)]
+    turned_out = [turn(outer[j]) for j in (1, 2)]
+    for k in range(4):
+        put(0, k, inner[k])
+        put(1, k, jnp.where(low, turned[k], turned[k + 1]))
+    put(0, 4, jnp.where(low, inner[4], turned_out[0]))
+    put(1, 4, jnp.where(low, turned[4], outer[2]))
+    put(0, 5, outer[0])
+    put(1, 5, jnp.where(low, turned_out[0], turned_out[1]))
+
+
+def flatten_attn(get, rows):
+    pairs = rows // 2
+    low = low_lanes(pairs)
+    even = [get(0, k) for k in range(6)]
+    odd = [get(1, k) for k in range(6)]
+    turned = [turn(odd[k]) for k in range(5)]
+    pieces = [(k, 9, even[k]) for k in range(4)]
+    pieces.append((4, 9, jnp.where(low, even[4], turned[0])))
+    for k in range(4):
+        pieces.append((5 + k, 9, jnp.where(low, turned[k], turned[k + 1])))
+    base = pairs * 9
+    pieces.append((base, 3, even[5]))
+    turned_out = turn(odd[5])
+    pieces.append((base + 1, 3, jnp.where(low, turn(even[4]), turned_out)))
+    pieces.append((base + 2, 3, jnp.where(low, turned_out, odd[4])))
+    return pieces
+
+
+def before_kernel(
+    group_ref, in_ref, out_ref, up_ref, down_ref, old_ref, mom_ref, small_ref, small_old_ref,
+    small_mom_ref, send_ref, wide_ref,
+):
+    rows = up_ref.shape[1]
+    mid = rows // 2
+    block = rows + mid
+    tiles = up_ref.shape[2] // LANES
+    small = small_old_ref.shape[1]
+
+    def flat(start, count, stride):
+        at = pl.ds(start, count, stride=stride)
+        return old_coef * old_ref[at, :] + mom_coef * mom_ref[at, :]
+
+    def put(start, tile, value):
+        send_ref[tile, pl.ds(block + start, rows // 2, stride=2), :] = value
+
+    def put_small(other, own):
+        own_terms = (
+            old_coef * small_old_ref[...] + mom_coef * small_mom_ref[...] + local_coef * own
+        )
+        send_ref[:, 2 * block :, :] = jnp.zeros((tiles, 8, LANES), f32)
+        for tile, value in enumerate((other, own_terms)):
+            for row in range(pl.cdiv(small, LANES)):
+                piece = value[:, row * LANES : (row + 1) * LANES]
+                at = 2 * block + row
+                send_ref[tile, at : at + 1, : piece.shape[1]] = piece
+
+    @pl.when(group_ref[0] == 0)
+    def _():
+        unflatten_attn(flat, put, rows)
+        for k, value in enumerate(attn_tiles(in_ref, out_ref)):
+            send_ref[k, block : block + rows, :] += local_coef * value
+        base = rows * tiles
+        for k in range(tiles):
+            columns = slice(k * LANES, (k + 1) * LANES)
+            send_ref[k, :mid, :] = up_ref[0, mid:, columns].astype(f32)
+            send_ref[k, mid:block, :] = down_ref[0, :, columns].astype(f32)
+            send_ref[k, block + rows : 2 * block, :] = flat(base + k, mid, tiles) + (
+                local_coef * up_ref[0, :mid, columns].astype(f32)
+            )
+        values = small_ref[...].astype(f32)
+        put_small(values[:, small:], values[:, :small])
+
+    @pl.when(group_ref[0] == 1)
+    def _():
+        for k, value in enumerate(attn_tiles(in_ref, out_ref)):
+            send_ref[k, :rows, :] = value
+        for k in range(tiles):
+            columns = slice(k * LANES, (k + 1) * LANES)
+            send_ref[k, rows:block, :] = up_ref[0, :mid, columns].astype(f32)
+            send_ref[k, block : block + mid, :] = flat(k, mid, tiles) + (
+                local_coef * up_ref[0, mid:, columns].astype(f32)
+            )
+        base = mid * tiles
+        pairs = tiles * HALF
+        low = low_lanes(pairs)
+        first, second, third = (flat(base + j, pairs, 3) for j in range(3))
+        turned, turned_more = turn(second), turn(third)
+        even, odd = pl.ds(0, pairs, stride=2), pl.ds(1, pairs, stride=2)
+        wide_ref[0, even, :] = first
+        wide_ref[1, even, :] = second
+        wide_ref[0, odd, :] = jnp.where(low, turned, turned_more)
+        wide_ref[1, odd, :] = turned_more
+        start = block + mid
+        for k in range(tiles):
+            columns = slice(k * LANES, (k + 1) * LANES)
+            upper = wide_ref[0, columns, :].T
+            lower = wide_ref[1, columns, :].T[:HALF]
+            send_ref[k, start : start + LANES, :] = upper + (
+                local_coef * down_ref[0, :LANES, columns].astype(f32)
+            )
+            send_ref[k, start + LANES : 2 * block, :] = lower + (
+                local_coef * down_ref[0, LANES:, columns].astype(f32)
+            )
+        values = small_ref[...].astype(f32)
+        put_small(values[:, :small], values[:, small:])
+
+
+def after_kernel(
+    group_ref, recv_ref, send_ref, in_ref, out_ref, up_ref, down_ref, old_ref, mom_ref, small_ref,
+    small_old_ref, small_mom_ref, in_next_ref, out_next_ref, up_next_ref, down_next_ref, moved_ref,
+    small_next_ref, small_moved_ref, sum_ref, wide_ref,
+):
+    rows = up_ref.shape[1]
+    mid = rows // 2
+    block = rows + mid
+    tiles = up_ref.shape[2] // LANES
+    small = small_old_ref.shape[1]
+
+    def put_moved(start, stride, value):
+        at = pl.ds(start, value.shape[0], stride=stride)
+        moved_ref[at, :] = momentum_coef * mom_ref[at, :] + (old_ref[at, :] - 0.5 * value)
+
+    def get(start, tile):
+        return sum_ref[tile, pl.ds(start, rows // 2, stride=2), :]
+
+    def put_attn(tile, value):
+        whole = in_ref.shape[-1] // LANES
+        if tile < whole:
+            in_next_ref[:, tile * LANES : (tile + 1) * LANES] = value
+        elif tile == whole:
+            in_next_ref[:, tile * LANES :] = value[:, :HALF]
+            out_next_ref[:, LANES:] = turn(value)[:, :HALF]
+        else:
+            out_next_ref[:, :LANES] = value
+
+    def small_row(ref, tile):
+        pieces = []
+        for row in range(pl.cdiv(small, LANES)):
+            at = 2 * block + row
+            pieces.append(ref[tile, at : at + 1, : min(LANES, small - row * LANES)])
+        return jnp.concatenate(pieces, axis=1)
+
+    def put_small(other, own, first):
+        theirs = small_row(recv_ref, 0)
+        mine = small_row(send_ref, 1) + local_coef * theirs
+        rest = small_row(recv_ref, 1) + local_coef * other
+        both = [mine, rest] if first else [rest, mine]
+        small_next_ref[...] = jnp.concatenate(both, axis=1)
+        small_moved_ref[...] = momentum_coef * small_mom_ref[...] + (
+            small_old_ref[...] - 0.5 * (own + theirs)
+        )
+
+    @pl.when(group_ref[0] == 0)
+    def _():
+        for k, value in enumerate(attn_tiles(in_ref, out_ref)):
+            theirs = recv_ref[k, :rows, :]
+            put_attn(k, send_ref[k, block : block + rows, :] + local_coef * theirs)
+            sum_ref[k, :, :] = value + theirs
+        for start, stride, value in flatten_attn(get, rows):
+            put_moved(start, stride, value)
+        base = rows * tiles
+        for k in range(tiles):
+            columns = slice(k * LANES, (k + 1) * LANES)
+            theirs = recv_ref[k, rows:block, :]
+            up_next_ref[:mid, columns] = (
+                send_ref[k, block + rows : 2 * block, :] + local_coef * theirs
+            )
+            put_moved(base + k, tiles, up_ref[0, :mid, columns].astype(f32) + theirs)
+            up_next_ref[mid:, columns] = recv_ref[k, block : block + mid, :] + (
+                local_coef * up_ref[0, mid:, columns].astype(f32)
+            )
+            down_next_ref[:, columns] = recv_ref[k, block + mid : 2 * block, :] + (
+                local_coef * down_ref[0, :, columns].astype(f32)
+            )
+        values = small_ref[...].astype(f32)
+        put_small(values[:, small:], values[:, :small], True)
+
+    @pl.when(group_ref[0] == 1)
+    def _():
+        for k, value in enumerate(attn_tiles(in_ref, out_ref)):
+            put_attn(k, recv_ref[k, block : block + rows, :] + local_coef * value)
+        for k in range(tiles):
+            columns = slice(k * LANES, (k + 1) * LANES)
+            up_next_ref[:mid, columns] = recv_ref[k, block + rows : 2 * block, :] + (
+                local_coef * up_ref[0, :mid, columns].astype(f32)
+            )
+            theirs = recv_ref[k, :mid, :]
+            up_next_ref[mid:, columns] = send_ref[k, block : block + mid, :] + local_coef * theirs
+            put_moved(k, tiles, up_ref[0, mid:, columns].astype(f32) + theirs)
+            theirs = recv_ref[k, mid:block, :]
+            down_next_ref[:, columns] = (
+                send_ref[k, block + mid : 2 * block, :] + local_coef * theirs
+            )
+            total = down_ref[0, :, columns].astype(f32) + theirs
+            wide_ref[0, columns, :] = total[:LANES].T
+            lower = jnp.concatenate([total[LANES:], total[LANES:]], axis=0)
+            wide_ref[1, columns, :] = lower.T
+        base = mid * tiles
+        pairs = tiles * HALF
+        low = low_lanes(pairs)
+        even, odd = pl.ds(0, pairs, stride=2), pl.ds(1, pairs, stride=2)
+        odd_first = turn(wide_ref[0, odd, :])
+        put_moved(base, 3, wide_ref[0, even, :])
+        put_moved(base + 1, 3, jnp.where(low, wide_ref[1, even, :], odd_first))
+        put_moved(base + 2, 3, jnp.where(low, odd_first, wide_ref[1, odd, :]))
+        values = small_ref[...].astype(f32)
+        put_small(values[:, :small], values[:, small:], False)
+
+
+WHOLE = pl.BlockSpec(memory_space=pltpu.VMEM)
+SCALAR = pl.BlockSpec(memory_space=pltpu.SMEM)
+
+
+def dense_before(group, matrices, flats, smalls):
+    _, rows, width = matrices[2].shape
+    return pl.pallas_call(
+        before_kernel,
+        in_specs=[SCALAR] + [WHOLE] * 9,
+        out_specs=WHOLE,
+        out_shape=jax.ShapeDtypeStruct((width // LANES, 3 * rows + 8, LANES), f32),
+        scratch_shapes=[pltpu.VMEM((2, width, LANES), f32)],
+        compiler_params=pltpu.CompilerParams(vmem_limit_bytes=20 * 2**20),
+        cost_estimate=pl.CostEstimate(
+            flops=9 * rows * width, bytes_accessed=30 * rows * width, transcendentals=0
+        ),
+        name="dense_before",
+    )(group, *matrices, *flats, *smalls)
+
+
+def dense_after(group, received, sent, matrices, flats, smalls):
+    _, rows, width = matrices[2].shape
+    outs = [matrix.shape[1:] for matrix in matrices]
+    outs += [flats[0].shape, smalls[0].shape, smalls[1].shape]
+    return pl.pallas_call(
+        after_kernel,
+        in_specs=[SCALAR] + [WHOLE] * 11,
+        out_specs=[WHOLE] * 7,
+        out_shape=[jax.ShapeDtypeStruct(shape, f32) for shape in outs],
+        scratch_shapes=[
+            pltpu.VMEM((width // LANES, rows, LANES), f32),
+            pltpu.VMEM((2, width, LANES), f32),
+        ],
+        compiler_params=pltpu.CompilerParams(vmem_limit_bytes=24 * 2**20),
+        cost_estimate=pl.CostEstimate(
+            flops=9 * rows * width, bytes_accessed=40 * rows * width, transcendentals=0
+        ),
+        name="dense_after",
+    )(group, received, sent, *matrices, *flats, *smalls)
+
+
+def paired(
+    attn_in_local,
+    attn_out_local,
+    ffn_in_local,
+    ffn_out_local,
+    small_local,
+    dense_old,
+    dense_momentum,
+    small_old,
+    small_momentum,
+    embed_local,
+    embed_old,
+    basis,
+    coeff_momentum,
+):
+    position = lax.axis_index("group")
+    group = position.astype(jnp.int32).reshape(1)
+    swap = [(0, 1), (1, 0)]
+    shards_count = lax.axis_size("shard")
+    near = [(i, i ^ 1) for i in range(shards_count)]
+    far = [(i, i ^ 2) for i in range(shards_count)]
+
+    basis_t = basis.T
+    local = embed_local[0]
+    theirs = partial_coeff(group, basis_t, local, embed_old, True)
+    theirs = lax.ppermute(theirs, "group", swap)
+    mine = partial_coeff(group, basis_t, local, embed_old, False)
+    columns = mine.shape[1] // 2
+
+    matrices = (attn_in_local, attn_out_local, ffn_in_local, jnp.swapaxes(ffn_out_local, 1, 2))
+    flats = (dense_old.reshape(-1, LANES), dense_momentum.reshape(-1, LANES))
+    smalls = (small_local, small_old[None, :], small_momentum[None, :])
+    sent = dense_before(group, matrices, flats, smalls)
+    received = lax.ppermute(sent, "group", swap)
+    dense = dense_after(group, received, sent, matrices, flats, smalls)
+
+    left = mine[:, :columns] + theirs[:, :columns]
+    right = mine[:, columns:] + theirs[:, columns:]
+    left, right = (
+        left + lax.ppermute(left, "shard", near),
+        right + lax.ppermute(right, "shard", far),
+    )
+    left, right = (
+        left + lax.ppermute(left, "shard", far),
+        right + lax.ppermute(right, "shard", near),
+    )
+    own = 0.5 * jnp.concatenate([left, right], axis=1)
+    rest = lax.ppermute(own, "group", swap)
+    done = embed_half(group, basis_t, own, coeff_momentum, embed_old, None)
+    embed_next, coeff_moved = embed_half(group, basis_t, rest, coeff_momentum, embed_old, done)
+
+    attn_in_next, attn_out_next, ffn_in_next, ffn_out_next, moved, small_next, small_moved = dense
+    return (
+        attn_in_next,
+        attn_out_next,
+        ffn_in_next,
+        ffn_out_next.T,
+        moved.reshape(dense_old.shape),
+        small_next[0],
+        small_moved[0],
+        embed_next,
+        coeff_moved,
+    )
+
+
+def is_paired(mesh, shapes):
+    attn_in, attn_out, ffn_in, ffn_out = (shape[1:] for shape in shapes[:4])
+    rows = ffn_in[0]
+    return (
+        mesh.shape["group"] == 2
+        and mesh.shape["shard"] == 4
+        and attn_in == (rows, 4 * LANES + HALF)
+        and attn_out == (rows, LANES + HALF)
+        and ffn_in[1] == 6 * LANES
+        and ffn_out == (6 * LANES, rows)
+        and rows == LANES + HALF
+        and shapes[7][0] <= 8 * LANES
+        and shapes[10][1] % (8 * LANES) == 0
     )
 
 
@@ -96,6 +563,11 @@
         P("shard", None),
         P(None, "tensor"),
     )
+
+    def shards(*args):
+        plan = paired if is_paired(mesh, [arg.shape for arg in args]) else general
+        return plan(*args)
+
     return jax.shard_map(
         shards,
         mesh=mesh,

time: 118 us -> 42.3 us (0.36)
  waiting for transfers between devices: 74.6 us -> 5.65 us
  between operations: 15.9 us -> 0.82 us
  Pallas kernels: 0 us -> 13.4 us
  starting transfers between devices: 0.12 us -> 8.55 us
  blocking collectives: 5.55 us -> 0 us
  other arithmetic: 6.97 us -> 1.74 us
  matrix products: 4.5 us -> 0 us
  local copies, waits for them, and re-layouts: 10.4 us -> 11.6 us
    psum x1 -> x0, waiting for transfers between devices: 49.1 us -> none  [shards(): coeff = lax.psum(partial_coeff, ('group', 'shard')) / groups]
    unnamed x4 -> x0, waiting for transfers between devices: 18.3 us -> none
    pallas_call x0 -> x6, Pallas kernels: none -> 13.4 us  [the longest x2 4.96 us: embed_half(): pl.pallas_call(embed_kernel, grid_spec=pltpu.PrefetchScalarGridSpec(num_s...]
    ppermute x0 -> x7, starting transfers between devices: none -> 8.55 us  [the longest x1 2.91 us: paired(): lax.ppermute(left, 'shard', near)]
    unnamed x30 -> x40, local copies, waits for them, and re-layouts: 4.13 us -> 11.6 us
    all_gather x1 -> x0, waiting for transfers between devices: 7.14 us -> none  [shards(): lax.all_gather(dense_new, 'group', axis=0, tiled=True)]
    ppermute x0 -> x7, waiting for transfers between devices: none -> 5.65 us  [the longest x1 2.18 us: paired(): lax.ppermute(left, 'shard', near)]
    unnamed x2 -> x0, blocking collectives: 5.55 us -> none
  transfers between devices with their start and end apart: 3 -> 7, of which waited for: 3 -> 3; matrix products, arithmetic and copies ran while one was open for 9% -> 3% of each run, Pallas kernels for 0% -> 23%
where the time goes in v1:
time: 42.3 us; the launch traced here: 41.7 us
  Pallas kernels  13.4 us (32%)
  local copies, waits for them, and re-layouts  11.6 us (27%)
  starting transfers between devices  8.55 us (20%)
  waiting for transfers between devices  5.65 us (13%)
  other arithmetic  1.74 us (4%)
  between operations  0.82 us (2%)
    unnamed x40, local copies, waits for them, and re-layouts  11.6 us
    pallas_call x2, Pallas kernels, embed_half(): pl.pallas_call(embed_kernel, grid_spec=pltpu.PrefetchScalarGridSpec(num_s...  4.96 us
    pallas_call x2, Pallas kernels, partial_coeff(): pl.pallas_call(partial_kernel, grid_spec=pltpu.PrefetchScalarGridSpec(num...  4.51 us
    pallas_call x1, Pallas kernels, dense_after(): pl.pallas_call(after_kernel, in_specs=[SCALAR] + [WHOLE] * 11, out_specs=...  3.52 us
    ppermute x1, starting transfers between devices, paired(): lax.ppermute(left, 'shard', near)  2.91 us
    ppermute x1, waiting for transfers between devices, paired(): lax.ppermute(left, 'shard', near)  2.18 us
    ppermute x1, waiting for transfers between devices, paired(): lax.ppermute(right, 'shard', near)  1.84 us
    ppermute x1, starting transfers between devices, paired(): lax.ppermute(left, 'shard', far)  1.83 us
  transfers between devices with their start and end apart: 7, of which 3 were waited for; matrix products, arithmetic and copies ran while one was open for 3% of the time, Pallas kernels for 23%

profile of v1, /device:TPU:0, one launch (start us, length us, event | category | flops | bytes accessed | tf_op | source)
XLA Modules:
  0.0 41.7 jit_solution(2258576804700287396)
XLA Ops:
  0.6 0.0 copy-start
  0.7 1.2 %copy-done = f32[1,221184]{1,0:T(1,128)S(1)} copy-done((f32[1,221184]{1,0:T(1,128)S(1)}, f32[1,221184]{1,0:T(1,128)}, u32[]{:S(2)}) %copy-start) | copy-done | bytes 884760
  1.8 1.2 %copy-done.2 = f32[1,221184]{1,0:T(1,128)S(1)} copy-done((f32[1,221184]{1,0:T(1,128)S(1)}, f32[1,221184]{1,0:T(1,128)}, u32[]{:S(2)}) %copy-start.2) | copy-done | bytes 884760
  3.0 1.0 %copy-done.4 = bf16[1,192,768]{2,1,0:T(8,128)(2,1)S(1)} copy-done((bf16[1,192,768]{2,1,0:T(8,128)(2,1)S(1)}, bf16[1,192,768]{2,1,0:T(8,128)(2,1)}, u32[]{:S(2)}) %copy-start.4) | copy-done | bytes 294936
  3.9 1.0 %copy-done.6 = bf16[1,768,192]{1,2,0:T(8,128)(2,1)S(1)} copy-done((bf16[1,768,192]{1,2,0:T(8,128)(2,1)S(1)}, bf16[1,768,192]{1,2,0:T(8,128)(2,1)}, u32[]{:S(2)}) %copy-start.6) | copy-done | bytes 294936
  4.9 0.9 %copy-done.8 = bf16[1,192,576]{2,1,0:T(8,128)(2,1)S(1)} copy-done((bf16[1,192,576]{2,1,0:T(8,128)(2,1)S(1)}, bf16[1,192,576]{2,1,0:T(8,128)(2,1)}, u32[]{:S(2)}) %copy-start.8) | copy-done | bytes 221208
  5.9 0.9 %copy-done.10 = bf16[1,192,192]{2,1,0:T(8,128)(2,1)S(1)} copy-done((bf16[1,192,192]{2,1,0:T(8,128)(2,1)S(1)}, bf16[1,192,192]{2,1,0:T(8,128)(2,1)}, u32[]{:S(2)}) %copy-start.10) | copy-done | bytes 73752
  6.7 0.7 %copy-done.12 = bf16[1,1920]{1,0:T(2,128)(2,1)S(1)} copy-done((bf16[1,1920]{1,0:T(2,128)(2,1)S(1)}, bf16[1,1920]{1,0:T(2,128)(2,1)}, u32[]{:S(2)}) %copy-start.12) | copy-done | bytes 3864
  7.4 0.7 %copy-done.14 = f32[960]{0:T(1024)S(1)} copy-done((f32[960]{0:T(1024)S(1)}, f32[960]{0:T(1024)}, u32[]{:S(2)}) %copy-start.14) | copy-done | bytes 3864
  8.1 0.7 %copy-done.16 = f32[960]{0:T(1024)S(1)} copy-done((f32[960]{0:T(1024)S(1)}, f32[960]{0:T(1024)}, u32[]{:S(2)}) %copy-start.16) | copy-done | bytes 3864
  8.8 0.4 dense_before.1.send_ref
  9.2 0.6 %collective-permute-start = (f32[6,584,128]{2,1,0:T(8,128)S(1)}, f32[6,584,128]{2,1,0:T(8,128)}, u32[]{:S(2)}, u32[]{:S(2)}) collective-permute-start(f32[6,584,128]{2,1,0:T(8,128)S(1)} %dense_before.1.send_ref), channel_id=1, source_target_pairs={{0,16},{16,0},{1,17},{17,1},{2,18},{18,2},{3,19},{19,3},{4,20},{20... | collective-permute-start | bytes 5382152 | tf_op jit(solution)/shard_map/ppermute | solution.py:502
  9.8 2.3 %partial_coeff.3 = f32[64,1024]{1,0:T(8,128)} custom-call(s32[1]{0:T(128)} %bitcast.group_ref, f32[64,192]{1,0:T(8,128)} %bitcast.23, bf16[192,2048]{1,0:T(8,128)(2,1)} %bitcast.21, f32[192,2048]{1,0:T(8,128)} %old_ref.7), custom_call_target="tpu_custom_call" | custom-call | flops 75497472 | bytes 1179648 | tf_op jit(solution)/shard_map/partial_coeff/pallas_call | solution.py:119
  12.1 0.0 collective-permute-start.1
  12.1 2.3 %partial_coeff.2 = f32[64,1024]{1,0:T(8,128)} custom-call(s32[1]{0:T(128)} %bitcast.group_ref, f32[64,192]{1,0:T(8,128)} %bitcast.24, bf16[192,2048]{1,0:T(8,128)(2,1)} %bitcast.22, f32[192,2048]{1,0:T(8,128)} %old_ref.7), custom_call_target="tpu_custom_call" | custom-call | flops 75497472 | bytes 1179648 | tf_op jit(solution)/shard_map/partial_coeff/pallas_call | solution.py:119
  14.4 1.0 %slice_add_fusion.1 = (f32[64,512]{1,0:T(8,128)S(1)}, f32[64,512]{1,0:T(8,128)S(1)}) fusion(f32[64,1024]{1,0:T(8,128)S(1)} %collective-permute-done.1, f32[64,1024]{1,0:T(8,128)} %partial_coeff.2), kind=kLoop, calls=%fused_computation.2 | loop fusion | flops 65536 | bytes 786432 | tf_op jit(solution)/shard_map/add | solution.py:505
  15.4 2.9 %collective-permute-start.2 = (f32[64,512]{1,0:T(8,128)S(1)}, f32[64,512]{1,0:T(8,128)S(1)}, u32[]{:S(2)}, u32[]{:S(2)}) collective-permute-start(f32[64,512]{1,0:T(8,128)S(1)} %get-tuple-element.31), channel_id=1, source_target_pairs={{0,4},{4,0},{8,12},{12,8},{1,5},{5,1},{9,13},{13,9},{2,6},{6,2},{1... | collective-permute-start | bytes 393224 | tf_op jit(solution)/shard_map/ppermute | solution.py:508
  18.3 1.5 %collective-permute-start.4 = (f32[64,512]{1,0:T(8,128)S(1)}, f32[64,512]{1,0:T(8,128)S(1)}, u32[]{:S(2)}, u32[]{:S(2)}) collective-permute-start(f32[64,512]{1,0:T(8,128)S(1)} %get-tuple-element.32), channel_id=1, source_target_pairs={{0,8},{4,12},{8,0},{12,4},{1,9},{5,13},{9,1},{13,5},{2,10},{6,14},... | collective-permute-start | bytes 393224 | tf_op jit(solution)/shard_map/ppermute | solution.py:509
  19.8 2.2 %collective-permute-done.2 = f32[64,512]{1,0:T(8,128)S(1)} collective-permute-done((f32[64,512]{1,0:T(8,128)S(1)}, f32[64,512]{1,0:T(8,128)S(1)}, u32[]{:S(2)}, u32[]{:S(2)}) %collective-permute-start.2) | collective-permute-done | bytes 131104 | tf_op jit(solution)/shard_map/ppermute | solution.py:508
  22.0 1.8 %collective-permute-start.3 = (f32[64,512]{1,0:T(8,128)S(1)}, f32[64,512]{1,0:T(8,128)S(1)}, u32[]{:S(2)}, u32[]{:S(2)}) collective-permute-start(f32[64,512]{1,0:T(8,128)S(1)} %add.19), channel_id=1, source_target_pairs={{0,8},{4,12},{8,0},{12,4},{1,9},{5,13},{9,1},{13,5},{2,10},{6,14},... | collective-permute-start | bytes 393224 | tf_op jit(solution)/shard_map/ppermute | solution.py:512
  23.9 1.6 %collective-permute-start.5 = (f32[64,512]{1,0:T(8,128)S(1)}, f32[64,512]{1,0:T(8,128)S(1)}, u32[]{:S(2)}, u32[]{:S(2)}) collective-permute-start(f32[64,512]{1,0:T(8,128)S(1)} %add.22), channel_id=1, source_target_pairs={{0,4},{4,0},{8,12},{12,8},{1,5},{5,1},{9,13},{13,9},{2,6},{6,2},{1... | collective-permute-start | bytes 393224 | tf_op jit(solution)/shard_map/ppermute | solution.py:513
  25.5 1.6 %collective-permute-done.3 = f32[64,512]{1,0:T(8,128)S(1)} collective-permute-done((f32[64,512]{1,0:T(8,128)S(1)}, f32[64,512]{1,0:T(8,128)S(1)}, u32[]{:S(2)}, u32[]{:S(2)}) %collective-permute-start.3) | collective-permute-done | bytes 131104 | tf_op jit(solution)/shard_map/ppermute | solution.py:512
  27.1 1.8 %collective-permute-done.5 = f32[64,512]{1,0:T(8,128)S(1)} collective-permute-done((f32[64,512]{1,0:T(8,128)S(1)}, f32[64,512]{1,0:T(8,128)S(1)}, u32[]{:S(2)}, u32[]{:S(2)}) %collective-permute-start.5) | collective-permute-done | bytes 131104 | tf_op jit(solution)/shard_map/ppermute | solution.py:513
  29.0 0.1 collective-permute-start.6
  29.1 0.6 %copy-done.18 = f32[64,1024]{1,0:T(8,128)} copy-done((f32[64,1024]{1,0:T(8,128)}, f32[64,1024]{1,0:T(8,128)S(1)}, u32[]{:S(2)}) %copy-start.18) | copy-done | bytes 262168
  29.7 2.4 %embed_half.2 = (f32[192,2048]{1,0:T(8,128)}, f32[64,2048]{1,0:T(8,128)}) custom-call(s32[1]{0:T(128)} %bitcast.group_ref, f32[64,192]{1,0:T(8,128)} %bitcast.25, f32[64,1024]{1,0:T(8,128)} %copy-done.18, f32[64,2048]{1,0:T(8,128)} %moment_ref.3, f32[192,2048]{1,0:T(8,128)} %old_ref.7), custom_call_target="tpu_custom_call" | custom-call | flops 75497472 | bytes 1572864 | tf_op jit(solution)/shard_map/embed_half/pallas_call | solution.py:168
  32.1 0.7 %copy-done.19 = f32[64,1024]{1,0:T(8,128)} copy-done((f32[64,1024]{1,0:T(8,128)}, f32[64,1024]{1,0:T(8,128)S(1)}, u32[]{:S(2)}) %copy-start.19) | copy-done | bytes 262168
  32.9 2.5 %embed_half.3 = (f32[192,2048]{1,0:T(8,128)}, f32[64,2048]{1,0:T(8,128)}) custom-call(s32[1]{0:T(128)} %bitcast.group_ref, f32[64,192]{1,0:T(8,128)} %bitcast.26, f32[64,1024]{1,0:T(8,128)} %copy-done.19, f32[64,2048]{1,0:T(8,128)} %moment_ref.3, f32[192,2048]{1,0:T(8,128)} %old_ref.7, ...), custom_call_target="tpu_custom_call", output_to_operand_aliasing={{0}: (5, {}), {1}: (6, {})} | custom-call | flops 75497472 | bytes 1572864 | tf_op jit(solution)/shard_map/embed_half/pallas_call | solution.py:168
  35.5 1.2 %copy-done.3 = f32[1,221184]{1,0:T(1,128)S(1)} copy-done((f32[1,221184]{1,0:T(1,128)S(1)}, f32[1,221184]{1,0:T(1,128)}, u32[]{:S(2)}) %copy-start.3) | copy-done | bytes 884760
  36.7 0.9 %copy-done.11 = bf16[1,192,192]{2,1,0:T(8,128)(2,1)S(1)} copy-done((bf16[1,192,192]{2,1,0:T(8,128)(2,1)S(1)}, bf16[1,192,192]{2,1,0:T(8,128)(2,1)}, u32[]{:S(2)}) %copy-start.11) | copy-done | bytes 73752
  37.6 3.5 %dense_after.1 = (f32[192,576]{1,0:T(8,128)}, f32[192,192]{1,0:T(8,128)}, f32[192,768]{1,0:T(8,128)}, f32[192,768]{1,0:T(8,128)}, f32[1728,128]{1,0:T(8,128)}, /*index=5*/f32[1,1920]{1,0:T(1,128)S(1)}, f32[1,960]{1,0:T(1,128)}) custom-call(s32[1]{0:T(128)} %bitcast.group_ref, f32[6,584,128]{2,1,0:T(8,128)} %collective-permute-done.recv_ref, ...), custom_call_target="tpu_custom_call" | custom-call | flops 1327104 | bytes 5898240 | tf_op jit(solution)/shard_map/dense_after/pallas_call | solution.py:452
  41.1 0.6 %reduce = f32[1920]{0:T(1024)} reduce(f32[1,1920]{1,0:T(1,128)S(1)} %get-tuple-element.25, f32[]{:T(128)} %constant.16), dimensions={0}, to_apply=%get-tuple-element.25.reduce_sub_computation | reduce | bytes 15364 | tf_op jit(solution)/shard_map/dense_after/pallas_call | solution.py:452
  (35 shorter events, 0.2 us)
Async XLA Ops:
  0.6 1.2 %copy-start = (f32[1,221184]{1,0:T(1,128)S(1)}, f32[1,221184]{1,0:T(1,128)}, u32[]{:S(2)}) copy-start(f32[1,221184]{1,0:T(1,128)} %param.18) | copy-start | bytes 2654212
  1.8 1.2 %copy-start.2 = (f32[1,221184]{1,0:T(1,128)S(1)}, f32[1,221184]{1,0:T(1,128)}, u32[]{:S(2)}) copy-start(f32[1,221184]{1,0:T(1,128)} %param.19) | copy-start | bytes 2654212
  3.0 1.0 %copy-start.4 = (bf16[1,192,768]{2,1,0:T(8,128)(2,1)S(1)}, bf16[1,192,768]{2,1,0:T(8,128)(2,1)}, u32[]{:S(2)}) copy-start(bf16[1,192,768]{2,1,0:T(8,128)(2,1)} %up_ref.3) | copy-start | bytes 884740
  3.9 1.0 %copy-start.6 = (bf16[1,768,192]{1,2,0:T(8,128)(2,1)S(1)}, bf16[1,768,192]{1,2,0:T(8,128)(2,1)}, u32[]{:S(2)}) copy-start(bf16[1,768,192]{1,2,0:T(8,128)(2,1)} %param.16) | copy-start | bytes 884740
  4.9 0.9 %copy-start.8 = (bf16[1,192,576]{2,1,0:T(8,128)(2,1)S(1)}, bf16[1,192,576]{2,1,0:T(8,128)(2,1)}, u32[]{:S(2)}) copy-start(bf16[1,192,576]{2,1,0:T(8,128)(2,1)} %in_ref.3) | copy-start | bytes 663556
  5.9 0.9 %copy-start.10 = (bf16[1,192,192]{2,1,0:T(8,128)(2,1)S(1)}, bf16[1,192,192]{2,1,0:T(8,128)(2,1)}, u32[]{:S(2)}) copy-start(bf16[1,192,192]{2,1,0:T(8,128)(2,1)} %out_ref.3) | copy-start | bytes 221188
  6.7 0.7 %copy-start.12 = (bf16[1,1920]{1,0:T(2,128)(2,1)S(1)}, bf16[1,1920]{1,0:T(2,128)(2,1)}, u32[]{:S(2)}) copy-start(bf16[1,1920]{1,0:T(2,128)(2,1)} %small_ref.3) | copy-start | bytes 11524
  7.4 0.7 %copy-start.14 = (f32[960]{0:T(1024)S(1)}, f32[960]{0:T(1024)}, u32[]{:S(2)}) copy-start(f32[960]{0:T(1024)} %param.20) | copy-start | bytes 11524
  8.1 0.7 %copy-start.16 = (f32[960]{0:T(1024)S(1)}, f32[960]{0:T(1024)}, u32[]{:S(2)}) copy-start(f32[960]{0:T(1024)} %param.21) | copy-start | bytes 11524
  9.2 26.2 %collective-permute-start = (f32[6,584,128]{2,1,0:T(8,128)S(1)}, f32[6,584,128]{2,1,0:T(8,128)}, u32[]{:S(2)}, u32[]{:S(2)}) collective-permute-start(f32[6,584,128]{2,1,0:T(8,128)S(1)} %dense_before.1.send_ref), channel_id=1, source_target_pairs={{0,16},{16,0},{1,17},{17,1},{2,18},{18,2},{3,19},{19,3},{4,20},{20... | collective-permute-start | bytes 5382152 | tf_op jit(solution)/shard_map/ppermute | solution.py:502
  12.1 2.3 %collective-permute-start.1 = (f32[64,1024]{1,0:T(8,128)}, f32[64,1024]{1,0:T(8,128)S(1)}, u32[]{:S(2)}, u32[]{:S(2)}) collective-permute-start(f32[64,1024]{1,0:T(8,128)} %partial_coeff.3), channel_id=1, source_target_pairs={{0,16},{16,0},{1,17},{17,1},{2,18},{18,2},{3,19},{19,3},{4,20},{20... | collective-permute-start | bytes 786440 | tf_op jit(solution)/shard_map/ppermute | solution.py:494
  15.4 6.6 %collective-permute-start.2 = (f32[64,512]{1,0:T(8,128)S(1)}, f32[64,512]{1,0:T(8,128)S(1)}, u32[]{:S(2)}, u32[]{:S(2)}) collective-permute-start(f32[64,512]{1,0:T(8,128)S(1)} %get-tuple-element.31), channel_id=1, source_target_pairs={{0,4},{4,0},{8,12},{12,8},{1,5},{5,1},{9,13},{13,9},{2,6},{6,2},{1... | collective-permute-start | bytes 393224 | tf_op jit(solution)/shard_map/ppermute | solution.py:508
  18.3 5.6 %collective-permute-start.4 = (f32[64,512]{1,0:T(8,128)S(1)}, f32[64,512]{1,0:T(8,128)S(1)}, u32[]{:S(2)}, u32[]{:S(2)}) collective-permute-start(f32[64,512]{1,0:T(8,128)S(1)} %get-tuple-element.32), channel_id=1, source_target_pairs={{0,8},{4,12},{8,0},{12,4},{1,9},{5,13},{9,1},{13,5},{2,10},{6,14},... | collective-permute-start | bytes 393224 | tf_op jit(solution)/shard_map/ppermute | solution.py:509
  22.0 5.0 %collective-permute-start.3 = (f32[64,512]{1,0:T(8,128)S(1)}, f32[64,512]{1,0:T(8,128)S(1)}, u32[]{:S(2)}, u32[]{:S(2)}) collective-permute-start(f32[64,512]{1,0:T(8,128)S(1)} %add.19), channel_id=1, source_target_pairs={{0,8},{4,12},{8,0},{12,4},{1,9},{5,13},{9,1},{13,5},{2,10},{6,14},... | collective-permute-start | bytes 393224 | tf_op jit(solution)/shard_map/ppermute | solution.py:512
  23.9 5.0 %collective-permute-start.5 = (f32[64,512]{1,0:T(8,128)S(1)}, f32[64,512]{1,0:T(8,128)S(1)}, u32[]{:S(2)}, u32[]{:S(2)}) collective-permute-start(f32[64,512]{1,0:T(8,128)S(1)} %add.22), channel_id=1, source_target_pairs={{0,4},{4,0},{8,12},{12,8},{1,5},{5,1},{9,13},{13,9},{2,6},{6,2},{1... | collective-permute-start | bytes 393224 | tf_op jit(solution)/shard_map/ppermute | solution.py:513
  29.0 0.7 %copy-start.18 = (f32[64,1024]{1,0:T(8,128)}, f32[64,1024]{1,0:T(8,128)S(1)}, u32[]{:S(2)}) copy-start(f32[64,1024]{1,0:T(8,128)S(1)} %maximum_multiply_fusion.coeff_ref) | copy-start | bytes 786436
  29.0 3.1 %collective-permute-start.6 = (f32[64,1024]{1,0:T(8,128)S(1)}, f32[64,1024]{1,0:T(8,128)S(1)}, u32[]{:S(2)}, u32[]{:S(2)}) collective-permute-start(f32[64,1024]{1,0:T(8,128)S(1)} %maximum_multiply_fusion.coeff_ref), channel_id=1, source_target_pairs={{0,16},{16,0},{1,17},{17,1},{2,18},{18,2},{3,19},{19,3},{4,20},{20... | collective-permute-start | bytes 786440 | tf_op jit(solution)/shard_map/ppermute | solution.py:516
  32.1 0.7 %copy-start.19 = (f32[64,1024]{1,0:T(8,128)}, f32[64,1024]{1,0:T(8,128)S(1)}, u32[]{:S(2)}) copy-start(f32[64,1024]{1,0:T(8,128)S(1)} %collective-permute-done.6.coeff_ref) | copy-start | bytes 786436
  32.8 2.6 %copy-start.1 = (f32[1,221184]{1,0:T(1,128)S(1)}, f32[1,221184]{1,0:T(1,128)}, u32[]{:S(2)}) copy-start(f32[1,221184]{1,0:T(1,128)} %param.18) | copy-start | bytes 2654212
  32.8 2.6 %copy-start.5 = (bf16[1,192,768]{2,1,0:T(8,128)(2,1)S(1)}, bf16[1,192,768]{2,1,0:T(8,128)(2,1)}, u32[]{:S(2)}) copy-start(bf16[1,192,768]{2,1,0:T(8,128)(2,1)} %up_ref.3) | copy-start | bytes 884740
  32.8 2.6 %copy-start.7 = (bf16[1,768,192]{1,2,0:T(8,128)(2,1)S(1)}, bf16[1,768,192]{1,2,0:T(8,128)(2,1)}, u32[]{:S(2)}) copy-start(bf16[1,768,192]{1,2,0:T(8,128)(2,1)} %param.16) | copy-start | bytes 884740
  32.8 2.6 %copy-start.9 = (bf16[1,192,576]{2,1,0:T(8,128)(2,1)S(1)}, bf16[1,192,576]{2,1,0:T(8,128)(2,1)}, u32[]{:S(2)}) copy-start(bf16[1,192,576]{2,1,0:T(8,128)(2,1)} %in_ref.3) | copy-start | bytes 663556
  32.8 2.6 %copy-start.13 = (bf16[1,1920]{1,0:T(2,128)(2,1)S(1)}, bf16[1,1920]{1,0:T(2,128)(2,1)}, u32[]{:S(2)}) copy-start(bf16[1,1920]{1,0:T(2,128)(2,1)} %small_ref.3) | copy-start | bytes 11524
  32.8 2.6 %copy-start.15 = (f32[960]{0:T(1024)S(1)}, f32[960]{0:T(1024)}, u32[]{:S(2)}) copy-start(f32[960]{0:T(1024)} %param.20) | copy-start | bytes 11524
  32.9 2.6 %copy-start.17 = (f32[960]{0:T(1024)S(1)}, f32[960]{0:T(1024)}, u32[]{:S(2)}) copy-start(f32[960]{0:T(1024)} %param.21) | copy-start | bytes 11524
  35.5 1.2 %copy-start.3 = (f32[1,221184]{1,0:T(1,128)S(1)}, f32[1,221184]{1,0:T(1,128)}, u32[]{:S(2)}) copy-start(f32[1,221184]{1,0:T(1,128)} %param.19) | copy-start | bytes 2654212
  36.7 0.9 %copy-start.11 = (bf16[1,192,192]{2,1,0:T(8,128)(2,1)S(1)}, bf16[1,192,192]{2,1,0:T(8,128)(2,1)}, u32[]{:S(2)}) copy-start(bf16[1,192,192]{2,1,0:T(8,128)(2,1)} %out_ref.3) | copy-start | bytes 221188

commit v2 on v1

--- a/solution.py
+++ b/solution.py
@@ -1,3 +1,5 @@
+import functools
+
 import jax
 import jax.numpy as jnp
 from jax import lax
@@ -95,100 +97,150 @@
     return high, (value - high.astype(f32)).astype(bf16)
 
 
-def partial_kernel(group_ref, basis_ref, local_ref, old_ref, out_ref):
-    del group_ref
-    rank = basis_ref.shape[0]
+CHUNKS = 2
+WHOLE = pl.BlockSpec(memory_space=pltpu.VMEM)
+SCALAR = pl.BlockSpec(memory_space=pltpu.SMEM)
+ANY = pl.BlockSpec(memory_space=pl.ANY)
+
+
+def in_hbm(arrays):
+    return [pltpu.with_memory_space_constraint(array, pltpu.HBM) for array in arrays]
+
+
+def side_start(side_ref, other, columns):
+    side = 1 - side_ref[0] if other else side_ref[0]
+    return side * columns
+
+
+def partial_kernel(other, side_ref, basis_hbm, local_hbm, old_hbm, moment_hbm, *refs):
+    if other:
+        out_ref, old_ref, basis_ref, local_ref, sems = refs
+    else:
+        out_ref, old_ref, moment_ref, stack_ref, basis_ref, local_ref, sems = refs
+    rank, columns = out_ref.shape
+    block = columns // CHUNKS
+    start = side_start(side_ref, other, columns)
+    copies = [pltpu.make_async_copy(basis_hbm, basis_ref, sems.at[0])]
+    for k in range(CHUNKS):
+        source = pl.ds(pl.multiple_of(start + k * block, block), block)
+        target = pl.ds(k * block, block)
+        copies.append(
+            pltpu.make_async_copy(
+                old_hbm.at[:, source], old_ref.at[:, target], sems.at[1 + 2 * k]
+            )
+        )
+        copies.append(
+            pltpu.make_async_copy(
+                local_hbm.at[:, source], local_ref.at[:, target], sems.at[2 + 2 * k]
+            )
+        )
+    if not other:
+        copies.append(pltpu.make_async_copy(moment_hbm, moment_ref, sems.at[1 + 2 * CHUNKS]))
+    for copy in copies:
+        copy.start()
+    copies[0].wait()
     high, low = split(basis_ref[...])
     both = jnp.concatenate([high, low], axis=0)
-    diff_high, diff_low = split(old_ref[...] - local_ref[...].astype(f32))
-    first = jnp.dot(both, diff_high, preferred_element_type=f32)
-    second = jnp.dot(high, diff_low, preferred_element_type=f32)
-    out_ref[...] = first[:rank] + first[rank:] + second
-
-
-def partial_coeff(group, basis_t, local, old, other):
+    for k in range(CHUNKS):
+        copies[1 + 2 * k].wait()
+        copies[2 + 2 * k].wait()
+        target = slice(k * block, (k + 1) * block)
+        diff_high, diff_low = split(old_ref[:, target] - local_ref[:, target].astype(f32))
+        first = jnp.dot(both, diff_high, preferred_element_type=f32)
+        second = jnp.dot(high, diff_low, preferred_element_type=f32)
+        out_ref[:, target] = first[:rank] + first[rank:] + second
+    if not other:
+        basis = basis_ref[...]
+        stack = jnp.concatenate([high.astype(f32), basis - high.astype(f32), high.astype(f32)], axis=0)
+        stack_ref[...] = stack.T.astype(bf16)
+        copies[-1].wait()
+
+
+def partial_coeff(side, basis_t, local, old, moment, other):
     rank, depth = basis_t.shape
-    columns = old.shape[1] // 2
-    steps = 2
-    block = columns // steps
-
-    def half(step, group_ref):
-        side = 1 - group_ref[0] if other else group_ref[0]
-        return (0, side * steps + step)
-
+    width = old.shape[1]
+    columns = width // 2
+    out_shape = [
+        jax.ShapeDtypeStruct((rank, columns), f32),
+        jax.ShapeDtypeStruct((depth, columns), f32),
+    ]
+    if not other:
+        out_shape += [
+            jax.ShapeDtypeStruct((rank, width), f32),
+            jax.ShapeDtypeStruct((depth, 3 * rank), bf16),
+        ]
     return pl.pallas_call(
-        partial_kernel,
-        grid_spec=pltpu.PrefetchScalarGridSpec(
-            num_scalar_prefetch=1,
-            grid=(steps,),
-            in_specs=[
-                pl.BlockSpec((rank, depth), lambda step, group_ref: (0, 0)),
-                pl.BlockSpec((depth, block), half),
-                pl.BlockSpec((depth, block), half),
-            ],
-            out_specs=pl.BlockSpec((rank, block), lambda step, group_ref: (0, step)),
-        ),
-        out_shape=jax.ShapeDtypeStruct((rank, columns), f32),
+        functools.partial(partial_kernel, other),
+        in_specs=[SCALAR] + [ANY] * 4,
+        out_specs=[WHOLE] * len(out_shape),
+        out_shape=out_shape,
+        scratch_shapes=[
+            pltpu.VMEM((rank, depth), f32),
+            pltpu.VMEM((depth, columns), bf16),
+            pltpu.SemaphoreType.DMA((2 + 2 * CHUNKS,)),
+        ],
+        compiler_params=pltpu.CompilerParams(vmem_limit_bytes=8 * 2**20),
         cost_estimate=pl.CostEstimate(
             flops=6 * rank * depth * columns, bytes_accessed=6 * depth * columns, transcendentals=0
         ),
         name="partial_coeff",
-    )(group, basis_t, local, old)
-
-
-def embed_kernel(group_ref, basis_ref, coeff_ref, moment_ref, old_ref, *refs):
-    del group_ref
-    embed_ref, moved_ref = refs[-2:]
-    moved = momentum_coef * moment_ref[...] + coeff_ref[...]
-    moved_ref[...] = moved
-    update = coeff_ref[...] + momentum_coef * moved
-    high, low = split(basis_ref[...])
-    up_high, up_low = split(update)
-    product = lax.dot_general(
-        jnp.concatenate([high, low, high], axis=0),
-        jnp.concatenate([up_high, up_high, up_low], axis=0),
-        (((0,), (0,)), ((), ())),
-        preferred_element_type=f32,
-    )
-    embed_ref[...] = old_ref[...] - outer_rate * product
-
-
-def embed_half(group, basis_t, coeff, moment, old, before):
-    rank, depth = basis_t.shape
-    width = old.shape[1]
-    columns = width // 2
-    steps = 2
-    block = columns // steps
-
-    def half(step, group_ref):
-        side = group_ref[0] if before is None else 1 - group_ref[0]
-        return (0, side * steps + step)
-
-    more = () if before is None else before
+    )(side, *in_hbm((basis_t, local, old, moment)))
+
+
+def embed_kernel(other, side_ref, stack_ref, coeff_ref, moment_ref, old_ref, *refs):
+    embed_hbm, moved_hbm, embed_ref, moved_ref, sems = refs[-5:]
+    columns = coeff_ref.shape[1]
+    block = columns // CHUNKS
+    start = side_start(side_ref, other, columns)
+    copies = []
+    for k in range(CHUNKS):
+        here = slice(k * block, (k + 1) * block)
+        there = pl.ds(pl.multiple_of(start + k * block, block), block)
+        coeff = coeff_ref[:, here]
+        moved = momentum_coef * moment_ref[:, there] + coeff
+        moved_ref[:, here] = moved
+        up_high, up_low = split(coeff + momentum_coef * moved)
+        product = jnp.dot(
+            stack_ref[...],
+            jnp.concatenate([up_high, up_high, up_low], axis=0),
+            preferred_element_type=f32,
+        )
+        embed_ref[:, here] = old_ref[:, here] - outer_rate * product
+        target = pl.ds(k * block, block)
+        for source_ref, target_hbm, at in ((moved_ref, moved_hbm, 0), (embed_ref, embed_hbm, 1)):
+            copy = pltpu.make_async_copy(
+                source_ref.at[:, target], target_hbm.at[:, there], sems.at[2 * k + at]
+            )
+            copy.start()
+            copies.append(copy)
+    for copy in copies:
+        copy.wait()
+
+
+def embed_half(side, stack, coeff, moment, old, before):
+    rank, columns = coeff.shape
+    depth = old.shape[0]
+    more = () if before is None else tuple(before)
     return pl.pallas_call(
-        embed_kernel,
-        grid_spec=pltpu.PrefetchScalarGridSpec(
-            num_scalar_prefetch=1,
-            grid=(steps,),
-            in_specs=[
-                pl.BlockSpec((rank, depth), lambda step, group_ref: (0, 0)),
-                pl.BlockSpec((rank, block), lambda step, group_ref: (0, step)),
-                pl.BlockSpec((rank, block), half),
-                pl.BlockSpec((depth, block), half),
-            ]
-            + [pl.BlockSpec(memory_space=pl.ANY)] * len(more),
-            out_specs=[pl.BlockSpec((depth, block), half), pl.BlockSpec((rank, block), half)],
-        ),
+        functools.partial(embed_kernel, before is not None),
+        in_specs=[SCALAR] + [WHOLE] * 4 + [ANY] * len(more),
+        out_specs=[ANY, ANY],
         out_shape=[
-            jax.ShapeDtypeStruct((depth, width), f32),
-            jax.ShapeDtypeStruct((rank, width), f32),
+            jax.ShapeDtypeStruct((depth, 2 * columns), f32),
+            jax.ShapeDtypeStruct((rank, 2 * columns), f32),
+        ],
+        scratch_shapes=[
+            pltpu.VMEM((depth, columns), f32),
+            pltpu.VMEM((rank, columns), f32),
+            pltpu.SemaphoreType.DMA((2 * CHUNKS,)),
         ],
         input_output_aliases={} if before is None else {5: 0, 6: 1},
+        compiler_params=pltpu.CompilerParams(vmem_limit_bytes=8 * 2**20),
         cost_estimate=pl.CostEstimate(
             flops=6 * rank * depth * columns, bytes_accessed=8 * depth * columns, transcendentals=0
         ),
         name="embed_half",
-    )(group, basis_t, coeff, moment, old, *more)
+    )(side, stack, coeff, moment, old, *more)
 
 
 def low_lanes(rows):
@@ -246,8 +298,9 @@
 
 def before_kernel(
     group_ref, in_ref, out_ref, up_ref, down_ref, old_ref, mom_ref, small_ref, small_old_ref,
-    small_mom_ref, send_ref, wide_ref,
+    small_mom_ref, send_ref, mark_ref, wide_ref,
 ):
+    mark_ref[...] = jnp.zeros(mark_ref.shape, f32)
     rows = up_ref.shape[1]
     mid = rows // 2
     block = rows + mid
@@ -425,30 +478,29 @@
         put_small(values[:, :small], values[:, small:], False)
 
 
-WHOLE = pl.BlockSpec(memory_space=pltpu.VMEM)
-SCALAR = pl.BlockSpec(memory_space=pltpu.SMEM)
-
-
-def dense_before(group, matrices, flats, smalls):
-    _, rows, width = matrices[2].shape
+def dense_before(group, operands):
+    _, rows, width = operands[2].shape
     return pl.pallas_call(
         before_kernel,
         in_specs=[SCALAR] + [WHOLE] * 9,
-        out_specs=WHOLE,
-        out_shape=jax.ShapeDtypeStruct((width // LANES, 3 * rows + 8, LANES), f32),
+        out_specs=[WHOLE] * 2,
+        out_shape=[
+            jax.ShapeDtypeStruct((width // LANES, 3 * rows + 8, LANES), f32),
+            jax.ShapeDtypeStruct((8, LANES), f32),
+        ],
         scratch_shapes=[pltpu.VMEM((2, width, LANES), f32)],
         compiler_params=pltpu.CompilerParams(vmem_limit_bytes=20 * 2**20),
         cost_estimate=pl.CostEstimate(
-            flops=9 * rows * width, bytes_accessed=30 * rows * width, transcendentals=0
+            flops=60000 * rows * width, bytes_accessed=30 * rows * width, transcendentals=0
         ),
         name="dense_before",
-    )(group, *matrices, *flats, *smalls)
-
-
-def dense_after(group, received, sent, matrices, flats, smalls):
-    _, rows, width = matrices[2].shape
-    outs = [matrix.shape[1:] for matrix in matrices]
-    outs += [flats[0].shape, smalls[0].shape, smalls[1].shape]
+    )(group, *operands)
+
+
+def dense_after(group, received, sent, operands):
+    _, rows, width = operands[2].shape
+    outs = [matrix.shape[1:] for matrix in operands[:4]]
+    outs += [operands[4].shape, operands[6].shape, operands[7].shape]
     return pl.pallas_call(
         after_kernel,
         in_specs=[SCALAR] + [WHOLE] * 11,
@@ -460,10 +512,10 @@
         ],
         compiler_params=pltpu.CompilerParams(vmem_limit_bytes=24 * 2**20),
         cost_estimate=pl.CostEstimate(
-            flops=9 * rows * width, bytes_accessed=40 * rows * width, transcendentals=0
+            flops=60000 * rows * width, bytes_accessed=40 * rows * width, transcendentals=0
         ),
         name="dense_after",
-    )(group, received, sent, *matrices, *flats, *smalls)
+    )(group, received, sent, *operands)
 
 
 def paired(
@@ -484,38 +536,54 @@
     position = lax.axis_index("group")
     group = position.astype(jnp.int32).reshape(1)
     swap = [(0, 1), (1, 0)]
-    shards_count = lax.axis_size("shard")
-    near = [(i, i ^ 1) for i in range(shards_count)]
-    far = [(i, i ^ 2) for i in range(shards_count)]
+    chips = lax.axis_size("shard")
+
+    def turned(chip):
+        return (chip ^ (chip >> 1)) & 1
+
+    first, second = (
+        [
+            (core * chips + chip, (1 - core) * chips + (chip ^ (1 + (core ^ turned(chip) ^ late))))
+            for core in range(2)
+            for chip in range(chips)
+        ]
+        for late in range(2)
+    )
+    side = group ^ turned(lax.axis_index("shard").astype(jnp.int32))
+    axes = ("group", "shard")
 
     basis_t = basis.T
-    local = embed_local[0]
-    theirs = partial_coeff(group, basis_t, local, embed_old, True)
+    embed = (basis_t, embed_local[0], embed_old, coeff_momentum)
+    theirs, old_rest = partial_coeff(side, *embed, True)
     theirs = lax.ppermute(theirs, "group", swap)
-    mine = partial_coeff(group, basis_t, local, embed_old, False)
-    columns = mine.shape[1] // 2
-
-    matrices = (attn_in_local, attn_out_local, ffn_in_local, jnp.swapaxes(ffn_out_local, 1, 2))
-    flats = (dense_old.reshape(-1, LANES), dense_momentum.reshape(-1, LANES))
-    smalls = (small_local, small_old[None, :], small_momentum[None, :])
-    sent = dense_before(group, matrices, flats, smalls)
+    mine, old_own, moment, stack = partial_coeff(side, *embed, False)
+    total = mine + theirs
+
+    operands = (
+        attn_in_local,
+        attn_out_local,
+        ffn_in_local,
+        jnp.swapaxes(ffn_out_local, 1, 2),
+        dense_old.reshape(-1, LANES),
+        dense_momentum.reshape(-1, LANES),
+        small_local,
+        small_old[None, :],
+        small_momentum[None, :],
+    )
+    total, group_later = lax.optimization_barrier((total, group))
+    moving = lax.ppermute(total, axes, first)
+    sent, mark = dense_before(group_later, operands)
     received = lax.ppermute(sent, "group", swap)
-    dense = dense_after(group, received, sent, matrices, flats, smalls)
-
-    left = mine[:, :columns] + theirs[:, :columns]
-    right = mine[:, columns:] + theirs[:, columns:]
-    left, right = (
-        left + lax.ppermute(left, "shard", near),
-        right + lax.ppermute(right, "shard", far),
-    )
-    left, right = (
-        left + lax.ppermute(left, "shard", far),
-        right + lax.ppermute(right, "shard", near),
-    )
-    own = 0.5 * jnp.concatenate([left, right], axis=1)
+    moving, mark = lax.optimization_barrier((moving, mark))
+    total = total + moving
+    moving = lax.ppermute(total, axes, second)
+    dense = list(dense_after(group, received, sent, operands))
+    moving, dense[-1] = lax.optimization_barrier((moving, dense[-1]))
+
+    own = 0.5 * (total + moving)
     rest = lax.ppermute(own, "group", swap)
-    done = embed_half(group, basis_t, own, coeff_momentum, embed_old, None)
-    embed_next, coeff_moved = embed_half(group, basis_t, rest, coeff_momentum, embed_old, done)
+    done = embed_half(side, stack, own, moment, old_own, None)
+    embed_next, coeff_moved = embed_half(side, stack, rest, moment, old_rest, done)
 
     attn_in_next, attn_out_next, ffn_in_next, ffn_out_next, moved, small_next, small_moved = dense
     return (

time: 42.3 us -> 22.1 us (0.52); the launches traced: 41.7 us -> 21.9 us
  local copies, waits for them, and re-layouts: 11.6 us -> 0.06 us
  Pallas kernels: 13.4 us -> 8.82 us
  starting transfers between devices: 8.55 us -> 5.43 us
  other arithmetic: 1.74 us -> 0.73 us
    unnamed x40 -> x18, local copies, waits for them, and re-layouts: 11.6 us -> 0.06 us
    pallas_call x4, Pallas kernels: 9.47 us -> 5.77 us  [the longest x2 3.4 us: partial_coeff(): pl.pallas_call(functools.partial(partial_kernel, other), in_specs=[SCALAR...]
    ppermute x4 -> x2, starting transfers between devices: 7.82 us -> 4.32 us  [the longest x1 2.49 us: paired(): moving = lax.ppermute(total, axes, first)]
    pallas_call x1, Pallas kernels: 3.52 us -> 2.05 us  [dense_after(): pl.pallas_call(after_kernel, in_specs=[SCALAR] + [WHOLE] * 11, out_specs=...]
    add x5 -> x2, other arithmetic: 1.1 us -> 0.08 us  [the longest x1 0.04 us: paired(): total = mine + theirs]
    pallas_call x1, Pallas kernels: 0.39 us -> 1 us  [dense_before(): pl.pallas_call(before_kernel, in_specs=[SCALAR] + [WHOLE] * 9, out_specs=...]
    ppermute x1, starting transfers between devices: 0.04 us -> 0.52 us  [paired(): theirs = lax.ppermute(theirs, 'group', swap)]
    ppermute x4 -> x2, waiting for transfers between devices: 5.64 us -> 6.06 us  [the longest x1 4.05 us: paired(): moving = lax.ppermute(total, axes, first)]
  transfers between devices with their start and end apart: 7 -> 5, of which waited for: 3 -> 2; matrix products, arithmetic and copies ran while one was open for 3% -> 3% of each run, Pallas kernels for 23% -> 23%
where the time goes in v2:
time: 22.1 us; the launch traced here: 21.9 us
  Pallas kernels  8.82 us (40%)
  waiting for transfers between devices  6.06 us (27%)
  starting transfers between devices  5.43 us (25%)
  between operations  0.84 us (4%)
  other arithmetic  0.73 us (3%)
    ppermute x1, waiting for transfers between devices, paired(): moving = lax.ppermute(total, axes, first)  4.05 us
    pallas_call x2, Pallas kernels, partial_coeff(): pl.pallas_call(functools.partial(partial_kernel, other), in_specs=[SCALAR...  3.4 us
    ppermute x1, starting transfers between devices, paired(): moving = lax.ppermute(total, axes, first)  2.49 us
    pallas_call x2, Pallas kernels, embed_half(): pl.pallas_call(functools.partial(embed_kernel, before is not None), in_sp...  2.36 us
    pallas_call x1, Pallas kernels, dense_after(): pl.pallas_call(after_kernel, in_specs=[SCALAR] + [WHOLE] * 11, out_specs=...  2.05 us
    ppermute x1, waiting for transfers between devices, paired(): moving = lax.ppermute(total, axes, second)  2 us
    ppermute x1, starting transfers between devices, paired(): moving = lax.ppermute(total, axes, second)  1.84 us
    pallas_call x1, Pallas kernels, dense_before(): pl.pallas_call(before_kernel, in_specs=[SCALAR] + [WHOLE] * 9, out_specs=...  1 us
  transfers between devices with their start and end apart: 5, of which 2 were waited for; matrix products, arithmetic and copies ran while one was open for 3% of the time, Pallas kernels for 23%

profile of v2, /device:TPU:0, one launch (start us, length us, event | category | flops | bytes accessed | tf_op | source)
XLA Modules:
  0.0 21.9 jit_solution(18441239970557730320)
XLA Ops:
  0.6 1.6 %partial_coeff.3 = (f32[64,1024]{1,0:T(8,128)S(1)}, f32[192,1024]{1,0:T(8,128)S(1)}) custom-call(s32[1]{0:T(128)S(6)} %xor.11.side_ref, f32[64,192]{1,0:T(8,128)} %bitcast.24, bf16[192,2048]{1,0:T(8,128)(2,1)} %bitcast.22, f32[192,2048]{1,0:T(8,128)} %old_hbm.3, f32[64,2048]{1,0:T(8,128)} %moment_hbm.3), custom_call_target="tpu_custom_call" | custom-call | flops 75497472 | bytes 1179648 | tf_op jit(solution)/shard_map/partial_coeff/pallas_call | solution.py:172
  2.3 0.0 copy-start
  2.3 0.0 copy-start.1
  2.3 0.0 copy-start.2
  2.3 0.0 copy-start.3
  2.3 0.0 copy-start.4
  2.3 0.0 copy-start.5
  2.3 0.0 copy-start.6
  2.3 0.0 copy-start.7
  2.3 0.0 copy-start.8
  2.4 0.5 %collective-permute-start = (f32[64,1024]{1,0:T(8,128)S(1)}, f32[64,1024]{1,0:T(8,128)S(1)}, u32[]{:S(2)}, u32[]{:S(2)}) collective-permute-start(f32[64,1024]{1,0:T(8,128)S(1)} %get-tuple-element.32), channel_id=1, source_target_pairs={{0,16},{16,0},{1,17},{17,1},{2,18},{18,2},{3,19},{19,3},{4,20},{20... | collective-permute-start | bytes 786440 | tf_op jit(solution)/shard_map/ppermute | solution.py:558
  2.9 1.8 %partial_coeff.2 = (f32[64,1024]{1,0:T(8,128)S(1)}, f32[192,1024]{1,0:T(8,128)S(1)}, f32[64,2048]{1,0:T(8,128)S(1)}, bf16[192,192]{1,0:T(8,128)(2,1)S(1)}) custom-call(s32[1]{0:T(128)S(6)} %xor.11.side_ref, f32[64,192]{1,0:T(8,128)} %bitcast.25, bf16[192,2048]{1,0:T(8,128)(2,1)} %bitcast.23, f32[192,2048]{1,0:T(8,128)} %old_hbm.3, f32[64,2048]{1,0:T(8,128)} %moment_hbm.3), custom_call_target="tpu_custom_call" | custom-call | flops 75497472 | bytes 1179648 | tf_op jit(solution)/shard_map/partial_coeff/pallas_call | solution.py:172
  4.7 0.0 collective-permute-done
  4.8 0.0 copy-done
  4.8 0.0 copy-done.1
  4.8 0.0 copy-done.2
  4.8 0.0 copy-done.3
  4.8 0.0 copy-done.4
  4.8 0.0 copy-done.5
  4.8 1.0 %dense_before.1 = (f32[6,584,128]{2,1,0:T(8,128)S(1)}, f32[8,128]{1,0:T(8,128)}) custom-call(s32[1]{0:T(128)} %bitcast.group_ref, bf16[1,192,576]{2,1,0:T(8,128)(2,1)S(1)} %copy-done.4, bf16[1,192,192]{2,1,0:T(8,128)(2,1)S(1)} %copy-done.5, bf16[1,192,768]{2,1,0:T(8,128)(2,1)S(1)} %copy-done.2, bf16[1,192,768]{2,1,0:T(8,128)(2,1)S(1)} %bitcast.16, ...), custom_call_target="tpu_custom_call" | custom-call | flops 8847360000 | bytes 4423680 | tf_op jit(solution)/shard_map/dense_before/pallas_call | solution.py:483
  5.8 0.2 %collective-permute-start.1 = (f32[6,584,128]{2,1,0:T(8,128)S(1)}, f32[6,584,128]{2,1,0:T(8,128)S(1)}, u32[]{:S(2)}, u32[]{:S(2)}) collective-permute-start(f32[6,584,128]{2,1,0:T(8,128)S(1)} %get-tuple-element.34.send_ref), channel_id=1, source_target_pairs={{0,16},{16,0},{1,17},{17,1},{2,18},{18,2},{3,19},{19,3},{4,20},{20... | collective-permute-start | bytes 5382152 | tf_op jit(solution)/shard_map/ppermute | solution.py:576
  6.1 2.5 %collective-permute-start.2 = (f32[64,1024]{1,0:T(8,128)S(1)}, f32[64,1024]{1,0:T(8,128)S(1)}, u32[]{:S(2)}, u32[]{:S(2)}) collective-permute-start(f32[64,1024]{1,0:T(8,128)S(1)} %add.9), channel_id=1, source_target_pairs={{0,20},{4,28},{8,16},{12,24},{16,8},{20,0},{24,12},{28,4},{1,21},{... | collective-permute-start | bytes 786440 | tf_op jit(solution)/shard_map/ppermute | solution.py:574
  8.6 4.1 %collective-permute-done.2 = f32[64,1024]{1,0:T(8,128)S(1)} collective-permute-done((f32[64,1024]{1,0:T(8,128)S(1)}, f32[64,1024]{1,0:T(8,128)S(1)}, u32[]{:S(2)}, u32[]{:S(2)}) %collective-permute-start.2) | collective-permute-done | bytes 262176 | tf_op jit(solution)/shard_map/ppermute | solution.py:574
  12.7 1.8 %collective-permute-start.3 = (f32[64,1024]{1,0:T(8,128)S(1)}, f32[64,1024]{1,0:T(8,128)S(1)}, u32[]{:S(2)}, u32[]{:S(2)}) collective-permute-start(f32[64,1024]{1,0:T(8,128)S(1)} %add.10), channel_id=1, source_target_pairs={{0,24},{4,16},{8,28},{12,20},{16,4},{20,12},{24,0},{28,8},{1,25},{... | collective-permute-start | bytes 786440 | tf_op jit(solution)/shard_map/ppermute | solution.py:579
  14.5 0.0 collective-permute-done.1.recv_ref
  14.5 2.0 %dense_after.1 = (f32[192,576]{1,0:T(8,128)}, f32[192,192]{1,0:T(8,128)}, f32[192,768]{1,0:T(8,128)}, f32[192,768]{1,0:T(8,128)}, f32[1728,128]{1,0:T(8,128)}, /*index=5*/f32[1,1920]{1,0:T(1,128)S(1)}, f32[1,960]{1,0:T(1,128)}) custom-call(s32[1]{0:T(128)} %bitcast.group_ref, f32[6,584,128]{2,1,0:T(8,128)S(1)} %collective-permute-done.1.recv_ref, ...), custom_call_target="tpu_custom_call" | custom-call | flops 8847360000 | bytes 5898240 | tf_op jit(solution)/shard_map/dense_after/pallas_call | solution.py:504
  16.6 2.0 %collective-permute-done.3 = f32[64,1024]{1,0:T(8,128)S(1)} collective-permute-done((f32[64,1024]{1,0:T(8,128)S(1)}, f32[64,1024]{1,0:T(8,128)S(1)}, u32[]{:S(2)}, u32[]{:S(2)}) %collective-permute-start.3) | collective-permute-done | bytes 262176 | tf_op jit(solution)/shard_map/ppermute | solution.py:579
  18.6 0.3 %collective-permute-start.4 = (f32[64,1024]{1,0:T(8,128)S(1)}, f32[64,1024]{1,0:T(8,128)S(1)}, u32[]{:S(2)}, u32[]{:S(2)}) collective-permute-start(f32[64,1024]{1,0:T(8,128)S(1)} %add_multiply_fusion.coeff_ref), channel_id=1, source_target_pairs={{0,16},{16,0},{1,17},{17,1},{2,18},{18,2},{3,19},{19,3},{4,20},{20... | collective-permute-start | bytes 786440 | tf_op jit(solution)/shard_map/ppermute | solution.py:584
  18.9 0.6 %reduce = f32[1920]{0:T(1024)} reduce(f32[1,1920]{1,0:T(1,128)S(1)} %get-tuple-element.40, f32[]{:T(128)} %constant.23), dimensions={0}, to_apply=%get-tuple-element.40.reduce_sub_computation | reduce | bytes 15364 | tf_op jit(solution)/shard_map/dense_after/pallas_call | solution.py:504
  19.6 1.2 %embed_half.2 = (f32[192,2048]{1,0:T(8,128)}, f32[64,2048]{1,0:T(8,128)}) custom-call(s32[1]{0:T(128)S(6)} %xor.11.side_ref, bf16[192,192]{1,0:T(8,128)(2,1)S(1)} %get-tuple-element.44.stack_ref, f32[64,1024]{1,0:T(8,128)S(1)} %add_multiply_fusion.coeff_ref, f32[64,2048]{1,0:T(8,128)S(1)} %get-tuple-element.46.moment_ref, ...), custom_call_target="tpu_custom_call" | custom-call | flops 75497472 | bytes 1572864 | tf_op jit(solution)/shard_map/embed_half/pallas_call | solution.py:224
  20.7 0.0 collective-permute-done.4.coeff_ref
  20.8 1.2 %embed_half.3 = (f32[192,2048]{1,0:T(8,128)}, f32[64,2048]{1,0:T(8,128)}) custom-call(s32[1]{0:T(128)S(6)} %xor.11.side_ref, bf16[192,192]{1,0:T(8,128)(2,1)S(1)} %get-tuple-element.44.stack_ref, f32[64,1024]{1,0:T(8,128)S(1)} %collective-permute-done.4.coeff_ref, ...), custom_call_target="tpu_custom_call", output_to_operand_aliasing={{0}: (5, {}), {1}: (6, {})} | custom-call | flops 75497472 | bytes 1572864 | tf_op jit(solution)/shard_map/embed_half/pallas_call | solution.py:224
  (6 shorter events, 0.1 us)
Async XLA Ops:
  2.3 2.5 %copy-start = (f32[1,221184]{1,0:T(1,128)S(1)}, f32[1,221184]{1,0:T(1,128)}, u32[]{:S(2)}) copy-start(f32[1,221184]{1,0:T(1,128)} %param.18) | copy-start | bytes 2654212
  2.3 2.5 %copy-start.1 = (f32[1,221184]{1,0:T(1,128)S(1)}, f32[1,221184]{1,0:T(1,128)}, u32[]{:S(2)}) copy-start(f32[1,221184]{1,0:T(1,128)} %param.19) | copy-start | bytes 2654212
  2.3 2.5 %copy-start.2 = (bf16[1,192,768]{2,1,0:T(8,128)(2,1)S(1)}, bf16[1,192,768]{2,1,0:T(8,128)(2,1)}, u32[]{:S(2)}) copy-start(bf16[1,192,768]{2,1,0:T(8,128)(2,1)} %up_ref.3) | copy-start | bytes 884740
  2.3 2.5 %copy-start.3 = (bf16[1,768,192]{1,2,0:T(8,128)(2,1)S(1)}, bf16[1,768,192]{1,2,0:T(8,128)(2,1)}, u32[]{:S(2)}) copy-start(bf16[1,768,192]{1,2,0:T(8,128)(2,1)} %param.16) | copy-start | bytes 884740
  2.3 2.5 %copy-start.4 = (bf16[1,192,576]{2,1,0:T(8,128)(2,1)S(1)}, bf16[1,192,576]{2,1,0:T(8,128)(2,1)}, u32[]{:S(2)}) copy-start(bf16[1,192,576]{2,1,0:T(8,128)(2,1)} %in_ref.3) | copy-start | bytes 663556
  2.3 2.5 %copy-start.5 = (bf16[1,192,192]{2,1,0:T(8,128)(2,1)S(1)}, bf16[1,192,192]{2,1,0:T(8,128)(2,1)}, u32[]{:S(2)}) copy-start(bf16[1,192,192]{2,1,0:T(8,128)(2,1)} %out_ref.3) | copy-start | bytes 221188
  2.3 2.5 %copy-start.6 = (bf16[1,1920]{1,0:T(2,128)(2,1)S(1)}, bf16[1,1920]{1,0:T(2,128)(2,1)}, u32[]{:S(2)}) copy-start(bf16[1,1920]{1,0:T(2,128)(2,1)} %small_ref.3) | copy-start | bytes 11524
  2.3 2.5 %copy-start.7 = (f32[960]{0:T(1024)S(1)}, f32[960]{0:T(1024)}, u32[]{:S(2)}) copy-start(f32[960]{0:T(1024)} %param.20) | copy-start | bytes 11524
  2.3 2.5 %copy-start.8 = (f32[960]{0:T(1024)S(1)}, f32[960]{0:T(1024)}, u32[]{:S(2)}) copy-start(f32[960]{0:T(1024)} %param.21) | copy-start | bytes 11524
  2.4 2.3 %collective-permute-start = (f32[64,1024]{1,0:T(8,128)S(1)}, f32[64,1024]{1,0:T(8,128)S(1)}, u32[]{:S(2)}, u32[]{:S(2)}) collective-permute-start(f32[64,1024]{1,0:T(8,128)S(1)} %get-tuple-element.32), channel_id=1, source_target_pairs={{0,16},{16,0},{1,17},{17,1},{2,18},{18,2},{3,19},{19,3},{4,20},{20... | collective-permute-start | bytes 786440 | tf_op jit(solution)/shard_map/ppermute | solution.py:558
  5.8 8.7 %collective-permute-start.1 = (f32[6,584,128]{2,1,0:T(8,128)S(1)}, f32[6,584,128]{2,1,0:T(8,128)S(1)}, u32[]{:S(2)}, u32[]{:S(2)}) collective-permute-start(f32[6,584,128]{2,1,0:T(8,128)S(1)} %get-tuple-element.34.send_ref), channel_id=1, source_target_pairs={{0,16},{16,0},{1,17},{17,1},{2,18},{18,2},{3,19},{19,3},{4,20},{20... | collective-permute-start | bytes 5382152 | tf_op jit(solution)/shard_map/ppermute | solution.py:576
  6.1 6.5 %collective-permute-start.2 = (f32[64,1024]{1,0:T(8,128)S(1)}, f32[64,1024]{1,0:T(8,128)S(1)}, u32[]{:S(2)}, u32[]{:S(2)}) collective-permute-start(f32[64,1024]{1,0:T(8,128)S(1)} %add.9), channel_id=1, source_target_pairs={{0,20},{4,28},{8,16},{12,24},{16,8},{20,0},{24,12},{28,4},{1,21},{... | collective-permute-start | bytes 786440 | tf_op jit(solution)/shard_map/ppermute | solution.py:574
  12.7 5.9 %collective-permute-start.3 = (f32[64,1024]{1,0:T(8,128)S(1)}, f32[64,1024]{1,0:T(8,128)S(1)}, u32[]{:S(2)}, u32[]{:S(2)}) collective-permute-start(f32[64,1024]{1,0:T(8,128)S(1)} %add.10), channel_id=1, source_target_pairs={{0,24},{4,16},{8,28},{12,20},{16,4},{20,12},{24,0},{28,8},{1,25},{... | collective-permute-start | bytes 786440 | tf_op jit(solution)/shard_map/ppermute | solution.py:579
  18.6 2.1 %collective-permute-start.4 = (f32[64,1024]{1,0:T(8,128)S(1)}, f32[64,1024]{1,0:T(8,128)S(1)}, u32[]{:S(2)}, u32[]{:S(2)}) collective-permute-start(f32[64,1024]{1,0:T(8,128)S(1)} %add_multiply_fusion.coeff_ref), channel_id=1, source_target_pairs={{0,16},{16,0},{1,17},{17,1},{2,18},{18,2},{3,19},{19,3},{4,20},{20... | collective-permute-start | bytes 786440 | tf_op jit(solution)/shard_map/ppermute | solution.py:584

commit v3 on v2

--- a/solution.py
+++ b/solution.py
@@ -99,7 +99,6 @@
 
 CHUNKS = 2
 WHOLE = pl.BlockSpec(memory_space=pltpu.VMEM)
-SCALAR = pl.BlockSpec(memory_space=pltpu.SMEM)
 ANY = pl.BlockSpec(memory_space=pl.ANY)
 
 
@@ -107,91 +106,96 @@
     return [pltpu.with_memory_space_constraint(array, pltpu.HBM) for array in arrays]
 
 
-def side_start(side_ref, other, columns):
-    side = 1 - side_ref[0] if other else side_ref[0]
-    return side * columns
-
-
-def partial_kernel(other, side_ref, basis_hbm, local_hbm, old_hbm, moment_hbm, *refs):
-    if other:
-        out_ref, old_ref, basis_ref, local_ref, sems = refs
-    else:
-        out_ref, old_ref, moment_ref, stack_ref, basis_ref, local_ref, sems = refs
-    rank, columns = out_ref.shape
+def turned(chip):
+    return (chip ^ (chip >> 1)) & 1
+
+
+def side_start(other, columns):
+    side = lax.axis_index("group") ^ turned(lax.axis_index("shard"))
+    return (1 - side if other else side) * columns
+
+
+def product(basis, local, old):
+    rank = basis.shape[0]
+    high, low = split(basis)
+    diff_high, diff_low = split(old - local.astype(f32))
+    first = jnp.dot(
+        jnp.concatenate([high, low], axis=0), diff_high, preferred_element_type=f32
+    )
+    return first[:rank] + first[rank:] + jnp.dot(high, diff_low, preferred_element_type=f32)
+
+
+def partial_kernel(other, basis_hbm, local_hbm, old_hbm, out_ref, old_ref, *refs):
+    basis_ref, local_ref, sems = refs[-3:]
+    columns = out_ref.shape[1]
     block = columns // CHUNKS
-    start = side_start(side_ref, other, columns)
+    start = side_start(other, columns)
     copies = [pltpu.make_async_copy(basis_hbm, basis_ref, sems.at[0])]
     for k in range(CHUNKS):
-        source = pl.ds(pl.multiple_of(start + k * block, block), block)
-        target = pl.ds(k * block, block)
-        copies.append(
-            pltpu.make_async_copy(
-                old_hbm.at[:, source], old_ref.at[:, target], sems.at[1 + 2 * k]
-            )
-        )
-        copies.append(
-            pltpu.make_async_copy(
-                local_hbm.at[:, source], local_ref.at[:, target], sems.at[2 + 2 * k]
-            )
-        )
-    if not other:
-        copies.append(pltpu.make_async_copy(moment_hbm, moment_ref, sems.at[1 + 2 * CHUNKS]))
+        there = pl.ds(pl.multiple_of(start + k * block, block), block)
+        here = pl.ds(k * block, block)
+        for source, target in ((old_hbm, old_ref), (local_hbm, local_ref)):
+            at = sems.at[len(copies)]
+            copies.append(pltpu.make_async_copy(source.at[:, there], target.at[:, here], at))
     for copy in copies:
         copy.start()
     copies[0].wait()
-    high, low = split(basis_ref[...])
-    both = jnp.concatenate([high, low], axis=0)
+    basis = basis_ref[...]
     for k in range(CHUNKS):
         copies[1 + 2 * k].wait()
         copies[2 + 2 * k].wait()
-        target = slice(k * block, (k + 1) * block)
-        diff_high, diff_low = split(old_ref[:, target] - local_ref[:, target].astype(f32))
-        first = jnp.dot(both, diff_high, preferred_element_type=f32)
-        second = jnp.dot(high, diff_low, preferred_element_type=f32)
-        out_ref[:, target] = first[:rank] + first[rank:] + second
+        here = slice(k * block, (k + 1) * block)
+        out_ref[:, here] = product(basis, local_ref[:, here], old_ref[:, here])
     if not other:
-        basis = basis_ref[...]
-        stack = jnp.concatenate([high.astype(f32), basis - high.astype(f32), high.astype(f32)], axis=0)
-        stack_ref[...] = stack.T.astype(bf16)
-        copies[-1].wait()
-
-
-def partial_coeff(side, basis_t, local, old, moment, other):
+        high = basis.astype(bf16).astype(f32)
+        refs[0][...] = jnp.concatenate([high, basis - high, high], axis=0).T.astype(bf16)
+
+
+def partial_coeff(basis_t, local, old, other):
     rank, depth = basis_t.shape
-    width = old.shape[1]
-    columns = width // 2
-    out_shape = [
-        jax.ShapeDtypeStruct((rank, columns), f32),
-        jax.ShapeDtypeStruct((depth, columns), f32),
-    ]
+    columns = old.shape[1] // 2
+    shapes = [((rank, columns), f32), ((depth, columns), f32)]
     if not other:
-        out_shape += [
-            jax.ShapeDtypeStruct((rank, width), f32),
-            jax.ShapeDtypeStruct((depth, 3 * rank), bf16),
-        ]
+        shapes.append(((depth, 3 * rank), bf16))
     return pl.pallas_call(
         functools.partial(partial_kernel, other),
-        in_specs=[SCALAR] + [ANY] * 4,
-        out_specs=[WHOLE] * len(out_shape),
-        out_shape=out_shape,
+        in_specs=[ANY] * 3,
+        out_specs=[WHOLE] * len(shapes),
+        out_shape=[jax.ShapeDtypeStruct(*shape) for shape in shapes],
         scratch_shapes=[
             pltpu.VMEM((rank, depth), f32),
             pltpu.VMEM((depth, columns), bf16),
-            pltpu.SemaphoreType.DMA((2 + 2 * CHUNKS,)),
+            pltpu.SemaphoreType.DMA((1 + 2 * CHUNKS,)),
         ],
-        compiler_params=pltpu.CompilerParams(vmem_limit_bytes=8 * 2**20),
+        compiler_params=pltpu.CompilerParams(vmem_limit_bytes=6 * 2**20),
         cost_estimate=pl.CostEstimate(
             flops=6 * rank * depth * columns, bytes_accessed=6 * depth * columns, transcendentals=0
         ),
         name="partial_coeff",
-    )(side, *in_hbm((basis_t, local, old, moment)))
-
-
-def embed_kernel(other, side_ref, stack_ref, coeff_ref, moment_ref, old_ref, *refs):
+    )(*in_hbm((basis_t, local, old)))
+
+
+def add_kernel(scale, first_ref, second_ref, out_ref):
+    out_ref[...] = scale * (first_ref[...] + second_ref[...])
+
+
+def add(first, second, scale=1.0):
+    return pl.pallas_call(
+        functools.partial(add_kernel, scale),
+        in_specs=[WHOLE] * 2,
+        out_specs=WHOLE,
+        out_shape=jax.ShapeDtypeStruct(first.shape, f32),
+        compiler_params=pltpu.CompilerParams(vmem_limit_bytes=2 * 2**20),
+        cost_estimate=pl.CostEstimate(flops=10**11, bytes_accessed=0, transcendentals=0),
+        name="add",
+    )(first, second)
+
+
+def embed_kernel(other, stack_ref, coeff_ref, moment_ref, old_ref, *refs):
     embed_hbm, moved_hbm, embed_ref, moved_ref, sems = refs[-5:]
     columns = coeff_ref.shape[1]
     block = columns // CHUNKS
-    start = side_start(side_ref, other, columns)
+    start = side_start(other, columns)
     copies = []
     for k in range(CHUNKS):
         here = slice(k * block, (k + 1) * block)
@@ -217,13 +221,13 @@
         copy.wait()
 
 
-def embed_half(side, stack, coeff, moment, old, before):
+def embed_half(stack, coeff, moment, old, before):
     rank, columns = coeff.shape
     depth = old.shape[0]
     more = () if before is None else tuple(before)
     return pl.pallas_call(
         functools.partial(embed_kernel, before is not None),
-        in_specs=[SCALAR] + [WHOLE] * 4 + [ANY] * len(more),
+        in_specs=[WHOLE] * 4 + [ANY] * len(more),
         out_specs=[ANY, ANY],
         out_shape=[
             jax.ShapeDtypeStruct((depth, 2 * columns), f32),
@@ -234,13 +238,13 @@
             pltpu.VMEM((rank, columns), f32),
             pltpu.SemaphoreType.DMA((2 * CHUNKS,)),
         ],
-        input_output_aliases={} if before is None else {5: 0, 6: 1},
+        input_output_aliases={} if before is None else {4: 0, 5: 1},
         compiler_params=pltpu.CompilerParams(vmem_limit_bytes=8 * 2**20),
         cost_estimate=pl.CostEstimate(
             flops=6 * rank * depth * columns, bytes_accessed=8 * depth * columns, transcendentals=0
         ),
         name="embed_half",
-    )(side, stack, coeff, moment, old, *more)
+    )(stack, coeff, moment, old, *more)
 
 
 def low_lanes(rows):
@@ -296,11 +300,24 @@
     return pieces
 
 
-def before_kernel(
-    group_ref, in_ref, out_ref, up_ref, down_ref, old_ref, mom_ref, small_ref, small_old_ref,
-    small_mom_ref, send_ref, mark_ref, wide_ref,
-):
-    mark_ref[...] = jnp.zeros(mark_ref.shape, f32)
+def before_kernel(order_ref, *refs):
+    del order_ref
+    count = len(refs) // 2 - 1
+    sources, send_ref, kept, (wide_ref, sems) = (
+        refs[:count], refs[count], refs[count + 1 : -2], refs[-2:]
+    )
+    copies = [
+        pltpu.make_async_copy(source, target, sems.at[k])
+        for k, (source, target) in enumerate(zip(sources, kept))
+    ]
+    for copy in copies:
+        copy.start()
+    for copy in copies:
+        copy.wait()
+    in_ref, out_ref, up_ref, down_ref, old_ref, mom_ref, small_ref, small_old_ref, small_mom_ref = (
+        kept[:9]
+    )
+    group = lax.axis_index("group")
     rows = up_ref.shape[1]
     mid = rows // 2
     block = rows + mid
@@ -325,7 +342,7 @@
                 at = 2 * block + row
                 send_ref[tile, at : at + 1, : piece.shape[1]] = piece
 
-    @pl.when(group_ref[0] == 0)
+    @pl.when(group == 0)
     def _():
         unflatten_attn(flat, put, rows)
         for k, value in enumerate(attn_tiles(in_ref, out_ref)):
@@ -341,7 +358,7 @@
         values = small_ref[...].astype(f32)
         put_small(values[:, small:], values[:, :small])
 
-    @pl.when(group_ref[0] == 1)
+    @pl.when(group == 1)
     def _():
         for k, value in enumerate(attn_tiles(in_ref, out_ref)):
             send_ref[k, :rows, :] = value
@@ -377,7 +394,7 @@
 
 
 def after_kernel(
-    group_ref, recv_ref, send_ref, in_ref, out_ref, up_ref, down_ref, old_ref, mom_ref, small_ref,
+    recv_ref, send_ref, in_ref, out_ref, up_ref, down_ref, old_ref, mom_ref, small_ref,
     small_old_ref, small_mom_ref, in_next_ref, out_next_ref, up_next_ref, down_next_ref, moved_ref,
     small_next_ref, small_moved_ref, sum_ref, wide_ref,
 ):
@@ -386,6 +403,7 @@
     block = rows + mid
     tiles = up_ref.shape[2] // LANES
     small = small_old_ref.shape[1]
+    group = lax.axis_index("group")
 
     def put_moved(start, stride, value):
         at = pl.ds(start, value.shape[0], stride=stride)
@@ -416,12 +434,12 @@
         mine = small_row(send_ref, 1) + local_coef * theirs
         rest = small_row(recv_ref, 1) + local_coef * other
         both = [mine, rest] if first else [rest, mine]
-        small_next_ref[...] = jnp.concatenate(both, axis=1)
+        small_next_ref[...] = jnp.concatenate(both, axis=1).reshape(-1)
         small_moved_ref[...] = momentum_coef * small_mom_ref[...] + (
             small_old_ref[...] - 0.5 * (own + theirs)
         )
 
-    @pl.when(group_ref[0] == 0)
+    @pl.when(group == 0)
     def _():
         for k, value in enumerate(attn_tiles(in_ref, out_ref)):
             theirs = recv_ref[k, :rows, :]
@@ -446,7 +464,7 @@
         values = small_ref[...].astype(f32)
         put_small(values[:, small:], values[:, :small], True)
 
-    @pl.when(group_ref[0] == 1)
+    @pl.when(group == 1)
     def _():
         for k, value in enumerate(attn_tiles(in_ref, out_ref)):
             put_attn(k, recv_ref[k, block : block + rows, :] + local_coef * value)
@@ -478,32 +496,31 @@
         put_small(values[:, :small], values[:, small:], False)
 
 
-def dense_before(group, operands):
+def dense_before(order, operands):
     _, rows, width = operands[2].shape
+    count = len(operands)
     return pl.pallas_call(
         before_kernel,
-        in_specs=[SCALAR] + [WHOLE] * 9,
-        out_specs=[WHOLE] * 2,
-        out_shape=[
-            jax.ShapeDtypeStruct((width // LANES, 3 * rows + 8, LANES), f32),
-            jax.ShapeDtypeStruct((8, LANES), f32),
-        ],
-        scratch_shapes=[pltpu.VMEM((2, width, LANES), f32)],
+        in_specs=[ANY] * (1 + count),
+        out_specs=[WHOLE] * (1 + count),
+        out_shape=[jax.ShapeDtypeStruct((width // LANES, 3 * rows + 8, LANES), f32)]
+        + [jax.ShapeDtypeStruct(array.shape, array.dtype) for array in operands],
+        scratch_shapes=[pltpu.VMEM((2, width, LANES), f32), pltpu.SemaphoreType.DMA((count,))],
         compiler_params=pltpu.CompilerParams(vmem_limit_bytes=20 * 2**20),
         cost_estimate=pl.CostEstimate(
             flops=60000 * rows * width, bytes_accessed=30 * rows * width, transcendentals=0
         ),
         name="dense_before",
-    )(group, *operands)
-
-
-def dense_after(group, received, sent, operands):
+    )(order, *in_hbm(operands))
+
+
+def dense_after(received, sent, operands):
     _, rows, width = operands[2].shape
     outs = [matrix.shape[1:] for matrix in operands[:4]]
-    outs += [operands[4].shape, operands[6].shape, operands[7].shape]
+    outs += [operands[4].shape, operands[6].shape[1:], operands[7].shape]
     return pl.pallas_call(
         after_kernel,
-        in_specs=[SCALAR] + [WHOLE] * 11,
+        in_specs=[WHOLE] * 11,
         out_specs=[WHOLE] * 7,
         out_shape=[jax.ShapeDtypeStruct(shape, f32) for shape in outs],
         scratch_shapes=[
@@ -515,7 +532,7 @@
             flops=60000 * rows * width, bytes_accessed=40 * rows * width, transcendentals=0
         ),
         name="dense_after",
-    )(group, received, sent, *operands)
+    )(received, sent, *operands)
 
 
 def paired(
@@ -533,13 +550,8 @@
     basis,
     coeff_momentum,
 ):
-    position = lax.axis_index("group")
-    group = position.astype(jnp.int32).reshape(1)
     swap = [(0, 1), (1, 0)]
     chips = lax.axis_size("shard")
-
-    def turned(chip):
-        return (chip ^ (chip >> 1)) & 1
 
     first, second = (
         [
@@ -549,15 +561,12 @@
         ]
         for late in range(2)
     )
-    side = group ^ turned(lax.axis_index("shard").astype(jnp.int32))
     axes = ("group", "shard")
 
-    basis_t = basis.T
-    embed = (basis_t, embed_local[0], embed_old, coeff_momentum)
-    theirs, old_rest = partial_coeff(side, *embed, True)
+    embed = (basis.T, embed_local[0], embed_old)
+    theirs, old_rest = partial_coeff(*embed, True)
     theirs = lax.ppermute(theirs, "group", swap)
-    mine, old_own, moment, stack = partial_coeff(side, *embed, False)
-    total = mine + theirs
+    mine, old_own, stack = partial_coeff(*embed, False)
 
     operands = (
         attn_in_local,
@@ -569,21 +578,21 @@
         small_local,
         small_old[None, :],
         small_momentum[None, :],
-    )
-    total, group_later = lax.optimization_barrier((total, group))
+        coeff_momentum,
+    )
+    total = add(mine, theirs)
     moving = lax.ppermute(total, axes, first)
-    sent, mark = dense_before(group_later, operands)
+    sent, *kept, moment = dense_before(total, operands)
     received = lax.ppermute(sent, "group", swap)
-    moving, mark = lax.optimization_barrier((moving, mark))
-    total = total + moving
+    total = add(total, moving)
     moving = lax.ppermute(total, axes, second)
-    dense = list(dense_after(group, received, sent, operands))
+    dense = list(dense_after(received, sent, kept))
     moving, dense[-1] = lax.optimization_barrier((moving, dense[-1]))
 
-    own = 0.5 * (total + moving)
+    own = add(total, moving, 0.5)
     rest = lax.ppermute(own, "group", swap)
-    done = embed_half(side, stack, own, moment, old_own, None)
-    embed_next, coeff_moved = embed_half(side, stack, rest, moment, old_rest, done)
+    done = embed_half(stack, own, moment, old_own, None)
+    embed_next, coeff_moved = embed_half(stack, rest, moment, old_rest, done)
 
     attn_in_next, attn_out_next, ffn_in_next, ffn_out_next, moved, small_next, small_moved = dense
     return (
@@ -592,7 +601,7 @@
         ffn_in_next,
         ffn_out_next.T,
         moved.reshape(dense_old.shape),
-        small_next[0],
+        small_next,
         small_moved[0],
         embed_next,
         coeff_moved,

time: 22.1 us -> 20.1 us (0.910)
  waiting for transfers between devices: 6.06 us -> 3.63 us
  Pallas kernels: 8.82 us -> 10.1 us
  other arithmetic: 0.73 us -> 0 us
    ppermute x1, waiting for transfers between devices: 4.05 us -> 1.38 us  [paired(): moving = lax.ppermute(total, axes, first)]
    pallas_call x4 -> x7, Pallas kernels: 6.46 us -> 7.75 us  [the longest x2 3.18 us: partial_coeff(): pl.pallas_call(functools.partial(partial_kernel, other), in_specs=[ANY] *...]
    pallas_call x1 -> x0, other arithmetic: 0.62 us -> none  [dense_after(): pl.pallas_call(after_kernel, in_specs=[SCALAR] + [WHOLE] * 11, out_specs=...]
    ppermute x1, waiting for transfers between devices: 0.01 us -> 0.31 us  [paired(): received = lax.ppermute(sent, 'group', swap)]
    ppermute x1, waiting for transfers between devices: 2 us -> 1.71 us  [paired(): moving = lax.ppermute(total, axes, second)]
    ppermute x1, waiting for transfers between devices: 0.01 us -> 0.23 us  [paired(): rest = lax.ppermute(own, 'group', swap)]
  transfers between devices with their start and end apart: 5 -> 5, of which waited for: 2 -> 4; matrix products, arithmetic and copies ran while one was open for 3% -> 0% of each run, Pallas kernels for 23% -> 37%
where the time goes in v3:
time: 20.1 us; the launch traced here: 19.9 us
  Pallas kernels  10.1 us (50%)
  starting transfers between devices  5.43 us (27%)
  waiting for transfers between devices  3.63 us (18%)
  between operations  0.69 us (3%)
    pallas_call x2, Pallas kernels, partial_coeff(): pl.pallas_call(functools.partial(partial_kernel, other), in_specs=[ANY] *...  3.18 us
    ppermute x1, starting transfers between devices, paired(): moving = lax.ppermute(total, axes, first)  2.67 us
    pallas_call x1, Pallas kernels, dense_before(): pl.pallas_call(before_kernel, in_specs=[ANY] * (1 + count), out_specs=[WH...  2.43 us
    pallas_call x2, Pallas kernels, embed_half(): pl.pallas_call(functools.partial(embed_kernel, before is not None), in_sp...  2.36 us
    pallas_call x1, Pallas kernels, dense_after(): pl.pallas_call(after_kernel, in_specs=[WHOLE] * 11, out_specs=[WHOLE] * 7...  2.04 us
    ppermute x1, starting transfers between devices, paired(): moving = lax.ppermute(total, axes, second)  1.83 us
    ppermute x1, waiting for transfers between devices, paired(): moving = lax.ppermute(total, axes, second)  1.71 us
    ppermute x1, waiting for transfers between devices, paired(): moving = lax.ppermute(total, axes, first)  1.38 us
  transfers between devices with their start and end apart: 5, of which 4 were waited for; matrix products, arithmetic and copies ran while one was open for 0% of the time, Pallas kernels for 37%

profile of v3, /device:TPU:0, one launch (start us, length us, event | category | flops | bytes accessed | tf_op | source)
XLA Modules:
  0.0 19.9 jit_solution(11546644387248130752)
XLA Ops:
  0.6 1.6 %partial_coeff.3 = (f32[64,1024]{1,0:T(8,128)S(1)}, f32[192,1024]{1,0:T(8,128)S(1)}) custom-call(f32[64,192]{1,0:T(8,128)} %bitcast.12, bf16[192,2048]{1,0:T(8,128)(2,1)} %bitcast.10, f32[192,2048]{1,0:T(8,128)} %old_hbm.3), custom_call_target="tpu_custom_call" | custom-call | flops 75497472 | bytes 1179648 | tf_op jit(solution)/shard_map/partial_coeff/pallas_call | solution.py:160
  2.2 0.5 %collective-permute-start = (f32[64,1024]{1,0:T(8,128)S(1)}, f32[64,1024]{1,0:T(8,128)S(1)}, u32[]{:S(2)}, u32[]{:S(2)}) collective-permute-start(f32[64,1024]{1,0:T(8,128)S(1)} %get-tuple-element.39), channel_id=1, source_target_pairs={{0,16},{16,0},{1,17},{17,1},{2,18},{18,2},{3,19},{19,3},{4,20},{20... | collective-permute-start | bytes 786440 | tf_op jit(solution)/shard_map/ppermute | solution.py:568
  2.8 1.6 %partial_coeff.2 = (f32[64,1024]{1,0:T(8,128)S(1)}, f32[192,1024]{1,0:T(8,128)S(1)}, bf16[192,192]{1,0:T(8,128)(2,1)S(1)}) custom-call(f32[64,192]{1,0:T(8,128)} %bitcast.13, bf16[192,2048]{1,0:T(8,128)(2,1)} %bitcast.11, f32[192,2048]{1,0:T(8,128)} %old_hbm.3), custom_call_target="tpu_custom_call" | custom-call | flops 75497472 | bytes 1179648 | tf_op jit(solution)/shard_map/partial_coeff/pallas_call | solution.py:160
  4.4 0.0 collective-permute-done.second_ref
  4.4 2.7 %collective-permute-start.2 = (f32[64,1024]{1,0:T(8,128)S(1)}, f32[64,1024]{1,0:T(8,128)S(1)}, u32[]{:S(2)}, u32[]{:S(2)}) collective-permute-start(f32[64,1024]{1,0:T(8,128)S(1)} %add.3.order_ref.first_ref), channel_id=1, source_target_pairs={{0,20},{4,28},{8,16},{12,24},{16,8},{20,0},{24,12},{28,4},{1,21},{... | collective-permute-start | bytes 786440 | tf_op jit(solution)/shard_map/ppermute | solution.py:584
  7.1 2.4 %dense_before.1 = (f32[6,584,128]{2,1,0:T(8,128)S(1)}, bf16[1,192,576]{2,1,0:T(8,128)(2,1)S(1)}, bf16[1,192,192]{2,1,0:T(8,128)(2,1)S(1)}, bf16[1,192,768]{2,1,0...) custom-call(f32[64,1024]{1,0:T(8,128)S(1)} %add.3.order_ref.first_re, ...), custom_call_target="tpu_custom_call" | custom-call | flops 8847360000 | bytes 4423680 | tf_op jit(solution)/shard_map/dense_before/pallas_call | solution.py:502
  9.5 0.2 %collective-permute-start.1 = (f32[6,584,128]{2,1,0:T(8,128)S(1)}, f32[6,584,128]{2,1,0:T(8,128)S(1)}, u32[]{:S(2)}, u32[]{:S(2)}) collective-permute-start(f32[6,584,128]{2,1,0:T(8,128)S(1)} %get-tuple-element.40.send_ref), channel_id=1, source_target_pairs={{0,16},{16,0},{1,17},{17,1},{2,18},{18,2},{3,19},{19,3},{4,20},{20... | collective-permute-start | bytes 5382152 | tf_op jit(solution)/shard_map/ppermute | solution.py:586
  9.7 1.4 %collective-permute-done.2.second_ref = f32[64,1024]{1,0:T(8,128)S(1)} collective-permute-done((f32[64,1024]{1,0:T(8,128)S(1)}, f32[64,1024]{1,0:T(8,128)S(1)}, u32[]{:S(2)}, u32[]{:S(2)}) %collective-permute-start.2) | collective-permute-done | bytes 262176 | tf_op jit(solution)/shard_map/ppermute | solution.py:584
  11.2 1.8 %collective-permute-start.3 = (f32[64,1024]{1,0:T(8,128)S(1)}, f32[64,1024]{1,0:T(8,128)S(1)}, u32[]{:S(2)}, u32[]{:S(2)}) collective-permute-start(f32[64,1024]{1,0:T(8,128)S(1)} %add.4.first_ref), channel_id=1, source_target_pairs={{0,24},{4,16},{8,28},{12,20},{16,4},{20,12},{24,0},{28,8},{1,25},{... | collective-permute-start | bytes 786440 | tf_op jit(solution)/shard_map/ppermute | solution.py:588
  13.0 0.3 %collective-permute-done.1.recv_ref = f32[6,584,128]{2,1,0:T(8,128)S(1)} collective-permute-done((f32[6,584,128]{2,1,0:T(8,128)S(1)}, f32[6,584,128]{2,1,0:T(8,128)S(1)}, u32[]{:S(2)}, u32[]{:S(2)}) %collective-permute-start.1) | collective-permute-done | bytes 1794080 | tf_op jit(solution)/shard_map/ppermute | solution.py:586
  13.3 2.0 %dense_after.1 = (f32[192,576]{1,0:T(8,128)}, f32[192,192]{1,0:T(8,128)}, f32[192,768]{1,0:T(8,128)}, f32[192,768]{1,0:T(8,128)}, f32[1728,128]{1,0:T(8,128)}, /*index=5*/f32[1920]{0:T(1024)}, f32[1,960]{1,0:T(1,128)}) custom-call(f32[6,584,128]{2,1,0:T(8,128)S(1)} %collective-permute-done.1.recv_ref, f32[6,584,128]{2,1,0:T(8,128)S(1)} %get-tuple-element.40.send_ref, ...), custom_call_target="tpu_custom_call" | custom-call | flops 8847360000 | bytes 5898240 | tf_op jit(solution)/shard_map/dense_after/pallas_call | solution.py:521
  15.3 1.7 %collective-permute-done.3.second_ref = f32[64,1024]{1,0:T(8,128)S(1)} collective-permute-done((f32[64,1024]{1,0:T(8,128)S(1)}, f32[64,1024]{1,0:T(8,128)S(1)}, u32[]{:S(2)}, u32[]{:S(2)}) %collective-permute-start.3) | collective-permute-done | bytes 262176 | tf_op jit(solution)/shard_map/ppermute | solution.py:588
  17.1 0.2 collective-permute-start.4
  17.3 1.2 %embed_half.2 = (f32[192,2048]{1,0:T(8,128)}, f32[64,2048]{1,0:T(8,128)}) custom-call(bf16[192,192]{1,0:T(8,128)(2,1)S(1)} %get-tuple-element.58.stack_ref, f32[64,1024]{1,0:T(8,128)S(1)} %add.5.coeff_ref, f32[64,2048]{1,0:T(8,128)S(1)} %get-tuple-element.60.moment_ref, f32[192,1024]{1,0:T(8,128)S(1)} %get-tuple-element.62.old_ref), custom_call_target="tpu_custom_call" | custom-call | flops 75497472 | bytes 1572864 | tf_op jit(solution)/shard_map/embed_half/pallas_call | solution.py:228
  18.5 0.2 %collective-permute-done.4.coeff_ref = f32[64,1024]{1,0:T(8,128)S(1)} collective-permute-done((f32[64,1024]{1,0:T(8,128)S(1)}, f32[64,1024]{1,0:T(8,128)S(1)}, u32[]{:S(2)}, u32[]{:S(2)}) %collective-permute-start.4) | collective-permute-done | bytes 262176 | tf_op jit(solution)/shard_map/ppermute | solution.py:593
  18.7 1.2 %embed_half.3 = (f32[192,2048]{1,0:T(8,128)}, f32[64,2048]{1,0:T(8,128)}) custom-call(bf16[192,192]{1,0:T(8,128)(2,1)S(1)} %get-tuple-element.58.stack_ref, f32[64,1024]{1,0:T(8,128)S(1)} %collective-permute-done.4.coeff_ref, f32[64,2048]{1,0:T(8,128)S(1)} %get-tuple-element.60.moment_ref, ...), custom_call_target="tpu_custom_call", output_to_operand_aliasing={{0}: (4, {}), {1}: (5, {})} | custom-call | flops 75497472 | bytes 1572864 | tf_op jit(solution)/shard_map/embed_half/pallas_call | solution.py:228
  (3 shorter events, 0.1 us)
Async XLA Ops:
  2.2 2.1 %collective-permute-start = (f32[64,1024]{1,0:T(8,128)S(1)}, f32[64,1024]{1,0:T(8,128)S(1)}, u32[]{:S(2)}, u32[]{:S(2)}) collective-permute-start(f32[64,1024]{1,0:T(8,128)S(1)} %get-tuple-element.39), channel_id=1, source_target_pairs={{0,16},{16,0},{1,17},{17,1},{2,18},{18,2},{3,19},{19,3},{4,20},{20... | collective-permute-start | bytes 786440 | tf_op jit(solution)/shard_map/ppermute | solution.py:568
  4.4 6.7 %collective-permute-start.2 = (f32[64,1024]{1,0:T(8,128)S(1)}, f32[64,1024]{1,0:T(8,128)S(1)}, u32[]{:S(2)}, u32[]{:S(2)}) collective-permute-start(f32[64,1024]{1,0:T(8,128)S(1)} %add.3.order_ref.first_ref), channel_id=1, source_target_pairs={{0,20},{4,28},{8,16},{12,24},{16,8},{20,0},{24,12},{28,4},{1,21},{... | collective-permute-start | bytes 786440 | tf_op jit(solution)/shard_map/ppermute | solution.py:584
  9.5 3.8 %collective-permute-start.1 = (f32[6,584,128]{2,1,0:T(8,128)S(1)}, f32[6,584,128]{2,1,0:T(8,128)S(1)}, u32[]{:S(2)}, u32[]{:S(2)}) collective-permute-start(f32[6,584,128]{2,1,0:T(8,128)S(1)} %get-tuple-element.40.send_ref), channel_id=1, source_target_pairs={{0,16},{16,0},{1,17},{17,1},{2,18},{18,2},{3,19},{19,3},{4,20},{20... | collective-permute-start | bytes 5382152 | tf_op jit(solution)/shard_map/ppermute | solution.py:586
  11.2 5.9 %collective-permute-start.3 = (f32[64,1024]{1,0:T(8,128)S(1)}, f32[64,1024]{1,0:T(8,128)S(1)}, u32[]{:S(2)}, u32[]{:S(2)}) collective-permute-start(f32[64,1024]{1,0:T(8,128)S(1)} %add.4.first_ref), channel_id=1, source_target_pairs={{0,24},{4,16},{8,28},{12,20},{16,4},{20,12},{24,0},{28,8},{1,25},{... | collective-permute-start | bytes 786440 | tf_op jit(solution)/shard_map/ppermute | solution.py:588
  17.1 1.6 %collective-permute-start.4 = (f32[64,1024]{1,0:T(8,128)S(1)}, f32[64,1024]{1,0:T(8,128)S(1)}, u32[]{:S(2)}, u32[]{:S(2)}) collective-permute-start(f32[64,1024]{1,0:T(8,128)S(1)} %add.5.coeff_ref), channel_id=1, source_target_pairs={{0,16},{16,0},{1,17},{17,1},{2,18},{18,2},{3,19},{19,3},{4,20},{20... | collective-permute-start | bytes 786440 | tf_op jit(solution)/shard_map/ppermute | solution.py:593

commit v4 on v3

--- a/solution.py
+++ b/solution.py
@@ -125,18 +125,21 @@
     return first[:rank] + first[rank:] + jnp.dot(high, diff_low, preferred_element_type=f32)
 
 
-def partial_kernel(other, basis_hbm, local_hbm, old_hbm, out_ref, old_ref, *refs):
-    basis_ref, local_ref, sems = refs[-3:]
+def first_kernel(
+    basis_hbm, local_hbm, old_hbm, out_ref, basis_ref, local_own, old_own, old_rest, local_rest, sems
+):
     columns = out_ref.shape[1]
     block = columns // CHUNKS
-    start = side_start(other, columns)
     copies = [pltpu.make_async_copy(basis_hbm, basis_ref, sems.at[0])]
     for k in range(CHUNKS):
-        there = pl.ds(pl.multiple_of(start + k * block, block), block)
+        there = pl.ds(pl.multiple_of(side_start(True, columns) + k * block, block), block)
         here = pl.ds(k * block, block)
-        for source, target in ((old_hbm, old_ref), (local_hbm, local_ref)):
+        for source, target in ((old_hbm, old_rest), (local_hbm, local_rest)):
             at = sems.at[len(copies)]
             copies.append(pltpu.make_async_copy(source.at[:, there], target.at[:, here], at))
+    there = pl.ds(pl.multiple_of(side_start(False, columns), columns), columns)
+    for source, target in ((old_hbm, old_own), (local_hbm, local_own)):
+        copies.append(pltpu.make_async_copy(source.at[:, there], target, sems.at[len(copies)]))
     for copy in copies:
         copy.start()
     copies[0].wait()
@@ -145,106 +148,133 @@
         copies[1 + 2 * k].wait()
         copies[2 + 2 * k].wait()
         here = slice(k * block, (k + 1) * block)
-        out_ref[:, here] = product(basis, local_ref[:, here], old_ref[:, here])
-    if not other:
-        high = basis.astype(bf16).astype(f32)
-        refs[0][...] = jnp.concatenate([high, basis - high, high], axis=0).T.astype(bf16)
-
-
-def partial_coeff(basis_t, local, old, other):
+        out_ref[:, here] = product(basis, local_rest[:, here], old_rest[:, here])
+    copies[-2].wait()
+    copies[-1].wait()
+
+
+def first_half(basis_t, local, old):
     rank, depth = basis_t.shape
     columns = old.shape[1] // 2
-    shapes = [((rank, columns), f32), ((depth, columns), f32)]
-    if not other:
-        shapes.append(((depth, 3 * rank), bf16))
+    shapes = [((rank, columns), f32), ((rank, depth), f32), ((depth, columns), bf16)]
+    shapes += [((depth, columns), f32)] * 2
     return pl.pallas_call(
-        functools.partial(partial_kernel, other),
+        first_kernel,
         in_specs=[ANY] * 3,
         out_specs=[WHOLE] * len(shapes),
         out_shape=[jax.ShapeDtypeStruct(*shape) for shape in shapes],
         scratch_shapes=[
-            pltpu.VMEM((rank, depth), f32),
             pltpu.VMEM((depth, columns), bf16),
-            pltpu.SemaphoreType.DMA((1 + 2 * CHUNKS,)),
+            pltpu.SemaphoreType.DMA((3 + 2 * CHUNKS,)),
         ],
-        compiler_params=pltpu.CompilerParams(vmem_limit_bytes=6 * 2**20),
+        compiler_params=pltpu.CompilerParams(vmem_limit_bytes=8 * 2**20),
+        cost_estimate=pl.CostEstimate(
+            flops=6 * rank * depth * columns, bytes_accessed=12 * depth * columns, transcendentals=0
+        ),
+        name="first_half",
+    )(*in_hbm((basis_t, local, old)))
+
+
+def second_kernel(basis_ref, local_ref, old_ref, out_ref, stack_ref):
+    basis = basis_ref[...]
+    out_ref[...] = product(basis, local_ref[...], old_ref[...])
+    high = basis.astype(bf16).astype(f32)
+    stack_ref[...] = jnp.concatenate([high, basis - high, high], axis=0).T.astype(bf16)
+
+
+def second_half(basis, local, old):
+    rank, depth = basis.shape
+    columns = old.shape[1]
+    return pl.pallas_call(
+        second_kernel,
+        in_specs=[WHOLE] * 3,
+        out_specs=[WHOLE] * 2,
+        out_shape=[
+            jax.ShapeDtypeStruct((rank, columns), f32),
+            jax.ShapeDtypeStruct((depth, 3 * rank), bf16),
+        ],
+        compiler_params=pltpu.CompilerParams(vmem_limit_bytes=4 * 2**20),
         cost_estimate=pl.CostEstimate(
             flops=6 * rank * depth * columns, bytes_accessed=6 * depth * columns, transcendentals=0
         ),
-        name="partial_coeff",
-    )(*in_hbm((basis_t, local, old)))
-
-
-def add_kernel(scale, first_ref, second_ref, out_ref):
-    out_ref[...] = scale * (first_ref[...] + second_ref[...])
-
-
-def add(first, second, scale=1.0):
+        name="second_half",
+    )(basis, local, old)
+
+
+def add_kernel(scale, first_ref, second_ref, *out_refs):
+    width = out_refs[0].shape[1]
+    for part, out_ref in enumerate(out_refs):
+        here = slice(part * width, (part + 1) * width)
+        out_ref[...] = scale * (first_ref[:, here] + second_ref[:, here])
+
+
+def add(first, second, parts=1, scale=1.0, flops=2 * 10**10):
+    rows, columns = first.shape
     return pl.pallas_call(
         functools.partial(add_kernel, scale),
         in_specs=[WHOLE] * 2,
-        out_specs=WHOLE,
-        out_shape=jax.ShapeDtypeStruct(first.shape, f32),
+        out_specs=[WHOLE] * parts,
+        out_shape=[jax.ShapeDtypeStruct((rows, columns // parts), f32)] * parts,
         compiler_params=pltpu.CompilerParams(vmem_limit_bytes=2 * 2**20),
-        cost_estimate=pl.CostEstimate(flops=10**11, bytes_accessed=0, transcendentals=0),
+        cost_estimate=pl.CostEstimate(flops=flops, bytes_accessed=0, transcendentals=0),
         name="add",
     )(first, second)
 
 
-def embed_kernel(other, stack_ref, coeff_ref, moment_ref, old_ref, *refs):
+def embed_kernel(pieces, stack_ref, moment_ref, *refs):
+    count = len(pieces)
+    coeffs, olds = refs[:count], refs[count : 2 * count]
     embed_hbm, moved_hbm, embed_ref, moved_ref, sems = refs[-5:]
-    columns = coeff_ref.shape[1]
-    block = columns // CHUNKS
-    start = side_start(other, columns)
+    width = coeffs[0].shape[1]
     copies = []
-    for k in range(CHUNKS):
-        here = slice(k * block, (k + 1) * block)
-        there = pl.ds(pl.multiple_of(start + k * block, block), block)
-        coeff = coeff_ref[:, here]
+    for k, (other, part) in enumerate(pieces):
+        start = side_start(other, olds[k].shape[1]) + part * width
+        there = pl.ds(pl.multiple_of(start, width), width)
+        coeff = coeffs[k][...]
         moved = momentum_coef * moment_ref[:, there] + coeff
-        moved_ref[:, here] = moved
+        moved_ref[k] = moved
         up_high, up_low = split(coeff + momentum_coef * moved)
-        product = jnp.dot(
+        change = jnp.dot(
             stack_ref[...],
             jnp.concatenate([up_high, up_high, up_low], axis=0),
             preferred_element_type=f32,
         )
-        embed_ref[:, here] = old_ref[:, here] - outer_rate * product
-        target = pl.ds(k * block, block)
-        for source_ref, target_hbm, at in ((moved_ref, moved_hbm, 0), (embed_ref, embed_hbm, 1)):
-            copy = pltpu.make_async_copy(
-                source_ref.at[:, target], target_hbm.at[:, there], sems.at[2 * k + at]
-            )
+        embed_ref[k] = olds[k][:, part * width : (part + 1) * width] - outer_rate * change
+        for source, target, at in ((moved_ref, moved_hbm, 0), (embed_ref, embed_hbm, 1)):
+            copy = pltpu.make_async_copy(source.at[k], target.at[:, there], sems.at[2 * k + at])
             copy.start()
             copies.append(copy)
     for copy in copies:
         copy.wait()
 
 
-def embed_half(stack, coeff, moment, old, before):
-    rank, columns = coeff.shape
-    depth = old.shape[0]
-    more = () if before is None else tuple(before)
+def embed_pieces(pieces, stack, moment, coeffs, olds, before):
+    count = len(pieces)
+    rank, width = coeffs[0].shape
+    depth, columns = olds[0].shape
+    first = 2 + 2 * count
     return pl.pallas_call(
-        functools.partial(embed_kernel, before is not None),
-        in_specs=[WHOLE] * 4 + [ANY] * len(more),
+        functools.partial(embed_kernel, pieces),
+        in_specs=[WHOLE] * first + [ANY] * len(before),
         out_specs=[ANY, ANY],
         out_shape=[
             jax.ShapeDtypeStruct((depth, 2 * columns), f32),
             jax.ShapeDtypeStruct((rank, 2 * columns), f32),
         ],
         scratch_shapes=[
-            pltpu.VMEM((depth, columns), f32),
-            pltpu.VMEM((rank, columns), f32),
-            pltpu.SemaphoreType.DMA((2 * CHUNKS,)),
+            pltpu.VMEM((count, depth, width), f32),
+            pltpu.VMEM((count, rank, width), f32),
+            pltpu.SemaphoreType.DMA((2 * count,)),
         ],
-        input_output_aliases={} if before is None else {4: 0, 5: 1},
+        input_output_aliases={first: 0, first + 1: 1} if before else {},
         compiler_params=pltpu.CompilerParams(vmem_limit_bytes=8 * 2**20),
         cost_estimate=pl.CostEstimate(
-            flops=6 * rank * depth * columns, bytes_accessed=8 * depth * columns, transcendentals=0
+            flops=6 * count * rank * depth * width,
+            bytes_accessed=8 * count * depth * width,
+            transcendentals=0,
         ),
-        name="embed_half",
-    )(stack, coeff, moment, old, *more)
+        name="embed_pieces",
+    )(stack, moment, *coeffs, *olds, *before)
 
 
 def low_lanes(rows):
@@ -300,23 +330,13 @@
     return pieces
 
 
-def before_kernel(order_ref, *refs):
+def before_kernel(
+    order_ref, moment_hbm, in_ref, out_ref, up_ref, down_ref, old_ref, mom_ref, small_ref,
+    small_old_ref, small_mom_ref, send_ref, moment_ref, wide_ref, sem,
+):
     del order_ref
-    count = len(refs) // 2 - 1
-    sources, send_ref, kept, (wide_ref, sems) = (
-        refs[:count], refs[count], refs[count + 1 : -2], refs[-2:]
-    )
-    copies = [
-        pltpu.make_async_copy(source, target, sems.at[k])
-        for k, (source, target) in enumerate(zip(sources, kept))
-    ]
-    for copy in copies:
-        copy.start()
-    for copy in copies:
-        copy.wait()
-    in_ref, out_ref, up_ref, down_ref, old_ref, mom_ref, small_ref, small_old_ref, small_mom_ref = (
-        kept[:9]
-    )
+    copy = pltpu.make_async_copy(moment_hbm, moment_ref, sem)
+    copy.start()
     group = lax.axis_index("group")
     rows = up_ref.shape[1]
     mid = rows // 2
@@ -392,6 +412,8 @@
         values = small_ref[...].astype(f32)
         put_small(values[:, :small], values[:, small:])
 
+    copy.wait()
+
 
 def after_kernel(
     recv_ref, send_ref, in_ref, out_ref, up_ref, down_ref, old_ref, mom_ref, small_ref,
@@ -496,22 +518,23 @@
         put_small(values[:, :small], values[:, small:], False)
 
 
-def dense_before(order, operands):
+def dense_before(order, moment, operands):
     _, rows, width = operands[2].shape
-    count = len(operands)
     return pl.pallas_call(
         before_kernel,
-        in_specs=[ANY] * (1 + count),
-        out_specs=[WHOLE] * (1 + count),
-        out_shape=[jax.ShapeDtypeStruct((width // LANES, 3 * rows + 8, LANES), f32)]
-        + [jax.ShapeDtypeStruct(array.shape, array.dtype) for array in operands],
-        scratch_shapes=[pltpu.VMEM((2, width, LANES), f32), pltpu.SemaphoreType.DMA((count,))],
-        compiler_params=pltpu.CompilerParams(vmem_limit_bytes=20 * 2**20),
+        in_specs=[ANY] * 2 + [WHOLE] * 9,
+        out_specs=[WHOLE] * 2,
+        out_shape=[
+            jax.ShapeDtypeStruct((width // LANES, 3 * rows + 8, LANES), f32),
+            jax.ShapeDtypeStruct(moment.shape, f32),
+        ],
+        scratch_shapes=[pltpu.VMEM((2, width, LANES), f32), pltpu.SemaphoreType.DMA],
+        compiler_params=pltpu.CompilerParams(vmem_limit_bytes=4 * 2**20),
         cost_estimate=pl.CostEstimate(
             flops=60000 * rows * width, bytes_accessed=30 * rows * width, transcendentals=0
         ),
         name="dense_before",
-    )(order, *in_hbm(operands))
+    )(order, *in_hbm([moment]), *operands)
 
 
 def dense_after(received, sent, operands):
@@ -527,7 +550,7 @@
             pltpu.VMEM((width // LANES, rows, LANES), f32),
             pltpu.VMEM((2, width, LANES), f32),
         ],
-        compiler_params=pltpu.CompilerParams(vmem_limit_bytes=24 * 2**20),
+        compiler_params=pltpu.CompilerParams(vmem_limit_bytes=8 * 2**20),
         cost_estimate=pl.CostEstimate(
             flops=60000 * rows * width, bytes_accessed=40 * rows * width, transcendentals=0
         ),
@@ -563,10 +586,11 @@
     )
     axes = ("group", "shard")
 
-    embed = (basis.T, embed_local[0], embed_old)
-    theirs, old_rest = partial_coeff(*embed, True)
+    theirs, basis_t, local_own, old_own, old_rest = first_half(
+        basis.T, embed_local[0], embed_old
+    )
     theirs = lax.ppermute(theirs, "group", swap)
-    mine, old_own, stack = partial_coeff(*embed, False)
+    mine, stack = second_half(basis_t, local_own, old_own)
 
     operands = (
         attn_in_local,
@@ -578,21 +602,27 @@
         small_local,
         small_old[None, :],
         small_momentum[None, :],
-        coeff_momentum,
-    )
-    total = add(mine, theirs)
-    moving = lax.ppermute(total, axes, first)
-    sent, *kept, moment = dense_before(total, operands)
+    )
+    totals = add(mine, theirs, 2)
+    moving = [lax.ppermute(total, axes, first) for total in totals]
+    sent, moment = dense_before(totals[0], coeff_momentum, operands)
     received = lax.ppermute(sent, "group", swap)
-    total = add(total, moving)
-    moving = lax.ppermute(total, axes, second)
-    dense = list(dense_after(received, sent, kept))
-    moving, dense[-1] = lax.optimization_barrier((moving, dense[-1]))
-
-    own = add(total, moving, 0.5)
-    rest = lax.ppermute(own, "group", swap)
-    done = embed_half(stack, own, moment, old_own, None)
-    embed_next, coeff_moved = embed_half(stack, rest, moment, old_rest, done)
+    totals = [
+        add(*pair, flops=flops)[0] for *pair, flops in zip(totals, moving, (10**4, 2 * 10**10))
+    ]
+    moving = [lax.ppermute(total, axes, second) for total in totals]
+    dense = list(dense_after(received, sent, operands))
+    moving[0], dense[-1] = lax.optimization_barrier((moving[0], dense[-1]))
+    own = [add(*pair, scale=0.5)[0] for pair in zip(totals, moving)]
+    rest = [lax.ppermute(part, "group", swap) for part in own]
+    done = ()
+    for pieces, coeffs in (
+        (((False, 0), (False, 1), (True, 0)), (*own, rest[0])),
+        (((True, 1),), rest[1:]),
+    ):
+        olds = [old_rest if other else old_own for other, _ in pieces]
+        done = embed_pieces(pieces, stack, moment, coeffs, olds, done)
+    embed_next, coeff_moved = done
 
     attn_in_next, attn_out_next, ffn_in_next, ffn_out_next, moved, small_next, small_moved = dense
     return (

time: 20.1 us -> 19.1 us (0.950)
  Pallas kernels: 10.1 us -> 7.6 us
  starting transfers between devices: 5.43 us -> 7.81 us
  waiting for transfers between devices: 3.63 us -> 2.62 us
    pallas_call x5, Pallas kernels: 7.97 us -> 5.48 us  [the longest x2 2.39 us: embed_pieces(): pl.pallas_call(functools.partial(embed_kernel, pieces), in_specs=[WHOLE]...]
    ppermute x3 -> x6, starting transfers between devices: 4.68 us -> 6.82 us  [the longest x2 3.29 us: paired(): moving = [lax.ppermute(total, axes, second) for total in totals]]
    ppermute x3 -> x6, waiting for transfers between devices: 3.32 us -> 1.76 us  [the longest x2 0.97 us: paired(): moving = [lax.ppermute(total, axes, first) for total in totals]]
    ppermute x1, waiting for transfers between devices: 0.01 us -> 0.85 us  [paired(): theirs = lax.ppermute(theirs, 'group', swap)]
    ppermute x1, waiting for transfers between devices: 0.31 us -> 0.01 us  [paired(): received = lax.ppermute(sent, 'group', swap)]
    ppermute x1, starting transfers between devices: 0.23 us -> 0.47 us  [paired(): received = lax.ppermute(sent, 'group', swap)]
  transfers between devices with their start and end apart: 5 -> 8, of which waited for: 4 -> 4; matrix products, arithmetic and copies ran while one was open for 0% -> 0% of each run, Pallas kernels for 37% -> 26%
where the time goes in v4:
time: 19.1 us; the launch traced here: 18.9 us
  starting transfers between devices  7.81 us (41%)
  Pallas kernels  7.6 us (40%)
  waiting for transfers between devices  2.62 us (14%)
  between operations  0.79 us (4%)
    ppermute x2, starting transfers between devices, paired(): moving = [lax.ppermute(total, axes, second) for total in totals]  3.29 us
    ppermute x2, starting transfers between devices, paired(): moving = [lax.ppermute(total, axes, first) for total in totals]  2.74 us
    pallas_call x2, Pallas kernels, embed_pieces(): pl.pallas_call(functools.partial(embed_kernel, pieces), in_specs=[WHOLE]...  2.39 us
    pallas_call x1, Pallas kernels, dense_after(): pl.pallas_call(after_kernel, in_specs=[WHOLE] * 11, out_specs=[WHOLE] * 7...  2.03 us
    pallas_call x1, Pallas kernels, first_half(): pl.pallas_call(first_kernel, in_specs=[ANY] * 3, out_specs=[WHOLE] * len(...  1.73 us
    pallas_call x1, Pallas kernels, dense_before(): pl.pallas_call(before_kernel, in_specs=[ANY] * 2 + [WHOLE] * 9, out_specs...  1.06 us
    ppermute x2, waiting for transfers between devices, paired(): moving = [lax.ppermute(total, axes, first) for total in totals]  0.97 us
    ppermute x1, waiting for transfers between devices, paired(): theirs = lax.ppermute(theirs, 'group', swap)  0.85 us
  transfers between devices with their start and end apart: 8, of which 4 were waited for; matrix products, arithmetic and copies ran while one was open for 0% of the time, Pallas kernels for 26%

profile of v4, /device:TPU:0, one launch (start us, length us, event | category | flops | bytes accessed | tf_op | source)
XLA Modules:
  0.0 18.9 jit_solution(5257666188612793374)
XLA Ops:
  0.6 1.7 %first_half.1 = (f32[64,1024]{1,0:T(8,128)S(1)}, f32[64,192]{1,0:T(8,128)S(1)}, bf16[192,1024]{1,0:T(8,128)(2,1)S(1)}, f32[192,1024]{1,0:T(8,128)S(1)}, f32[192,1024]{1,0:T(8,128)S(1)}) custom-call(f32[64,192]{1,0:T(8,128)} %bitcast.21, bf16[192,2048]{1,0:T(8,128)(2,1)} %bitcast.20, f32[192,2048]{1,0:T(8,128)} %old_hbm.1), custom_call_target="tpu_custom_call" | custom-call | flops 75497472 | bytes 2359296 | tf_op jit(solution)/shard_map/first_half/pallas_call | solution.py:161
  2.4 0.5 %collective-permute-start = (f32[64,1024]{1,0:T(8,128)S(1)}, f32[64,1024]{1,0:T(8,128)S(1)}, u32[]{:S(2)}, u32[]{:S(2)}) collective-permute-start(f32[64,1024]{1,0:T(8,128)S(1)} %get-tuple-element.37), channel_id=1, source_target_pairs={{0,16},{16,0},{1,17},{17,1},{2,18},{18,2},{3,19},{19,3},{4,20},{20... | collective-permute-start | bytes 786440 | tf_op jit(solution)/shard_map/ppermute | solution.py:592
  2.9 0.3 %second_half.1 = (f32[64,1024]{1,0:T(8,128)S(1)}, bf16[192,192]{1,0:T(8,128)(2,1)S(1)}) custom-call(f32[64,192]{1,0:T(8,128)S(1)} %get-tuple-element.33.basis_ref, bf16[192,1024]{1,0:T(8,128)(2,1)S(1)} %get-tuple-element.34.local_ref, f32[192,1024]{1,0:T(8,128)S(1)} %get-tuple-element.35.old_ref.refs_3_.refs_4_), custom_call_target="tpu_custom_call" | custom-call | flops 75497472 | bytes 1179648 | tf_op jit(solution)/shard_map/second_half/pallas_call | solution.py:188
  3.2 0.9 %collective-permute-done.second_ref = f32[64,1024]{1,0:T(8,128)S(1)} collective-permute-done((f32[64,1024]{1,0:T(8,128)S(1)}, f32[64,1024]{1,0:T(8,128)S(1)}, u32[]{:S(2)}, u32[]{:S(2)}) %collective-permute-start) | collective-permute-done | bytes 262176 | tf_op jit(solution)/shard_map/ppermute | solution.py:592
  4.1 0.0 copy-start.5
  4.1 0.0 copy-start.6
  4.1 0.0 copy-start.7
  4.1 0.0 copy-start.8
  4.2 2.7 %collective-permute-start.2 = (f32[64,512]{1,0:T(8,128)S(1)}, f32[64,512]{1,0:T(8,128)S(1)}, u32[]{:S(2)}, u32[]{:S(2)}) collective-permute-start(f32[64,512]{1,0:T(8,128)S(1)} %get-tuple-element.38.order_ref.first_ref), channel_id=1, source_target_pairs={{0,20},{4,28},{8,16},{12,24},{16,8},{20,0},{24,12},{28,4},{1,21},{... | collective-permute-start | bytes 393224 | tf_op jit(solution)/shard_map/ppermute | solution.py:607
  6.8 0.1 collective-permute-start.4
  6.9 0.0 copy-done
  6.9 0.0 copy-done.4
  6.9 0.0 copy-done.5
  6.9 0.0 copy-done.6
  7.0 0.0 copy-done.7
  7.0 0.0 copy-done.8
  7.0 1.1 %dense_before.1 = (f32[6,584,128]{2,1,0:T(8,128)S(1)}, f32[64,2048]{1,0:T(8,128)S(1)}) custom-call(f32[64,512]{1,0:T(8,128)S(1)} %get-tuple-element.38.order_ref.first_ref, f32[64,2048]{1,0:T(8,128)} %moment_hbm.1, bf16[1,192,576]{2,1,0:T(8,128)(2,1)S(1)} %copy-done.4, bf16[1,192,192]{2,1,0:T(8,128)(2,1)S(1)} %copy-done.5, ...), custom_call_target="tpu_custom_call" | custom-call | flops 8847360000 | bytes 4423680 | tf_op jit(solution)/shard_map/dense_before/pallas_call | solution.py:523
  8.0 0.5 %collective-permute-start.1 = (f32[6,584,128]{2,1,0:T(8,128)S(1)}, f32[6,584,128]{2,1,0:T(8,128)S(1)}, u32[]{:S(2)}, u32[]{:S(2)}) collective-permute-start(f32[6,584,128]{2,1,0:T(8,128)S(1)} %get-tuple-element.39.send_ref), channel_id=1, source_target_pairs={{0,16},{16,0},{1,17},{17,1},{2,18},{18,2},{3,19},{19,3},{4,20},{20... | collective-permute-start | bytes 5382152 | tf_op jit(solution)/shard_map/ppermute | solution.py:609
  8.5 1.0 %collective-permute-done.2.second_ref = f32[64,512]{1,0:T(8,128)S(1)} collective-permute-done((f32[64,512]{1,0:T(8,128)S(1)}, f32[64,512]{1,0:T(8,128)S(1)}, u32[]{:S(2)}, u32[]{:S(2)}) %collective-permute-start.2) | collective-permute-done | bytes 131104 | tf_op jit(solution)/shard_map/ppermute | solution.py:607
  9.5 2.1 %collective-permute-start.3 = (f32[64,512]{1,0:T(8,128)S(1)}, f32[64,512]{1,0:T(8,128)S(1)}, u32[]{:S(2)}, u32[]{:S(2)}) collective-permute-start(f32[64,512]{1,0:T(8,128)S(1)} %add.6.first_ref), channel_id=1, source_target_pairs={{0,24},{4,16},{8,28},{12,20},{16,4},{20,12},{24,0},{28,8},{1,25},{... | collective-permute-start | bytes 393224 | tf_op jit(solution)/shard_map/ppermute | solution.py:613
  11.6 0.0 collective-permute-done.4.second_ref
  11.7 1.2 %collective-permute-start.5 = (f32[64,512]{1,0:T(8,128)S(1)}, f32[64,512]{1,0:T(8,128)S(1)}, u32[]{:S(2)}, u32[]{:S(2)}) collective-permute-start(f32[64,512]{1,0:T(8,128)S(1)} %add.7.first_ref), channel_id=1, source_target_pairs={{0,24},{4,16},{8,28},{12,20},{16,4},{20,12},{24,0},{28,8},{1,25},{... | collective-permute-start | bytes 393224 | tf_op jit(solution)/shard_map/ppermute | solution.py:613
  12.8 0.0 collective-permute-done.1.recv_ref
  12.8 2.0 %dense_after.1 = (f32[192,576]{1,0:T(8,128)}, f32[192,192]{1,0:T(8,128)}, f32[192,768]{1,0:T(8,128)}, f32[192,768]{1,0:T(8,128)}, f32[1728,128]{1,0:T(8,128)}, /*index=5*/f32[1920]{0:T(1024)}, f32[1,960]{1,0:T(1,128)}) custom-call(f32[6,584,128]{2,1,0:T(8,128)S(1)} %collective-permute-done.1.recv_ref, f32[6,584,128]{2,1,0:T(8,128)S(1)} %get-tuple-element.39.send_ref, ...), custom_call_target="tpu_custom_call" | custom-call | flops 8847360000 | bytes 5898240 | tf_op jit(solution)/shard_map/dense_after/pallas_call | solution.py:544
  14.8 0.0 collective-permute-done.3.second_ref
  14.9 0.6 %collective-permute-start.7 = (f32[64,512]{1,0:T(8,128)S(1)}, f32[64,512]{1,0:T(8,128)S(1)}, u32[]{:S(2)}, u32[]{:S(2)}) collective-permute-start(f32[64,512]{1,0:T(8,128)S(1)} %add.9.refs_0_), channel_id=1, source_target_pairs={{0,16},{16,0},{1,17},{17,1},{2,18},{18,2},{3,19},{19,3},{4,20},{20... | collective-permute-start | bytes 393224 | tf_op jit(solution)/shard_map/ppermute | solution.py:617
  15.5 0.6 %collective-permute-done.5.second_ref = f32[64,512]{1,0:T(8,128)S(1)} collective-permute-done((f32[64,512]{1,0:T(8,128)S(1)}, f32[64,512]{1,0:T(8,128)S(1)}, u32[]{:S(2)}, u32[]{:S(2)}) %collective-permute-start.5) | collective-permute-done | bytes 131104 | tf_op jit(solution)/shard_map/ppermute | solution.py:613
  16.1 0.2 collective-permute-start.6
  16.3 0.1 collective-permute-done.7.refs_2_
  16.5 1.4 %embed_pieces.2 = (f32[192,2048]{1,0:T(8,128)}, f32[64,2048]{1,0:T(8,128)}) custom-call(bf16[192,192]{1,0:T(8,128)(2,1)S(1)} %get-tuple-element.48.stack_ref, f32[64,2048]{1,0:T(8,128)S(1)} %get-tuple-element.49.moment_ref, f32[64,512]{1,0:T(8,128)S(1)} %add.9.refs_0_, f32[64,512]{1,0:T(8,128)S(1)} %add.8.refs_1_, ...), custom_call_target="tpu_custom_call" | custom-call | flops 113246208 | bytes 2359296 | tf_op jit(solution)/shard_map/embed_pieces/pallas_call | solution.py:256
  17.8 0.0 collective-permute-done.6.refs_0_
  17.9 1.0 %embed_pieces.3 = (f32[192,2048]{1,0:T(8,128)}, f32[64,2048]{1,0:T(8,128)}) custom-call(bf16[192,192]{1,0:T(8,128)(2,1)S(1)} %get-tuple-element.48.stack_ref, f32[64,2048]{1,0:T(8,128)S(1)} %get-tuple-element.49.moment_ref, f32[64,512]{1,0:T(8,128)S(1)} %collective-permute-done.6.refs_0_, ...), custom_call_target="tpu_custom_call", output_to_operand_aliasing={{0}: (4, {}), {1}: (5, {})} | custom-call | flops 37748736 | bytes 786432 | tf_op jit(solution)/shard_map/embed_pieces/pallas_call | solution.py:256
  (13 shorter events, 0.1 us)
Async XLA Ops:
  2.4 1.7 %collective-permute-start = (f32[64,1024]{1,0:T(8,128)S(1)}, f32[64,1024]{1,0:T(8,128)S(1)}, u32[]{:S(2)}, u32[]{:S(2)}) collective-permute-start(f32[64,1024]{1,0:T(8,128)S(1)} %get-tuple-element.37), channel_id=1, source_target_pairs={{0,16},{16,0},{1,17},{17,1},{2,18},{18,2},{3,19},{19,3},{4,20},{20... | collective-permute-start | bytes 786440 | tf_op jit(solution)/shard_map/ppermute | solution.py:592
  4.1 2.8 %copy-start = (f32[1,221184]{1,0:T(1,128)S(1)}, f32[1,221184]{1,0:T(1,128)}, u32[]{:S(2)}) copy-start(f32[1,221184]{1,0:T(1,128)} %param.18) | copy-start | bytes 2654212
  4.1 2.9 %copy-start.1 = (f32[1,221184]{1,0:T(1,128)S(1)}, f32[1,221184]{1,0:T(1,128)}, u32[]{:S(2)}) copy-start(f32[1,221184]{1,0:T(1,128)} %param.19) | copy-start | bytes 2654212
  4.1 2.9 %copy-start.2 = (bf16[1,192,768]{2,1,0:T(8,128)(2,1)S(1)}, bf16[1,192,768]{2,1,0:T(8,128)(2,1)}, u32[]{:S(2)}) copy-start(bf16[1,192,768]{2,1,0:T(8,128)(2,1)} %up_ref.3) | copy-start | bytes 884740
  4.1 2.9 %copy-start.3 = (bf16[1,768,192]{1,2,0:T(8,128)(2,1)S(1)}, bf16[1,768,192]{1,2,0:T(8,128)(2,1)}, u32[]{:S(2)}) copy-start(bf16[1,768,192]{1,2,0:T(8,128)(2,1)} %param.16) | copy-start | bytes 884740
  4.1 2.9 %copy-start.4 = (bf16[1,192,576]{2,1,0:T(8,128)(2,1)S(1)}, bf16[1,192,576]{2,1,0:T(8,128)(2,1)}, u32[]{:S(2)}) copy-start(bf16[1,192,576]{2,1,0:T(8,128)(2,1)} %in_ref.3) | copy-start | bytes 663556
  4.1 2.9 %copy-start.5 = (bf16[1,192,192]{2,1,0:T(8,128)(2,1)S(1)}, bf16[1,192,192]{2,1,0:T(8,128)(2,1)}, u32[]{:S(2)}) copy-start(bf16[1,192,192]{2,1,0:T(8,128)(2,1)} %out_ref.3) | copy-start | bytes 221188
  4.1 2.9 %copy-start.6 = (bf16[1,1920]{1,0:T(2,128)(2,1)S(1)}, bf16[1,1920]{1,0:T(2,128)(2,1)}, u32[]{:S(2)}) copy-start(bf16[1,1920]{1,0:T(2,128)(2,1)} %small_ref.3) | copy-start | bytes 11524
  4.1 2.9 %copy-start.7 = (f32[960]{0:T(1024)S(1)}, f32[960]{0:T(1024)}, u32[]{:S(2)}) copy-start(f32[960]{0:T(1024)} %param.20) | copy-start | bytes 11524
  4.1 2.9 %copy-start.8 = (f32[960]{0:T(1024)S(1)}, f32[960]{0:T(1024)}, u32[]{:S(2)}) copy-start(f32[960]{0:T(1024)} %param.21) | copy-start | bytes 11524
  4.2 5.3 %collective-permute-start.2 = (f32[64,512]{1,0:T(8,128)S(1)}, f32[64,512]{1,0:T(8,128)S(1)}, u32[]{:S(2)}, u32[]{:S(2)}) collective-permute-start(f32[64,512]{1,0:T(8,128)S(1)} %get-tuple-element.38.order_ref.first_ref), channel_id=1, source_target_pairs={{0,20},{4,28},{8,16},{12,24},{16,8},{20,0},{24,12},{28,4},{1,21},{... | collective-permute-start | bytes 393224 | tf_op jit(solution)/shard_map/ppermute | solution.py:607
  6.8 4.8 %collective-permute-start.4 = (f32[64,512]{1,0:T(8,128)S(1)}, f32[64,512]{1,0:T(8,128)S(1)}, u32[]{:S(2)}, u32[]{:S(2)}) collective-permute-start(f32[64,512]{1,0:T(8,128)S(1)} %get-tuple-element.50.first_ref), channel_id=1, source_target_pairs={{0,20},{4,28},{8,16},{12,24},{16,8},{20,0},{24,12},{28,4},{1,21},{... | collective-permute-start | bytes 393224 | tf_op jit(solution)/shard_map/ppermute | solution.py:607
  8.0 4.8 %collective-permute-start.1 = (f32[6,584,128]{2,1,0:T(8,128)S(1)}, f32[6,584,128]{2,1,0:T(8,128)S(1)}, u32[]{:S(2)}, u32[]{:S(2)}) collective-permute-start(f32[6,584,128]{2,1,0:T(8,128)S(1)} %get-tuple-element.39.send_ref), channel_id=1, source_target_pairs={{0,16},{16,0},{1,17},{17,1},{2,18},{18,2},{3,19},{19,3},{4,20},{20... | collective-permute-start | bytes 5382152 | tf_op jit(solution)/shard_map/ppermute | solution.py:609
  9.5 5.3 %collective-permute-start.3 = (f32[64,512]{1,0:T(8,128)S(1)}, f32[64,512]{1,0:T(8,128)S(1)}, u32[]{:S(2)}, u32[]{:S(2)}) collective-permute-start(f32[64,512]{1,0:T(8,128)S(1)} %add.6.first_ref), channel_id=1, source_target_pairs={{0,24},{4,16},{8,28},{12,20},{16,4},{20,12},{24,0},{28,8},{1,25},{... | collective-permute-start | bytes 393224 | tf_op jit(solution)/shard_map/ppermute | solution.py:613
  11.7 4.5 %collective-permute-start.5 = (f32[64,512]{1,0:T(8,128)S(1)}, f32[64,512]{1,0:T(8,128)S(1)}, u32[]{:S(2)}, u32[]{:S(2)}) collective-permute-start(f32[64,512]{1,0:T(8,128)S(1)} %add.7.first_ref), channel_id=1, source_target_pairs={{0,24},{4,16},{8,28},{12,20},{16,4},{20,12},{24,0},{28,8},{1,25},{... | collective-permute-start | bytes 393224 | tf_op jit(solution)/shard_map/ppermute | solution.py:613
  14.9 1.6 %collective-permute-start.7 = (f32[64,512]{1,0:T(8,128)S(1)}, f32[64,512]{1,0:T(8,128)S(1)}, u32[]{:S(2)}, u32[]{:S(2)}) collective-permute-start(f32[64,512]{1,0:T(8,128)S(1)} %add.9.refs_0_), channel_id=1, source_target_pairs={{0,16},{16,0},{1,17},{17,1},{2,18},{18,2},{3,19},{19,3},{4,20},{20... | collective-permute-start | bytes 393224 | tf_op jit(solution)/shard_map/ppermute | solution.py:617
  16.1 1.7 %collective-permute-start.6 = (f32[64,512]{1,0:T(8,128)S(1)}, f32[64,512]{1,0:T(8,128)S(1)}, u32[]{:S(2)}, u32[]{:S(2)}) collective-permute-start(f32[64,512]{1,0:T(8,128)S(1)} %add.8.refs_1_), channel_id=1, source_target_pairs={{0,16},{16,0},{1,17},{17,1},{2,18},{18,2},{3,19},{19,3},{4,20},{20... | collective-permute-start | bytes 393224 | tf_op jit(solution)/shard_map/ppermute | solution.py:617

commit v5 on v4

--- a/solution.py
+++ b/solution.py
@@ -125,10 +125,10 @@
     return first[:rank] + first[rank:] + jnp.dot(high, diff_low, preferred_element_type=f32)
 
 
-def first_kernel(
-    basis_hbm, local_hbm, old_hbm, out_ref, basis_ref, local_own, old_own, old_rest, local_rest, sems
-):
-    columns = out_ref.shape[1]
+def first_kernel(basis_hbm, local_hbm, old_hbm, *refs):
+    out_refs = refs[:CHUNKS]
+    basis_ref, local_own, old_own, old_rest, local_rest, sems = refs[CHUNKS:]
+    columns = old_own.shape[1]
     block = columns // CHUNKS
     copies = [pltpu.make_async_copy(basis_hbm, basis_ref, sems.at[0])]
     for k in range(CHUNKS):
@@ -148,7 +148,7 @@
         copies[1 + 2 * k].wait()
         copies[2 + 2 * k].wait()
         here = slice(k * block, (k + 1) * block)
-        out_ref[:, here] = product(basis, local_rest[:, here], old_rest[:, here])
+        out_refs[k][...] = product(basis, local_rest[:, here], old_rest[:, here])
     copies[-2].wait()
     copies[-1].wait()
 
@@ -156,7 +156,8 @@
 def first_half(basis_t, local, old):
     rank, depth = basis_t.shape
     columns = old.shape[1] // 2
-    shapes = [((rank, columns), f32), ((rank, depth), f32), ((depth, columns), bf16)]
+    shapes = [((rank, columns // CHUNKS), f32)] * CHUNKS
+    shapes += [((rank, depth), f32), ((depth, columns), bf16)]
     shapes += [((depth, columns), f32)] * 2
     return pl.pallas_call(
         first_kernel,
@@ -175,9 +176,13 @@
     )(*in_hbm((basis_t, local, old)))
 
 
-def second_kernel(basis_ref, local_ref, old_ref, out_ref, stack_ref):
+def second_kernel(basis_ref, local_ref, old_ref, *refs):
+    *out_refs, stack_ref = refs
     basis = basis_ref[...]
-    out_ref[...] = product(basis, local_ref[...], old_ref[...])
+    block = old_ref.shape[1] // CHUNKS
+    for k, out_ref in enumerate(out_refs):
+        here = slice(k * block, (k + 1) * block)
+        out_ref[...] = product(basis, local_ref[:, here], old_ref[:, here])
     high = basis.astype(bf16).astype(f32)
     stack_ref[...] = jnp.concatenate([high, basis - high, high], axis=0).T.astype(bf16)
 
@@ -188,14 +193,12 @@
     return pl.pallas_call(
         second_kernel,
         in_specs=[WHOLE] * 3,
-        out_specs=[WHOLE] * 2,
-        out_shape=[
-            jax.ShapeDtypeStruct((rank, columns), f32),
-            jax.ShapeDtypeStruct((depth, 3 * rank), bf16),
-        ],
+        out_specs=[WHOLE] * (CHUNKS + 1),
+        out_shape=[jax.ShapeDtypeStruct((rank, columns // CHUNKS), f32)] * CHUNKS
+        + [jax.ShapeDtypeStruct((depth, 3 * rank), bf16)],
         compiler_params=pltpu.CompilerParams(vmem_limit_bytes=4 * 2**20),
         cost_estimate=pl.CostEstimate(
-            flops=6 * rank * depth * columns, bytes_accessed=6 * depth * columns, transcendentals=0
+            flops=10**10, bytes_accessed=6 * depth * columns, transcendentals=0
         ),
         name="second_half",
     )(basis, local, old)
@@ -586,11 +589,11 @@
     )
     axes = ("group", "shard")
 
-    theirs, basis_t, local_own, old_own, old_rest = first_half(
+    *theirs, basis_t, local_own, old_own, old_rest = first_half(
         basis.T, embed_local[0], embed_old
     )
-    theirs = lax.ppermute(theirs, "group", swap)
-    mine, stack = second_half(basis_t, local_own, old_own)
+    theirs = [lax.ppermute(part, "group", swap) for part in theirs]
+    *mine, stack = second_half(basis_t, local_own, old_own)
 
     operands = (
         attn_in_local,
@@ -603,7 +606,7 @@
         small_old[None, :],
         small_momentum[None, :],
     )
-    totals = add(mine, theirs, 2)
+    totals = [add(*pair, flops=10**4)[0] for pair in zip(mine, theirs)]
     moving = [lax.ppermute(total, axes, first) for total in totals]
     sent, moment = dense_before(totals[0], coeff_momentum, operands)
     received = lax.ppermute(sent, "group", swap)

time: 19.1 us -> 18.8 us (0.984)
  waiting for transfers between devices: 2.62 us -> 2.21 us
    ppermute x1 -> x2, waiting for transfers between devices: 0.85 us -> 0.53 us  [paired(): theirs = [lax.ppermute(part, 'group', swap) for part in theirs]]
    ppermute x2, starting transfers between devices: 2.74 us -> 3.01 us  [paired(): moving = [lax.ppermute(total, axes, first) for total in totals]]
    ppermute x1, starting transfers between devices: 0.47 us -> 0.28 us  [paired(): received = lax.ppermute(sent, 'group', swap)]
    ppermute x1 -> x2, starting transfers between devices: 0.52 us -> 0.6 us  [paired(): theirs = [lax.ppermute(part, 'group', swap) for part in theirs]]
  transfers between devices with their start and end apart: 8 -> 9, of which waited for: 4 -> 4; matrix products, arithmetic and copies ran while one was open for 0% -> 0% of each run, Pallas kernels for 26% -> 26%
where the time goes in v5:
time: 18.8 us; the launch traced here: 18.6 us
  starting transfers between devices  7.94 us (42%)
  Pallas kernels  7.6 us (40%)
  waiting for transfers between devices  2.21 us (12%)
  between operations  0.8 us (4%)
    ppermute x2, starting transfers between devices, paired(): moving = [lax.ppermute(total, axes, second) for total in totals]  3.36 us
    ppermute x2, starting transfers between devices, paired(): moving = [lax.ppermute(total, axes, first) for total in totals]  3.01 us
    pallas_call x2, Pallas kernels, embed_pieces(): pl.pallas_call(functools.partial(embed_kernel, pieces), in_specs=[WHOLE]...  2.39 us
    pallas_call x1, Pallas kernels, dense_after(): pl.pallas_call(after_kernel, in_specs=[WHOLE] * 11, out_specs=[WHOLE] * 7...  2.03 us
    pallas_call x1, Pallas kernels, first_half(): pl.pallas_call(first_kernel, in_specs=[ANY] * 3, out_specs=[WHOLE] * len(...  1.73 us
    pallas_call x1, Pallas kernels, dense_before(): pl.pallas_call(before_kernel, in_specs=[ANY] * 2 + [WHOLE] * 9, out_specs...  1.06 us
    ppermute x2, waiting for transfers between devices, paired(): moving = [lax.ppermute(total, axes, first) for total in totals]  0.88 us
    ppermute x2, starting transfers between devices, paired(): rest = [lax.ppermute(part, 'group', swap) for part in own]  0.7 us
  transfers between devices with their start and end apart: 9, of which 4 were waited for; matrix products, arithmetic and copies ran while one was open for 0% of the time, Pallas kernels for 26%

profile of v5, /device:TPU:0, one launch (start us, length us, event | category | flops | bytes accessed | tf_op | source)
XLA Modules:
  0.0 18.6 jit_solution(14611349937594820429)
XLA Ops:
  0.6 1.7 %first_half.1 = (f32[64,512]{1,0:T(8,128)S(1)}, f32[64,512]{1,0:T(8,128)S(1)}, f32[64,192]{1,0:T(8,128)S(1)}, bf16[192,1024]{1,0:T(8,128)(2,1)S(1)}, f32[192,1024]{1,0:T(8,128)S(1)}, /*index=5*/f32[192,1024]{1,0:T(8,128)S(1)}) custom-call(f32[64,192]{1,0:T(8,128)} %bitcast.21, bf16[192,2048]{1,0:T(8,128)(2,1)} %bitcast.20, f32[192,2048]{1,0:T(8,128)} %old_hbm.1), custom_call_target="tpu_custom_call" | custom-call | flops 75497472 | bytes 2359296 | tf_op jit(solution)/shard_map/first_half/pallas_call | solution.py:162
  2.4 0.5 %collective-permute-start = (f32[64,512]{1,0:T(8,128)S(1)}, f32[64,512]{1,0:T(8,128)S(1)}, u32[]{:S(2)}, u32[]{:S(2)}) collective-permute-start(f32[64,512]{1,0:T(8,128)S(1)} %get-tuple-element.37), channel_id=1, source_target_pairs={{0,16},{16,0},{1,17},{17,1},{2,18},{18,2},{3,19},{19,3},{4,20},{20... | collective-permute-start | bytes 393224 | tf_op jit(solution)/shard_map/ppermute | solution.py:595
  2.9 0.1 collective-permute-start.4
  3.0 0.0 copy-start.4
  3.0 0.0 copy-start.5
  3.0 0.0 copy-start.6
  3.0 0.0 copy-start.7
  3.0 0.0 copy-start.8
  3.0 0.3 %second_half.1 = (f32[64,512]{1,0:T(8,128)S(1)}, f32[64,512]{1,0:T(8,128)S(1)}, bf16[192,192]{1,0:T(8,128)(2,1)S(1)}) custom-call(f32[64,192]{1,0:T(8,128)S(1)} %get-tuple-element.33.basis_ref, bf16[192,1024]{1,0:T(8,128)(2,1)S(1)} %get-tuple-element.34.local_ref, f32[192,1024]{1,0:T(8,128)S(1)} %get-tuple-element.35.old_ref.refs_3_.refs_4_), custom_call_target="tpu_custom_call" | custom-call | flops 10000000000 | bytes 1179648 | tf_op jit(solution)/shard_map/second_half/pallas_call | solution.py:193
  3.4 0.5 %collective-permute-done.second_ref = f32[64,512]{1,0:T(8,128)S(1)} collective-permute-done((f32[64,512]{1,0:T(8,128)S(1)}, f32[64,512]{1,0:T(8,128)S(1)}, u32[]{:S(2)}, u32[]{:S(2)}) %collective-permute-start) | collective-permute-done | bytes 131104 | tf_op jit(solution)/shard_map/ppermute | solution.py:595
  3.9 2.7 %collective-permute-start.2 = (f32[64,512]{1,0:T(8,128)S(1)}, f32[64,512]{1,0:T(8,128)S(1)}, u32[]{:S(2)}, u32[]{:S(2)}) collective-permute-start(f32[64,512]{1,0:T(8,128)S(1)} %add.6.order_ref.first_ref), channel_id=1, source_target_pairs={{0,20},{4,28},{8,16},{12,24},{16,8},{20,0},{24,12},{28,4},{1,21},{... | collective-permute-start | bytes 393224 | tf_op jit(solution)/shard_map/ppermute | solution.py:610
  6.6 0.0 collective-permute-done.4.second_ref
  6.6 0.3 %collective-permute-start.5 = (f32[64,512]{1,0:T(8,128)S(1)}, f32[64,512]{1,0:T(8,128)S(1)}, u32[]{:S(2)}, u32[]{:S(2)}) collective-permute-start(f32[64,512]{1,0:T(8,128)S(1)} %add.8.first_ref), channel_id=1, source_target_pairs={{0,20},{4,28},{8,16},{12,24},{16,8},{20,0},{24,12},{28,4},{1,21},{... | collective-permute-start | bytes 393224 | tf_op jit(solution)/shard_map/ppermute | solution.py:610
  6.9 0.0 copy-done
  6.9 0.0 copy-done.1
  6.9 0.0 copy-done.2
  7.0 1.1 %dense_before.1 = (f32[6,584,128]{2,1,0:T(8,128)S(1)}, f32[64,2048]{1,0:T(8,128)S(1)}) custom-call(f32[64,512]{1,0:T(8,128)S(1)} %add.6.order_ref.first_ref, f32[64,2048]{1,0:T(8,128)} %moment_hbm.1, bf16[1,192,576]{2,1,0:T(8,128)(2,1)S(1)} %copy-done.4, bf16[1,192,192]{2,1,0:T(8,128)(2,1)S(1)} %copy-done.5, bf16[1,192,768]{2,1,0:T(8,128)(2,1)S(1)} %copy-done.2, ...), custom_call_target="tpu_custom_call" | custom-call | flops 8847360000 | bytes 4423680 | tf_op jit(solution)/shard_map/dense_before/pallas_call | solution.py:526
  8.1 0.3 %collective-permute-start.1 = (f32[6,584,128]{2,1,0:T(8,128)S(1)}, f32[6,584,128]{2,1,0:T(8,128)S(1)}, u32[]{:S(2)}, u32[]{:S(2)}) collective-permute-start(f32[6,584,128]{2,1,0:T(8,128)S(1)} %get-tuple-element.38.send_ref), channel_id=1, source_target_pairs={{0,16},{16,0},{1,17},{17,1},{2,18},{18,2},{3,19},{19,3},{4,20},{20... | collective-permute-start | bytes 5382152 | tf_op jit(solution)/shard_map/ppermute | solution.py:612
  8.3 0.9 %collective-permute-done.2.second_ref = f32[64,512]{1,0:T(8,128)S(1)} collective-permute-done((f32[64,512]{1,0:T(8,128)S(1)}, f32[64,512]{1,0:T(8,128)S(1)}, u32[]{:S(2)}, u32[]{:S(2)}) %collective-permute-start.2) | collective-permute-done | bytes 131104 | tf_op jit(solution)/shard_map/ppermute | solution.py:610
  9.2 2.1 %collective-permute-start.3 = (f32[64,512]{1,0:T(8,128)S(1)}, f32[64,512]{1,0:T(8,128)S(1)}, u32[]{:S(2)}, u32[]{:S(2)}) collective-permute-start(f32[64,512]{1,0:T(8,128)S(1)} %add.7.first_ref), channel_id=1, source_target_pairs={{0,24},{4,16},{8,28},{12,20},{16,4},{20,12},{24,0},{28,8},{1,25},{... | collective-permute-start | bytes 393224 | tf_op jit(solution)/shard_map/ppermute | solution.py:616
  11.4 0.0 collective-permute-done.5.second_ref
  11.4 1.2 %collective-permute-start.6 = (f32[64,512]{1,0:T(8,128)S(1)}, f32[64,512]{1,0:T(8,128)S(1)}, u32[]{:S(2)}, u32[]{:S(2)}) collective-permute-start(f32[64,512]{1,0:T(8,128)S(1)} %add.9.first_ref), channel_id=1, source_target_pairs={{0,24},{4,16},{8,28},{12,20},{16,4},{20,12},{24,0},{28,8},{1,25},{... | collective-permute-start | bytes 393224 | tf_op jit(solution)/shard_map/ppermute | solution.py:616
  12.6 0.0 collective-permute-done.1.recv_ref
  12.6 2.0 %dense_after.1 = (f32[192,576]{1,0:T(8,128)}, f32[192,192]{1,0:T(8,128)}, f32[192,768]{1,0:T(8,128)}, f32[192,768]{1,0:T(8,128)}, f32[1728,128]{1,0:T(8,128)}, /*index=5*/f32[1920]{0:T(1024)}, f32[1,960]{1,0:T(1,128)}) custom-call(f32[6,584,128]{2,1,0:T(8,128)S(1)} %collective-permute-done.1.recv_ref, f32[6,584,128]{2,1,0:T(8,128)S(1)} %get-tuple-element.38.send_ref, ...), custom_call_target="tpu_custom_call" | custom-call | flops 8847360000 | bytes 5898240 | tf_op jit(solution)/shard_map/dense_after/pallas_call | solution.py:547
  14.7 0.0 collective-permute-done.3.second_ref
  14.7 0.5 %collective-permute-start.8 = (f32[64,512]{1,0:T(8,128)S(1)}, f32[64,512]{1,0:T(8,128)S(1)}, u32[]{:S(2)}, u32[]{:S(2)}) collective-permute-start(f32[64,512]{1,0:T(8,128)S(1)} %add.11.refs_0_), channel_id=1, source_target_pairs={{0,16},{16,0},{1,17},{17,1},{2,18},{18,2},{3,19},{19,3},{4,20},{20... | collective-permute-start | bytes 393224 | tf_op jit(solution)/shard_map/ppermute | solution.py:620
  15.2 0.7 %collective-permute-done.6.second_ref = f32[64,512]{1,0:T(8,128)S(1)} collective-permute-done((f32[64,512]{1,0:T(8,128)S(1)}, f32[64,512]{1,0:T(8,128)S(1)}, u32[]{:S(2)}, u32[]{:S(2)}) %collective-permute-start.6) | collective-permute-done | bytes 131104 | tf_op jit(solution)/shard_map/ppermute | solution.py:616
  15.9 0.2 collective-permute-start.7
  16.1 0.1 collective-permute-done.8.refs_2_
  16.2 1.4 %embed_pieces.2 = (f32[192,2048]{1,0:T(8,128)}, f32[64,2048]{1,0:T(8,128)}) custom-call(bf16[192,192]{1,0:T(8,128)(2,1)S(1)} %get-tuple-element.47.stack_ref, f32[64,2048]{1,0:T(8,128)S(1)} %get-tuple-element.48.moment_ref, f32[64,512]{1,0:T(8,128)S(1)} %add.11.refs_0_, f32[64,512]{1,0:T(8,128)S(1)} %add.10.refs_1_, ...), custom_call_target="tpu_custom_call" | custom-call | flops 113246208 | bytes 2359296 | tf_op jit(solution)/shard_map/embed_pieces/pallas_call | solution.py:259
  17.6 0.0 collective-permute-done.7.refs_0_
  17.6 1.0 %embed_pieces.3 = (f32[192,2048]{1,0:T(8,128)}, f32[64,2048]{1,0:T(8,128)}) custom-call(bf16[192,192]{1,0:T(8,128)(2,1)S(1)} %get-tuple-element.47.stack_ref, f32[64,2048]{1,0:T(8,128)S(1)} %get-tuple-element.48.moment_ref, f32[64,512]{1,0:T(8,128)S(1)} %collective-permute-done.7.refs_0_, ...), custom_call_target="tpu_custom_call", output_to_operand_aliasing={{0}: (4, {}), {1}: (5, {})} | custom-call | flops 37748736 | bytes 786432 | tf_op jit(solution)/shard_map/embed_pieces/pallas_call | solution.py:259
  (16 shorter events, 0.1 us)
Async XLA Ops:
  2.4 1.5 %collective-permute-start = (f32[64,512]{1,0:T(8,128)S(1)}, f32[64,512]{1,0:T(8,128)S(1)}, u32[]{:S(2)}, u32[]{:S(2)}) collective-permute-start(f32[64,512]{1,0:T(8,128)S(1)} %get-tuple-element.37), channel_id=1, source_target_pairs={{0,16},{16,0},{1,17},{17,1},{2,18},{18,2},{3,19},{19,3},{4,20},{20... | collective-permute-start | bytes 393224 | tf_op jit(solution)/shard_map/ppermute | solution.py:595
  2.9 3.7 %collective-permute-start.4 = (f32[64,512]{1,0:T(8,128)S(1)}, f32[64,512]{1,0:T(8,128)S(1)}, u32[]{:S(2)}, u32[]{:S(2)}) collective-permute-start(f32[64,512]{1,0:T(8,128)S(1)} %get-tuple-element.50), channel_id=1, source_target_pairs={{0,16},{16,0},{1,17},{17,1},{2,18},{18,2},{3,19},{19,3},{4,20},{20... | collective-permute-start | bytes 393224 | tf_op jit(solution)/shard_map/ppermute | solution.py:595
  3.0 4.0 %copy-start = (f32[1,221184]{1,0:T(1,128)S(1)}, f32[1,221184]{1,0:T(1,128)}, u32[]{:S(2)}) copy-start(f32[1,221184]{1,0:T(1,128)} %param.18) | copy-start | bytes 2654212
  3.0 4.0 %copy-start.1 = (f32[1,221184]{1,0:T(1,128)S(1)}, f32[1,221184]{1,0:T(1,128)}, u32[]{:S(2)}) copy-start(f32[1,221184]{1,0:T(1,128)} %param.19) | copy-start | bytes 2654212
  3.0 4.0 %copy-start.2 = (bf16[1,192,768]{2,1,0:T(8,128)(2,1)S(1)}, bf16[1,192,768]{2,1,0:T(8,128)(2,1)}, u32[]{:S(2)}) copy-start(bf16[1,192,768]{2,1,0:T(8,128)(2,1)} %up_ref.3) | copy-start | bytes 884740
  3.0 4.0 %copy-start.3 = (bf16[1,768,192]{1,2,0:T(8,128)(2,1)S(1)}, bf16[1,768,192]{1,2,0:T(8,128)(2,1)}, u32[]{:S(2)}) copy-start(bf16[1,768,192]{1,2,0:T(8,128)(2,1)} %param.16) | copy-start | bytes 884740
  3.0 4.0 %copy-start.4 = (bf16[1,192,576]{2,1,0:T(8,128)(2,1)S(1)}, bf16[1,192,576]{2,1,0:T(8,128)(2,1)}, u32[]{:S(2)}) copy-start(bf16[1,192,576]{2,1,0:T(8,128)(2,1)} %in_ref.3) | copy-start | bytes 663556
  3.0 4.0 %copy-start.5 = (bf16[1,192,192]{2,1,0:T(8,128)(2,1)S(1)}, bf16[1,192,192]{2,1,0:T(8,128)(2,1)}, u32[]{:S(2)}) copy-start(bf16[1,192,192]{2,1,0:T(8,128)(2,1)} %out_ref.3) | copy-start | bytes 221188
  3.0 4.0 %copy-start.6 = (bf16[1,1920]{1,0:T(2,128)(2,1)S(1)}, bf16[1,1920]{1,0:T(2,128)(2,1)}, u32[]{:S(2)}) copy-start(bf16[1,1920]{1,0:T(2,128)(2,1)} %small_ref.3) | copy-start | bytes 11524
  3.0 4.0 %copy-start.7 = (f32[960]{0:T(1024)S(1)}, f32[960]{0:T(1024)}, u32[]{:S(2)}) copy-start(f32[960]{0:T(1024)} %param.20) | copy-start | bytes 11524
  3.0 4.0 %copy-start.8 = (f32[960]{0:T(1024)S(1)}, f32[960]{0:T(1024)}, u32[]{:S(2)}) copy-start(f32[960]{0:T(1024)} %param.21) | copy-start | bytes 11524
  3.9 5.3 %collective-permute-start.2 = (f32[64,512]{1,0:T(8,128)S(1)}, f32[64,512]{1,0:T(8,128)S(1)}, u32[]{:S(2)}, u32[]{:S(2)}) collective-permute-start(f32[64,512]{1,0:T(8,128)S(1)} %add.6.order_ref.first_ref), channel_id=1, source_target_pairs={{0,20},{4,28},{8,16},{12,24},{16,8},{20,0},{24,12},{28,4},{1,21},{... | collective-permute-start | bytes 393224 | tf_op jit(solution)/shard_map/ppermute | solution.py:610
  6.6 4.8 %collective-permute-start.5 = (f32[64,512]{1,0:T(8,128)S(1)}, f32[64,512]{1,0:T(8,128)S(1)}, u32[]{:S(2)}, u32[]{:S(2)}) collective-permute-start(f32[64,512]{1,0:T(8,128)S(1)} %add.8.first_ref), channel_id=1, source_target_pairs={{0,20},{4,28},{8,16},{12,24},{16,8},{20,0},{24,12},{28,4},{1,21},{... | collective-permute-start | bytes 393224 | tf_op jit(solution)/shard_map/ppermute | solution.py:610
  8.1 4.6 %collective-permute-start.1 = (f32[6,584,128]{2,1,0:T(8,128)S(1)}, f32[6,584,128]{2,1,0:T(8,128)S(1)}, u32[]{:S(2)}, u32[]{:S(2)}) collective-permute-start(f32[6,584,128]{2,1,0:T(8,128)S(1)} %get-tuple-element.38.send_ref), channel_id=1, source_target_pairs={{0,16},{16,0},{1,17},{17,1},{2,18},{18,2},{3,19},{19,3},{4,20},{20... | collective-permute-start | bytes 5382152 | tf_op jit(solution)/shard_map/ppermute | solution.py:612
  9.2 5.4 %collective-permute-start.3 = (f32[64,512]{1,0:T(8,128)S(1)}, f32[64,512]{1,0:T(8,128)S(1)}, u32[]{:S(2)}, u32[]{:S(2)}) collective-permute-start(f32[64,512]{1,0:T(8,128)S(1)} %add.7.first_ref), channel_id=1, source_target_pairs={{0,24},{4,16},{8,28},{12,20},{16,4},{20,12},{24,0},{28,8},{1,25},{... | collective-permute-start | bytes 393224 | tf_op jit(solution)/shard_map/ppermute | solution.py:616
  11.4 4.5 %collective-permute-start.6 = (f32[64,512]{1,0:T(8,128)S(1)}, f32[64,512]{1,0:T(8,128)S(1)}, u32[]{:S(2)}, u32[]{:S(2)}) collective-permute-start(f32[64,512]{1,0:T(8,128)S(1)} %add.9.first_ref), channel_id=1, source_target_pairs={{0,24},{4,16},{8,28},{12,20},{16,4},{20,12},{24,0},{28,8},{1,25},{... | collective-permute-start | bytes 393224 | tf_op jit(solution)/shard_map/ppermute | solution.py:616
  14.7 1.5 %collective-permute-start.8 = (f32[64,512]{1,0:T(8,128)S(1)}, f32[64,512]{1,0:T(8,128)S(1)}, u32[]{:S(2)}, u32[]{:S(2)}) collective-permute-start(f32[64,512]{1,0:T(8,128)S(1)} %add.11.refs_0_), channel_id=1, source_target_pairs={{0,16},{16,0},{1,17},{17,1},{2,18},{18,2},{3,19},{19,3},{4,20},{20... | collective-permute-start | bytes 393224 | tf_op jit(solution)/shard_map/ppermute | solution.py:620
  15.9 1.7 %collective-permute-start.7 = (f32[64,512]{1,0:T(8,128)S(1)}, f32[64,512]{1,0:T(8,128)S(1)}, u32[]{:S(2)}, u32[]{:S(2)}) collective-permute-start(f32[64,512]{1,0:T(8,128)S(1)} %add.10.refs_1_), channel_id=1, source_target_pairs={{0,16},{16,0},{1,17},{17,1},{2,18},{18,2},{3,19},{19,3},{4,20},{20... | collective-permute-start | bytes 393224 | tf_op jit(solution)/shard_map/ppermute | solution.py:620

commit v6 on v5

--- a/solution.py
+++ b/solution.py
@@ -98,6 +98,7 @@
 
 
 CHUNKS = 2
+ROW_CUTS = 2
 WHOLE = pl.BlockSpec(memory_space=pltpu.VMEM)
 ANY = pl.BlockSpec(memory_space=pl.ANY)
 
@@ -125,159 +126,185 @@
     return first[:rank] + first[rank:] + jnp.dot(high, diff_low, preferred_element_type=f32)
 
 
-def first_kernel(basis_hbm, local_hbm, old_hbm, *refs):
-    out_refs = refs[:CHUNKS]
-    basis_ref, local_own, old_own, old_rest, local_rest, sems = refs[CHUNKS:]
-    columns = old_own.shape[1]
-    block = columns // CHUNKS
+def first_kernel(basis_hbm, local_hbm, old_hbm, out_ref, basis_ref, local_ref, old_ref, sems):
+    block = out_ref.shape[1]
+    start = side_start(True, CHUNKS * block)
+    there = pl.ds(pl.multiple_of(start, block), block)
+    rows = old_hbm.shape[0] // ROW_CUTS
     copies = [pltpu.make_async_copy(basis_hbm, basis_ref, sems.at[0])]
-    for k in range(CHUNKS):
-        there = pl.ds(pl.multiple_of(side_start(True, columns) + k * block, block), block)
-        here = pl.ds(k * block, block)
-        for source, target in ((old_hbm, old_rest), (local_hbm, local_rest)):
+    for k in range(ROW_CUTS):
+        cut = pl.ds(k * rows, rows)
+        for source, target in ((old_hbm, old_ref), (local_hbm, local_ref)):
             at = sems.at[len(copies)]
-            copies.append(pltpu.make_async_copy(source.at[:, there], target.at[:, here], at))
-    there = pl.ds(pl.multiple_of(side_start(False, columns), columns), columns)
-    for source, target in ((old_hbm, old_own), (local_hbm, local_own)):
-        copies.append(pltpu.make_async_copy(source.at[:, there], target, sems.at[len(copies)]))
+            copies.append(pltpu.make_async_copy(source.at[cut, there], target.at[cut, :], at))
     for copy in copies:
         copy.start()
-    copies[0].wait()
-    basis = basis_ref[...]
-    for k in range(CHUNKS):
-        copies[1 + 2 * k].wait()
-        copies[2 + 2 * k].wait()
-        here = slice(k * block, (k + 1) * block)
-        out_refs[k][...] = product(basis, local_rest[:, here], old_rest[:, here])
-    copies[-2].wait()
-    copies[-1].wait()
-
-
-def first_half(basis_t, local, old):
+    for copy in copies:
+        copy.wait()
+    out_ref[...] = product(basis_ref[...], local_ref[...], old_ref[...])
+
+
+def first_part(basis_t, local, old):
     rank, depth = basis_t.shape
-    columns = old.shape[1] // 2
-    shapes = [((rank, columns // CHUNKS), f32)] * CHUNKS
-    shapes += [((rank, depth), f32), ((depth, columns), bf16)]
-    shapes += [((depth, columns), f32)] * 2
+    block = old.shape[1] // (2 * CHUNKS)
     return pl.pallas_call(
         first_kernel,
         in_specs=[ANY] * 3,
-        out_specs=[WHOLE] * len(shapes),
-        out_shape=[jax.ShapeDtypeStruct(*shape) for shape in shapes],
+        out_specs=WHOLE,
+        out_shape=jax.ShapeDtypeStruct((rank, block), f32),
         scratch_shapes=[
-            pltpu.VMEM((depth, columns), bf16),
-            pltpu.SemaphoreType.DMA((3 + 2 * CHUNKS,)),
+            pltpu.VMEM((rank, depth), f32),
+            pltpu.VMEM((depth, block), bf16),
+            pltpu.VMEM((depth, block), f32),
+            pltpu.SemaphoreType.DMA((1 + 2 * ROW_CUTS,)),
         ],
-        compiler_params=pltpu.CompilerParams(vmem_limit_bytes=8 * 2**20),
+        compiler_params=pltpu.CompilerParams(vmem_limit_bytes=4 * 2**20),
         cost_estimate=pl.CostEstimate(
-            flops=6 * rank * depth * columns, bytes_accessed=12 * depth * columns, transcendentals=0
+            flops=6 * rank * depth * block, bytes_accessed=6 * depth * block, transcendentals=0
         ),
-        name="first_half",
+        name="first_part",
     )(*in_hbm((basis_t, local, old)))
 
 
-def second_kernel(basis_ref, local_ref, old_ref, *refs):
+def other_kernel(basis_ref, local_ref, old_ref, rest_ref, *refs):
     *out_refs, stack_ref = refs
     basis = basis_ref[...]
-    block = old_ref.shape[1] // CHUNKS
-    for k, out_ref in enumerate(out_refs):
-        here = slice(k * block, (k + 1) * block)
-        out_ref[...] = product(basis, local_ref[:, here], old_ref[:, here])
+    block = rest_ref.shape[1]
+    columns = CHUNKS * block
+    places = [(True, k) for k in range(1, CHUNKS)] + [(False, k) for k in range(CHUNKS)]
+    for (other, k), out_ref in zip(places, (rest_ref, *out_refs)):
+        there = pl.ds(pl.multiple_of(side_start(other, columns) + k * block, block), block)
+        out_ref[...] = product(basis, local_ref[:, there], old_ref[:, there])
     high = basis.astype(bf16).astype(f32)
     stack_ref[...] = jnp.concatenate([high, basis - high, high], axis=0).T.astype(bf16)
 
 
-def second_half(basis, local, old):
-    rank, depth = basis.shape
-    columns = old.shape[1]
+def other_parts(basis_t, local, old):
+    rank, depth = basis_t.shape
+    block = old.shape[1] // (2 * CHUNKS)
     return pl.pallas_call(
-        second_kernel,
+        other_kernel,
         in_specs=[WHOLE] * 3,
-        out_specs=[WHOLE] * (CHUNKS + 1),
-        out_shape=[jax.ShapeDtypeStruct((rank, columns // CHUNKS), f32)] * CHUNKS
+        out_specs=[WHOLE] * (2 * CHUNKS),
+        out_shape=[jax.ShapeDtypeStruct((rank, block), f32)] * (2 * CHUNKS - 1)
         + [jax.ShapeDtypeStruct((depth, 3 * rank), bf16)],
         compiler_params=pltpu.CompilerParams(vmem_limit_bytes=4 * 2**20),
         cost_estimate=pl.CostEstimate(
-            flops=10**10, bytes_accessed=6 * depth * columns, transcendentals=0
+            flops=10**10, bytes_accessed=18 * depth * block, transcendentals=0
         ),
-        name="second_half",
-    )(basis, local, old)
-
-
-def add_kernel(scale, first_ref, second_ref, *out_refs):
-    width = out_refs[0].shape[1]
-    for part, out_ref in enumerate(out_refs):
-        here = slice(part * width, (part + 1) * width)
-        out_ref[...] = scale * (first_ref[:, here] + second_ref[:, here])
-
-
-def add(first, second, parts=1, scale=1.0, flops=2 * 10**10):
-    rows, columns = first.shape
+        name="other_parts",
+    )(basis_t, local, old)
+
+
+def add_kernel(scale, first_ref, second_ref, *refs):
+    refs[-1][...] = scale * (first_ref[...] + second_ref[...])
+
+
+def add(first, second, after=(), scale=1.0, flops=2 * 10**10):
     return pl.pallas_call(
         functools.partial(add_kernel, scale),
-        in_specs=[WHOLE] * 2,
-        out_specs=[WHOLE] * parts,
-        out_shape=[jax.ShapeDtypeStruct((rows, columns // parts), f32)] * parts,
+        in_specs=[WHOLE] * 2 + [ANY] * len(after),
+        out_specs=WHOLE,
+        out_shape=jax.ShapeDtypeStruct(first.shape, f32),
         compiler_params=pltpu.CompilerParams(vmem_limit_bytes=2 * 2**20),
         cost_estimate=pl.CostEstimate(flops=flops, bytes_accessed=0, transcendentals=0),
         name="add",
-    )(first, second)
-
-
-def embed_kernel(pieces, stack_ref, moment_ref, *refs):
+    )(first, second, *after)
+
+
+def embed_piece(start, width, coeff, stack_ref, moment_ref, old_ref):
+    there = pl.ds(pl.multiple_of(start, width), width)
+    moved = momentum_coef * moment_ref[:, there] + coeff
+    up_high, up_low = split(coeff + momentum_coef * moved)
+    change = jnp.dot(
+        stack_ref[...],
+        jnp.concatenate([up_high, up_high, up_low], axis=0),
+        preferred_element_type=f32,
+    )
+    return old_ref[:, there] - outer_rate * change, moved
+
+
+def early_kernel(stack_ref, moment_ref, old_ref, coeff_ref, embed_ref, moved_ref):
+    start = side_start(False, old_ref.shape[1] // 2)
+    embed_ref[...], moved_ref[...] = embed_piece(
+        start, coeff_ref.shape[1], coeff_ref[...], stack_ref, moment_ref, old_ref
+    )
+
+
+def embed_early(stack, moment, old, coeff):
+    depth, (rank, width) = old.shape[0], coeff.shape
+    return pl.pallas_call(
+        early_kernel,
+        in_specs=[WHOLE] * 4,
+        out_specs=[WHOLE] * 2,
+        out_shape=[
+            jax.ShapeDtypeStruct((depth, width), f32),
+            jax.ShapeDtypeStruct((rank, width), f32),
+        ],
+        compiler_params=pltpu.CompilerParams(vmem_limit_bytes=4 * 2**20),
+        cost_estimate=pl.CostEstimate(
+            flops=6 * rank * depth * width, bytes_accessed=8 * depth * width, transcendentals=0
+        ),
+        name="embed_early",
+    )(stack, moment, old, coeff)
+
+
+def embed_kernel(pieces, ready, stack_ref, moment_ref, old_ref, *refs):
     count = len(pieces)
-    coeffs, olds = refs[:count], refs[count : 2 * count]
+    coeffs, refs = refs[:count], refs[count:]
     embed_hbm, moved_hbm, embed_ref, moved_ref, sems = refs[-5:]
     width = coeffs[0].shape[1]
     copies = []
-    for k, (other, part) in enumerate(pieces):
-        start = side_start(other, olds[k].shape[1]) + part * width
+
+    def start_of(other, part):
+        return side_start(other, old_ref.shape[1] // 2) + part * width
+
+    def send(start, embed, moved):
         there = pl.ds(pl.multiple_of(start, width), width)
-        coeff = coeffs[k][...]
-        moved = momentum_coef * moment_ref[:, there] + coeff
-        moved_ref[k] = moved
-        up_high, up_low = split(coeff + momentum_coef * moved)
-        change = jnp.dot(
-            stack_ref[...],
-            jnp.concatenate([up_high, up_high, up_low], axis=0),
-            preferred_element_type=f32,
+        for source, target in ((moved, moved_hbm), (embed, embed_hbm)):
+            copies.append(
+                pltpu.make_async_copy(source, target.at[:, there], sems.at[len(copies)])
+            )
+            copies[-1].start()
+
+    if ready:
+        send(start_of(*ready), refs[0], refs[1])
+    for k, piece in enumerate(pieces):
+        start = start_of(*piece)
+        embed_ref[k], moved_ref[k] = embed_piece(
+            start, width, coeffs[k][...], stack_ref, moment_ref, old_ref
         )
-        embed_ref[k] = olds[k][:, part * width : (part + 1) * width] - outer_rate * change
-        for source, target, at in ((moved_ref, moved_hbm, 0), (embed_ref, embed_hbm, 1)):
-            copy = pltpu.make_async_copy(source.at[k], target.at[:, there], sems.at[2 * k + at])
-            copy.start()
-            copies.append(copy)
+        send(start, embed_ref.at[k], moved_ref.at[k])
     for copy in copies:
         copy.wait()
 
 
-def embed_pieces(pieces, stack, moment, coeffs, olds, before):
+def embed_pieces(pieces, ready, stack, moment, old, coeffs, early, before):
     count = len(pieces)
     rank, width = coeffs[0].shape
-    depth, columns = olds[0].shape
-    first = 2 + 2 * count
+    first = 3 + count + len(early)
     return pl.pallas_call(
-        functools.partial(embed_kernel, pieces),
+        functools.partial(embed_kernel, pieces, ready),
         in_specs=[WHOLE] * first + [ANY] * len(before),
         out_specs=[ANY, ANY],
         out_shape=[
-            jax.ShapeDtypeStruct((depth, 2 * columns), f32),
-            jax.ShapeDtypeStruct((rank, 2 * columns), f32),
+            jax.ShapeDtypeStruct(old.shape, f32),
+            jax.ShapeDtypeStruct(moment.shape, f32),
         ],
         scratch_shapes=[
-            pltpu.VMEM((count, depth, width), f32),
+            pltpu.VMEM((count, old.shape[0], width), f32),
             pltpu.VMEM((count, rank, width), f32),
-            pltpu.SemaphoreType.DMA((2 * count,)),
+            pltpu.SemaphoreType.DMA((2 * count + len(early),)),
         ],
         input_output_aliases={first: 0, first + 1: 1} if before else {},
         compiler_params=pltpu.CompilerParams(vmem_limit_bytes=8 * 2**20),
         cost_estimate=pl.CostEstimate(
-            flops=6 * count * rank * depth * width,
-            bytes_accessed=8 * count * depth * width,
+            flops=6 * count * rank * old.shape[0] * width,
+            bytes_accessed=8 * count * old.shape[0] * width,
             transcendentals=0,
         ),
         name="embed_pieces",
-    )(stack, moment, *coeffs, *olds, *before)
+    )(stack, moment, old, *coeffs, *early, *before)
 
 
 def low_lanes(rows):
@@ -420,9 +447,22 @@
 
 def after_kernel(
     recv_ref, send_ref, in_ref, out_ref, up_ref, down_ref, old_ref, mom_ref, small_ref,
-    small_old_ref, small_mom_ref, in_next_ref, out_next_ref, up_next_ref, down_next_ref, moved_ref,
-    small_next_ref, small_moved_ref, sum_ref, wide_ref,
+    small_old_ref, small_mom_ref, *refs,
 ):
+    targets, sources, (sum_ref, wide_ref, sems) = refs[:7], refs[7:14], refs[14:]
+    (
+        in_next_ref, out_next_ref, up_next_ref, down_next_ref, moved_ref, small_next_ref,
+        small_moved_ref,
+    ) = sources
+    copies = [
+        pltpu.make_async_copy(source, target, sems.at[k])
+        for k, (source, target) in enumerate(zip(sources, targets))
+    ]
+
+    def go(*numbers):
+        for k in numbers:
+            copies[k].start()
+
     rows = up_ref.shape[1]
     mid = rows // 2
     block = rows + mid
@@ -470,6 +510,7 @@
             theirs = recv_ref[k, :rows, :]
             put_attn(k, send_ref[k, block : block + rows, :] + local_coef * theirs)
             sum_ref[k, :, :] = value + theirs
+        go(0, 1)
         for start, stride, value in flatten_attn(get, rows):
             put_moved(start, stride, value)
         base = rows * tiles
@@ -486,13 +527,18 @@
             down_next_ref[:, columns] = recv_ref[k, block + mid : 2 * block, :] + (
                 local_coef * down_ref[0, :, columns].astype(f32)
             )
+        go(2, 3, 4)
         values = small_ref[...].astype(f32)
         put_small(values[:, small:], values[:, :small], True)
+        go(5, 6)
+        for copy in copies:
+            copy.wait()
 
     @pl.when(group == 1)
     def _():
         for k, value in enumerate(attn_tiles(in_ref, out_ref)):
             put_attn(k, recv_ref[k, block : block + rows, :] + local_coef * value)
+        go(0, 1)
         for k in range(tiles):
             columns = slice(k * LANES, (k + 1) * LANES)
             up_next_ref[:mid, columns] = recv_ref[k, block + rows : 2 * block, :] + (
@@ -509,6 +555,7 @@
             wide_ref[0, columns, :] = total[:LANES].T
             lower = jnp.concatenate([total[LANES:], total[LANES:]], axis=0)
             wide_ref[1, columns, :] = lower.T
+        go(2, 3)
         base = mid * tiles
         pairs = tiles * HALF
         low = low_lanes(pairs)
@@ -517,8 +564,12 @@
         put_moved(base, 3, wide_ref[0, even, :])
         put_moved(base + 1, 3, jnp.where(low, wide_ref[1, even, :], odd_first))
         put_moved(base + 2, 3, jnp.where(low, odd_first, wide_ref[1, odd, :]))
+        go(4)
         values = small_ref[...].astype(f32)
         put_small(values[:, :small], values[:, small:], False)
+        go(5, 6)
+        for copy in copies:
+            copy.wait()
 
 
 def dense_before(order, moment, operands):
@@ -547,11 +598,13 @@
     return pl.pallas_call(
         after_kernel,
         in_specs=[WHOLE] * 11,
-        out_specs=[WHOLE] * 7,
+        out_specs=[ANY] * 7,
         out_shape=[jax.ShapeDtypeStruct(shape, f32) for shape in outs],
-        scratch_shapes=[
+        scratch_shapes=[pltpu.VMEM(shape, f32) for shape in outs]
+        + [
             pltpu.VMEM((width // LANES, rows, LANES), f32),
             pltpu.VMEM((2, width, LANES), f32),
+            pltpu.SemaphoreType.DMA((7,)),
         ],
         compiler_params=pltpu.CompilerParams(vmem_limit_bytes=8 * 2**20),
         cost_estimate=pl.CostEstimate(
@@ -589,11 +642,10 @@
     )
     axes = ("group", "shard")
 
-    *theirs, basis_t, local_own, old_own, old_rest = first_half(
-        basis.T, embed_local[0], embed_old
-    )
-    theirs = [lax.ppermute(part, "group", swap) for part in theirs]
-    *mine, stack = second_half(basis_t, local_own, old_own)
+    embed = (basis.T, embed_local[0], embed_old)
+    theirs = [lax.ppermute(first_part(*embed), "group", swap)]
+    late, *mine, stack = other_parts(*embed)
+    theirs.append(lax.ppermute(late, "group", swap))
 
     operands = (
         attn_in_local,
@@ -606,25 +658,26 @@
         small_old[None, :],
         small_momentum[None, :],
     )
-    totals = [add(*pair, flops=10**4)[0] for pair in zip(mine, theirs)]
+    totals = [add(*pair, flops=10**4) for pair in zip(mine, theirs)]
     moving = [lax.ppermute(total, axes, first) for total in totals]
     sent, moment = dense_before(totals[0], coeff_momentum, operands)
     received = lax.ppermute(sent, "group", swap)
     totals = [
-        add(*pair, flops=flops)[0] for *pair, flops in zip(totals, moving, (10**4, 2 * 10**10))
+        add(*pair, flops=flops) for *pair, flops in zip(totals, moving, (10**4, 2 * 10**10))
     ]
     moving = [lax.ppermute(total, axes, second) for total in totals]
     dense = list(dense_after(received, sent, operands))
     moving[0], dense[-1] = lax.optimization_barrier((moving[0], dense[-1]))
-    own = [add(*pair, scale=0.5)[0] for pair in zip(totals, moving)]
-    rest = [lax.ppermute(part, "group", swap) for part in own]
-    done = ()
-    for pieces, coeffs in (
-        (((False, 0), (False, 1), (True, 0)), (*own, rest[0])),
-        (((True, 1),), rest[1:]),
-    ):
-        olds = [old_rest if other else old_own for other, _ in pieces]
-        done = embed_pieces(pieces, stack, moment, coeffs, olds, done)
+    own = [add(totals[0], moving[0], scale=0.5)]
+    rest = [lax.ppermute(own[0], "group", swap)]
+    early = embed_early(stack, moment, embed_old, own[0])
+    own.append(add(totals[1], moving[1], early[:1], scale=0.5))
+    rest.append(lax.ppermute(own[1], "group", swap))
+    shared = (stack, moment, embed_old)
+    done = embed_pieces(
+        ((False, 1), (True, 0)), (False, 0), *shared, (own[1], rest[0]), early, ()
+    )
+    done = embed_pieces(((True, 1),), None, *shared, rest[1:], (), done)
     embed_next, coeff_moved = done
 
     attn_in_next, attn_out_next, ffn_in_next, ffn_out_next, moved, small_next, small_moved = dense

time: 18.8 us -> 18.6 us (0.989)
  waiting for transfers between devices: 2.21 us -> 1.39 us
  starting transfers between devices: 7.94 us -> 8.63 us
  Pallas kernels: 7.6 us -> 7.4 us
    ppermute x2, starting transfers between devices: 3.01 us -> 3.49 us  [paired(): moving = [lax.ppermute(total, axes, first) for total in totals]]
    ppermute x2, waiting for transfers between devices: 0.88 us -> 0.44 us  [paired(): moving = [lax.ppermute(total, axes, first) for total in totals]]
    ppermute x4, starting transfers between devices: 1.3 us -> 1.54 us  [the longest x1 0.66 us: paired(): rest = [lax.ppermute(own[0], 'group', swap)]]
    ppermute x4, waiting for transfers between devices: 0.66 us -> 0.45 us  [the longest x1 0.38 us: paired(): theirs = [lax.ppermute(first_part(*embed), 'group', swap)]]
    pallas_call x5 -> x6, Pallas kernels: 6.45 us -> 6.25 us  [the longest x2 2.24 us: embed_pieces(): pl.pallas_call(functools.partial(embed_kernel, pieces, ready), in_specs=[...]
where the time goes in v6:
time: 18.6 us; the launch traced here: 18.4 us
  starting transfers between devices  8.63 us (46%)
  Pallas kernels  7.4 us (40%)
  waiting for transfers between devices  1.39 us (7%)
  between operations  0.87 us (5%)
    ppermute x2, starting transfers between devices, paired(): moving = [lax.ppermute(total, axes, first) for total in totals]  3.49 us
    ppermute x2, starting transfers between devices, paired(): moving = [lax.ppermute(total, axes, second) for total in totals]  3.36 us
    pallas_call x2, Pallas kernels, embed_pieces(): pl.pallas_call(functools.partial(embed_kernel, pieces, ready), in_specs=[...  2.24 us
    pallas_call x1, Pallas kernels, dense_after(): pl.pallas_call(after_kernel, in_specs=[WHOLE] * 11, out_specs=[ANY] * 7,...  1.79 us
    pallas_call x1, Pallas kernels, first_part(): pl.pallas_call(first_kernel, in_specs=[ANY] * 3, out_specs=WHOLE, out_sha...  1.58 us
    pallas_call x1, Pallas kernels, dense_before(): pl.pallas_call(before_kernel, in_specs=[ANY] * 2 + [WHOLE] * 9, out_specs...  1.06 us
    ppermute x1, starting transfers between devices, paired(): rest = [lax.ppermute(own[0], 'group', swap)]  0.66 us
    ppermute x1, starting transfers between devices, paired(): theirs = [lax.ppermute(first_part(*embed), 'group', swap)]  0.52 us
  transfers between devices with their start and end apart: 9, of which 4 were waited for; matrix products, arithmetic and copies ran while one was open for 0% of the time, Pallas kernels for 26%

profile of v6, /device:TPU:0, one launch (start us, length us, event | category | flops | bytes accessed | tf_op | source)
XLA Modules:
  0.0 18.4 jit_solution(11492414200541772812)
XLA Ops:
  0.7 1.6 %first_part.1 = f32[64,512]{1,0:T(8,128)S(1)} custom-call(f32[64,192]{1,0:T(8,128)} %bitcast.12, bf16[192,2048]{1,0:T(8,128)(2,1)} %bitcast.10, f32[192,2048]{1,0:T(8,128)} %old_ref.7), custom_call_target="tpu_custom_call" | custom-call | flops 37748736 | bytes 589824 | tf_op jit(solution)/shard_map/first_part/pallas_call | solution.py:150
  2.3 0.0 copy-start.3
  2.3 0.0 copy-start.4
  2.3 0.0 copy-start.5
  2.3 0.0 copy-start.6
  2.3 0.0 copy-start.7
  2.3 0.0 copy-start.8
  2.3 0.0 copy-start.9
  2.3 0.0 copy-start.10
  2.4 0.0 copy-start.11
  2.4 0.5 %collective-permute-start = (f32[64,512]{1,0:T(8,128)S(1)}, f32[64,512]{1,0:T(8,128)S(1)}, u32[]{:S(2)}, u32[]{:S(2)}) collective-permute-start(f32[64,512]{1,0:T(8,128)S(1)} %first_part.1), channel_id=1, source_target_pairs={{0,16},{16,0},{1,17},{17,1},{2,18},{18,2},{3,19},{19,3},{4,20},{20... | collective-permute-start | bytes 393224 | tf_op jit(solution)/shard_map/ppermute | solution.py:646
  2.9 0.4 %other_parts.1 = (f32[64,512]{1,0:T(8,128)S(1)}, f32[64,512]{1,0:T(8,128)S(1)}, f32[64,512]{1,0:T(8,128)S(1)}, bf16[192,192]{1,0:T(8,128)(2,1)S(1)}) custom-call(f32[64,192]{1,0:T(8,128)S(1)} %bitcast.13, bf16[192,2048]{1,0:T(8,128)(2,1)S(1)} %bitcast.11, f32[192,2048]{1,0:T(8,128)S(1)} %copy-done), custom_call_target="tpu_custom_call" | custom-call | flops 10000000000 | bytes 1769472 | tf_op jit(solution)/shard_map/other_parts/pallas_call | solution.py:185
  3.3 0.2 collective-permute-start.4
  3.5 0.4 %collective-permute-done.second_ref = f32[64,512]{1,0:T(8,128)S(1)} collective-permute-done((f32[64,512]{1,0:T(8,128)S(1)}, f32[64,512]{1,0:T(8,128)S(1)}, u32[]{:S(2)}, u32[]{:S(2)}) %collective-permute-start) | collective-permute-done | bytes 131104 | tf_op jit(solution)/shard_map/ppermute | solution.py:646
  3.9 2.7 %collective-permute-start.2 = (f32[64,512]{1,0:T(8,128)S(1)}, f32[64,512]{1,0:T(8,128)S(1)}, u32[]{:S(2)}, u32[]{:S(2)}) collective-permute-start(f32[64,512]{1,0:T(8,128)S(1)} %add.6.order_ref.first_ref), channel_id=1, source_target_pairs={{0,20},{4,28},{8,16},{12,24},{16,8},{20,0},{24,12},{28,4},{1,21},{... | collective-permute-start | bytes 393224 | tf_op jit(solution)/shard_map/ppermute | solution.py:662
  6.6 0.0 collective-permute-done.4.second_ref
  6.6 0.8 %collective-permute-start.5 = (f32[64,512]{1,0:T(8,128)S(1)}, f32[64,512]{1,0:T(8,128)S(1)}, u32[]{:S(2)}, u32[]{:S(2)}) collective-permute-start(f32[64,512]{1,0:T(8,128)S(1)} %add.8.first_ref), channel_id=1, source_target_pairs={{0,20},{4,28},{8,16},{12,24},{16,8},{20,0},{24,12},{28,4},{1,21},{... | collective-permute-start | bytes 393224 | tf_op jit(solution)/shard_map/ppermute | solution.py:662
  7.5 1.1 %dense_before.1 = (f32[6,584,128]{2,1,0:T(8,128)S(1)}, f32[64,2048]{1,0:T(8,128)S(1)}) custom-call(f32[64,512]{1,0:T(8,128)S(1)} %add.6.order_ref.first_ref, f32[64,2048]{1,0:T(8,128)} %moment_hbm.1, bf16[1,192,576]{2,1,0:T(8,128)(2,1)S(1)} %copy-done.7, bf16[1,192,192]{2,1,0:T(8,128)(2,1)S(1)} %copy-done.8, bf16[1,192,768]{2,1,0:T(8,128)(2,1)S(1)} %copy-done.5, ...), custom_call_target="tpu_custom_call" | custom-call | flops 8847360000 | bytes 4423680 | tf_op jit(solution)/shard_map/dense_before/pallas_call | solution.py:577
  8.5 0.2 %collective-permute-start.1 = (f32[6,584,128]{2,1,0:T(8,128)S(1)}, f32[6,584,128]{2,1,0:T(8,128)S(1)}, u32[]{:S(2)}, u32[]{:S(2)}) collective-permute-start(f32[6,584,128]{2,1,0:T(8,128)S(1)} %get-tuple-element.31.send_ref), channel_id=1, source_target_pairs={{0,16},{16,0},{1,17},{17,1},{2,18},{18,2},{3,19},{19,3},{4,20},{20... | collective-permute-start | bytes 5382152 | tf_op jit(solution)/shard_map/ppermute | solution.py:664
  8.8 0.4 %collective-permute-done.2.second_ref = f32[64,512]{1,0:T(8,128)S(1)} collective-permute-done((f32[64,512]{1,0:T(8,128)S(1)}, f32[64,512]{1,0:T(8,128)S(1)}, u32[]{:S(2)}, u32[]{:S(2)}) %collective-permute-start.2) | collective-permute-done | bytes 131104 | tf_op jit(solution)/shard_map/ppermute | solution.py:662
  9.2 2.1 %collective-permute-start.3 = (f32[64,512]{1,0:T(8,128)S(1)}, f32[64,512]{1,0:T(8,128)S(1)}, u32[]{:S(2)}, u32[]{:S(2)}) collective-permute-start(f32[64,512]{1,0:T(8,128)S(1)} %add.7.first_ref), channel_id=1, source_target_pairs={{0,24},{4,16},{8,28},{12,20},{16,4},{20,12},{24,0},{28,8},{1,25},{... | collective-permute-start | bytes 393224 | tf_op jit(solution)/shard_map/ppermute | solution.py:668
  11.4 0.0 collective-permute-done.5.second_ref
  11.4 1.2 %collective-permute-start.6 = (f32[64,512]{1,0:T(8,128)S(1)}, f32[64,512]{1,0:T(8,128)S(1)}, u32[]{:S(2)}, u32[]{:S(2)}) collective-permute-start(f32[64,512]{1,0:T(8,128)S(1)} %add.9.first_ref), channel_id=1, source_target_pairs={{0,24},{4,16},{8,28},{12,20},{16,4},{20,12},{24,0},{28,8},{1,25},{... | collective-permute-start | bytes 393224 | tf_op jit(solution)/shard_map/ppermute | solution.py:668
  12.6 0.0 collective-permute-done.1.recv_ref
  12.6 1.8 %dense_after.1 = (f32[192,576]{1,0:T(8,128)}, f32[192,192]{1,0:T(8,128)}, f32[192,768]{1,0:T(8,128)}, f32[192,768]{1,0:T(8,128)}, f32[1728,128]{1,0:T(8,128)}, /*index=5*/f32[1920]{0:T(1024)}, f32[1,960]{1,0:T(1,128)}) custom-call(f32[6,584,128]{2,1,0:T(8,128)S(1)} %collective-permute-done.1.recv_ref, f32[6,584,128]{2,1,0:T(8,128)S(1)} %get-tuple-element.31.send_ref, ...), custom_call_target="tpu_custom_call" | custom-call | flops 8847360000 | bytes 5898240 | tf_op jit(solution)/shard_map/dense_after/pallas_call | solution.py:598
  14.5 0.7 %collective-permute-start.8 = (f32[64,512]{1,0:T(8,128)S(1)}, f32[64,512]{1,0:T(8,128)S(1)}, u32[]{:S(2)}, u32[]{:S(2)}) collective-permute-start(f32[64,512]{1,0:T(8,128)S(1)} %add.10.coeff_ref), channel_id=1, source_target_pairs={{0,16},{16,0},{1,17},{17,1},{2,18},{18,2},{3,19},{19,3},{4,20},{20... | collective-permute-start | bytes 393224 | tf_op jit(solution)/shard_map/ppermute | solution.py:672
  15.1 0.2 %embed_early.1 = (f32[192,512]{1,0:T(8,128)S(1)}, f32[64,512]{1,0:T(8,128)S(1)}) custom-call(bf16[192,192]{1,0:T(8,128)(2,1)S(1)} %get-tuple-element.40.stack_ref, f32[64,2048]{1,0:T(8,128)S(1)} %get-tuple-element.41.moment_ref, f32[192,2048]{1,0:T(8,128)S(1)} %copy-done, f32[64,512]{1,0:T(8,128)S(1)} %add.10.coeff_ref), custom_call_target="tpu_custom_call" | custom-call | flops 37748736 | bytes 786432 | tf_op jit(solution)/shard_map/embed_early/pallas_call | solution.py:236
  15.3 0.5 %collective-permute-done.6.second_ref = f32[64,512]{1,0:T(8,128)S(1)} collective-permute-done((f32[64,512]{1,0:T(8,128)S(1)}, f32[64,512]{1,0:T(8,128)S(1)}, u32[]{:S(2)}, u32[]{:S(2)}) %collective-permute-start.6) | collective-permute-done | bytes 131104 | tf_op jit(solution)/shard_map/ppermute | solution.py:668
  15.9 0.2 collective-permute-start.7
  16.0 0.1 collective-permute-done.8.refs_1_
  16.1 1.2 %embed_pieces.2 = (f32[192,2048]{1,0:T(8,128)}, f32[64,2048]{1,0:T(8,128)}) custom-call(bf16[192,192]{1,0:T(8,128)(2,1)S(1)} %get-tuple-element.40.stack_ref, f32[64,2048]{1,0:T(8,128)S(1)} %get-tuple-element.41.moment_ref, f32[192,2048]{1,0:T(8,128)S(1)} %copy-done, f32[64,512]{1,0:T(8,128)S(1)} %add.11.refs_0_, ...), custom_call_target="tpu_custom_call" | custom-call | flops 75497472 | bytes 1572864 | tf_op jit(solution)/shard_map/embed_pieces/pallas_call | solution.py:286
  17.4 1.0 %embed_pieces.3 = (f32[192,2048]{1,0:T(8,128)}, f32[64,2048]{1,0:T(8,128)}) custom-call(bf16[192,192]{1,0:T(8,128)(2,1)S(1)} %get-tuple-element.40.stack_ref, f32[64,2048]{1,0:T(8,128)S(1)} %get-tuple-element.41.moment_ref, f32[192,2048]{1,0:T(8,128)S(1)} %copy-done, ...), custom_call_target="tpu_custom_call", output_to_operand_aliasing={{0}: (4, {}), {1}: (5, {})} | custom-call | flops 37748736 | bytes 786432 | tf_op jit(solution)/shard_map/embed_pieces/pallas_call | solution.py:286
  (23 shorter events, 0.1 us)
Async XLA Ops:
  0.6 2.3 %copy-start = (f32[192,2048]{1,0:T(8,128)S(1)}, f32[192,2048]{1,0:T(8,128)}, u32[]{:S(2)}) copy-start(f32[192,2048]{1,0:T(8,128)} %old_ref.7) | copy-start | bytes 4718596
  0.7 2.2 %copy-start.2 = (f32[192,64]{0,1:T(8,128)S(1)}, f32[192,64]{0,1:T(8,128)}, u32[]{:S(2)}) copy-start(f32[192,64]{0,1:T(8,128)} %param.24) | copy-start | bytes 147460
  0.7 2.2 %copy-start.1 = (bf16[1,192,2048]{2,1,0:T(8,128)(2,1)S(1)}, bf16[1,192,2048]{2,1,0:T(8,128)(2,1)}, u32[]{:S(2)}) copy-start(bf16[1,192,2048]{2,1,0:T(8,128)(2,1)} %param.22) | copy-start | bytes 2359300
  2.3 5.1 %copy-start.3 = (f32[1,221184]{1,0:T(1,128)S(1)}, f32[1,221184]{1,0:T(1,128)}, u32[]{:S(2)}) copy-start(f32[1,221184]{1,0:T(1,128)} %param.18) | copy-start | bytes 2654212
  2.3 5.1 %copy-start.4 = (f32[1,221184]{1,0:T(1,128)S(1)}, f32[1,221184]{1,0:T(1,128)}, u32[]{:S(2)}) copy-start(f32[1,221184]{1,0:T(1,128)} %param.19) | copy-start | bytes 2654212
  2.3 5.1 %copy-start.5 = (bf16[1,192,768]{2,1,0:T(8,128)(2,1)S(1)}, bf16[1,192,768]{2,1,0:T(8,128)(2,1)}, u32[]{:S(2)}) copy-start(bf16[1,192,768]{2,1,0:T(8,128)(2,1)} %up_ref.3) | copy-start | bytes 884740
  2.3 5.1 %copy-start.6 = (bf16[1,768,192]{1,2,0:T(8,128)(2,1)S(1)}, bf16[1,768,192]{1,2,0:T(8,128)(2,1)}, u32[]{:S(2)}) copy-start(bf16[1,768,192]{1,2,0:T(8,128)(2,1)} %param.16) | copy-start | bytes 884740
  2.3 5.1 %copy-start.7 = (bf16[1,192,576]{2,1,0:T(8,128)(2,1)S(1)}, bf16[1,192,576]{2,1,0:T(8,128)(2,1)}, u32[]{:S(2)}) copy-start(bf16[1,192,576]{2,1,0:T(8,128)(2,1)} %in_ref.3) | copy-start | bytes 663556
  2.3 5.1 %copy-start.8 = (bf16[1,192,192]{2,1,0:T(8,128)(2,1)S(1)}, bf16[1,192,192]{2,1,0:T(8,128)(2,1)}, u32[]{:S(2)}) copy-start(bf16[1,192,192]{2,1,0:T(8,128)(2,1)} %out_ref.3) | copy-start | bytes 221188
  2.3 5.1 %copy-start.9 = (bf16[1,1920]{1,0:T(2,128)(2,1)S(1)}, bf16[1,1920]{1,0:T(2,128)(2,1)}, u32[]{:S(2)}) copy-start(bf16[1,1920]{1,0:T(2,128)(2,1)} %small_ref.3) | copy-start | bytes 11524
  2.3 5.1 %copy-start.10 = (f32[960]{0:T(1024)S(1)}, f32[960]{0:T(1024)}, u32[]{:S(2)}) copy-start(f32[960]{0:T(1024)} %param.20) | copy-start | bytes 11524
  2.4 5.1 %copy-start.11 = (f32[960]{0:T(1024)S(1)}, f32[960]{0:T(1024)}, u32[]{:S(2)}) copy-start(f32[960]{0:T(1024)} %param.21) | copy-start | bytes 11524
  2.4 1.5 %collective-permute-start = (f32[64,512]{1,0:T(8,128)S(1)}, f32[64,512]{1,0:T(8,128)S(1)}, u32[]{:S(2)}, u32[]{:S(2)}) collective-permute-start(f32[64,512]{1,0:T(8,128)S(1)} %first_part.1), channel_id=1, source_target_pairs={{0,16},{16,0},{1,17},{17,1},{2,18},{18,2},{3,19},{19,3},{4,20},{20... | collective-permute-start | bytes 393224 | tf_op jit(solution)/shard_map/ppermute | solution.py:646
  3.3 3.3 %collective-permute-start.4 = (f32[64,512]{1,0:T(8,128)S(1)}, f32[64,512]{1,0:T(8,128)S(1)}, u32[]{:S(2)}, u32[]{:S(2)}) collective-permute-start(f32[64,512]{1,0:T(8,128)S(1)} %get-tuple-element.43), channel_id=1, source_target_pairs={{0,16},{16,0},{1,17},{17,1},{2,18},{18,2},{3,19},{19,3},{4,20},{20... | collective-permute-start | bytes 393224 | tf_op jit(solution)/shard_map/ppermute | solution.py:648
  3.9 5.3 %collective-permute-start.2 = (f32[64,512]{1,0:T(8,128)S(1)}, f32[64,512]{1,0:T(8,128)S(1)}, u32[]{:S(2)}, u32[]{:S(2)}) collective-permute-start(f32[64,512]{1,0:T(8,128)S(1)} %add.6.order_ref.first_ref), channel_id=1, source_target_pairs={{0,20},{4,28},{8,16},{12,24},{16,8},{20,0},{24,12},{28,4},{1,21},{... | collective-permute-start | bytes 393224 | tf_op jit(solution)/shard_map/ppermute | solution.py:662
  6.6 4.8 %collective-permute-start.5 = (f32[64,512]{1,0:T(8,128)S(1)}, f32[64,512]{1,0:T(8,128)S(1)}, u32[]{:S(2)}, u32[]{:S(2)}) collective-permute-start(f32[64,512]{1,0:T(8,128)S(1)} %add.8.first_ref), channel_id=1, source_target_pairs={{0,20},{4,28},{8,16},{12,24},{16,8},{20,0},{24,12},{28,4},{1,21},{... | collective-permute-start | bytes 393224 | tf_op jit(solution)/shard_map/ppermute | solution.py:662
  8.5 4.1 %collective-permute-start.1 = (f32[6,584,128]{2,1,0:T(8,128)S(1)}, f32[6,584,128]{2,1,0:T(8,128)S(1)}, u32[]{:S(2)}, u32[]{:S(2)}) collective-permute-start(f32[6,584,128]{2,1,0:T(8,128)S(1)} %get-tuple-element.31.send_ref), channel_id=1, source_target_pairs={{0,16},{16,0},{1,17},{17,1},{2,18},{18,2},{3,19},{19,3},{4,20},{20... | collective-permute-start | bytes 5382152 | tf_op jit(solution)/shard_map/ppermute | solution.py:664
  9.2 5.2 %collective-permute-start.3 = (f32[64,512]{1,0:T(8,128)S(1)}, f32[64,512]{1,0:T(8,128)S(1)}, u32[]{:S(2)}, u32[]{:S(2)}) collective-permute-start(f32[64,512]{1,0:T(8,128)S(1)} %add.7.first_ref), channel_id=1, source_target_pairs={{0,24},{4,16},{8,28},{12,20},{16,4},{20,12},{24,0},{28,8},{1,25},{... | collective-permute-start | bytes 393224 | tf_op jit(solution)/shard_map/ppermute | solution.py:668
  11.4 4.5 %collective-permute-start.6 = (f32[64,512]{1,0:T(8,128)S(1)}, f32[64,512]{1,0:T(8,128)S(1)}, u32[]{:S(2)}, u32[]{:S(2)}) collective-permute-start(f32[64,512]{1,0:T(8,128)S(1)} %add.9.first_ref), channel_id=1, source_target_pairs={{0,24},{4,16},{8,28},{12,20},{16,4},{20,12},{24,0},{28,8},{1,25},{... | collective-permute-start | bytes 393224 | tf_op jit(solution)/shard_map/ppermute | solution.py:668
  14.5 1.6 %collective-permute-start.8 = (f32[64,512]{1,0:T(8,128)S(1)}, f32[64,512]{1,0:T(8,128)S(1)}, u32[]{:S(2)}, u32[]{:S(2)}) collective-permute-start(f32[64,512]{1,0:T(8,128)S(1)} %add.10.coeff_ref), channel_id=1, source_target_pairs={{0,16},{16,0},{1,17},{17,1},{2,18},{18,2},{3,19},{19,3},{4,20},{20... | collective-permute-start | bytes 393224 | tf_op jit(solution)/shard_map/ppermute | solution.py:672
  15.9 1.5 %collective-permute-start.7 = (f32[64,512]{1,0:T(8,128)S(1)}, f32[64,512]{1,0:T(8,128)S(1)}, u32[]{:S(2)}, u32[]{:S(2)}) collective-permute-start(f32[64,512]{1,0:T(8,128)S(1)} %add.11.refs_0_), channel_id=1, source_target_pairs={{0,16},{16,0},{1,17},{17,1},{2,18},{18,2},{3,19},{19,3},{4,20},{20... | collective-permute-start | bytes 393224 | tf_op jit(solution)/shard_map/ppermute | solution.py:675

commit v7 on v6

--- a/solution.py
+++ b/solution.py
@@ -98,7 +98,6 @@
 
 
 CHUNKS = 2
-ROW_CUTS = 2
 WHOLE = pl.BlockSpec(memory_space=pltpu.VMEM)
 ANY = pl.BlockSpec(memory_space=pl.ANY)
 
@@ -126,22 +125,20 @@
     return first[:rank] + first[rank:] + jnp.dot(high, diff_low, preferred_element_type=f32)
 
 
-def first_kernel(basis_hbm, local_hbm, old_hbm, out_ref, basis_ref, local_ref, old_ref, sems):
-    block = out_ref.shape[1]
-    start = side_start(True, CHUNKS * block)
-    there = pl.ds(pl.multiple_of(start, block), block)
-    rows = old_hbm.shape[0] // ROW_CUTS
-    copies = [pltpu.make_async_copy(basis_hbm, basis_ref, sems.at[0])]
-    for k in range(ROW_CUTS):
-        cut = pl.ds(k * rows, rows)
-        for source, target in ((old_hbm, old_ref), (local_hbm, local_ref)):
-            at = sems.at[len(copies)]
-            copies.append(pltpu.make_async_copy(source.at[cut, there], target.at[cut, :], at))
+def first_kernel(basis_hbm, local_hbm, old_hbm, out_ref, *refs):
+    *held, sems = refs
+    columns = out_ref.shape[1]
+    there = pl.ds(pl.multiple_of(side_start(True, CHUNKS * columns), columns), columns)
+    sources = (basis_hbm, local_hbm.at[:, there], old_hbm.at[:, there])
+    copies = [
+        pltpu.make_async_copy(source, target, sems.at[k])
+        for k, (source, target) in enumerate(zip(sources, held))
+    ]
     for copy in copies:
         copy.start()
     for copy in copies:
         copy.wait()
-    out_ref[...] = product(basis_ref[...], local_ref[...], old_ref[...])
+    out_ref[...] = product(*(ref[...] for ref in held))
 
 
 def first_part(basis_t, local, old):
@@ -156,7 +153,7 @@
             pltpu.VMEM((rank, depth), f32),
             pltpu.VMEM((depth, block), bf16),
             pltpu.VMEM((depth, block), f32),
-            pltpu.SemaphoreType.DMA((1 + 2 * ROW_CUTS,)),
+            pltpu.SemaphoreType.DMA((3,)),
         ],
         compiler_params=pltpu.CompilerParams(vmem_limit_bytes=4 * 2**20),
         cost_estimate=pl.CostEstimate(
@@ -361,12 +358,10 @@
 
 
 def before_kernel(
-    order_ref, moment_hbm, in_ref, out_ref, up_ref, down_ref, old_ref, mom_ref, small_ref,
-    small_old_ref, small_mom_ref, send_ref, moment_ref, wide_ref, sem,
+    order_ref, in_ref, out_ref, up_ref, down_ref, old_ref, mom_ref, small_ref, small_old_ref,
+    small_mom_ref, send_ref, wide_ref,
 ):
     del order_ref
-    copy = pltpu.make_async_copy(moment_hbm, moment_ref, sem)
-    copy.start()
     group = lax.axis_index("group")
     rows = up_ref.shape[1]
     mid = rows // 2
@@ -442,14 +437,12 @@
         values = small_ref[...].astype(f32)
         put_small(values[:, :small], values[:, small:])
 
-    copy.wait()
-
 
 def after_kernel(
     recv_ref, send_ref, in_ref, out_ref, up_ref, down_ref, old_ref, mom_ref, small_ref,
-    small_old_ref, small_mom_ref, *refs,
+    small_old_ref, small_mom_ref, moment_hbm, *refs,
 ):
-    targets, sources, (sum_ref, wide_ref, sems) = refs[:7], refs[7:14], refs[14:]
+    targets, moment_ref, sources, (sum_ref, wide_ref, sems) = refs[:7], refs[7], refs[8:15], refs[15:]
     (
         in_next_ref, out_next_ref, up_next_ref, down_next_ref, moved_ref, small_next_ref,
         small_moved_ref,
@@ -458,6 +451,8 @@
         pltpu.make_async_copy(source, target, sems.at[k])
         for k, (source, target) in enumerate(zip(sources, targets))
     ]
+    copies.append(pltpu.make_async_copy(moment_hbm, moment_ref, sems.at[7]))
+    copies[7].start()
 
     def go(*numbers):
         for k in numbers:
@@ -572,46 +567,43 @@
             copy.wait()
 
 
-def dense_before(order, moment, operands):
+def dense_before(order, operands):
     _, rows, width = operands[2].shape
     return pl.pallas_call(
         before_kernel,
-        in_specs=[ANY] * 2 + [WHOLE] * 9,
-        out_specs=[WHOLE] * 2,
-        out_shape=[
-            jax.ShapeDtypeStruct((width // LANES, 3 * rows + 8, LANES), f32),
-            jax.ShapeDtypeStruct(moment.shape, f32),
-        ],
-        scratch_shapes=[pltpu.VMEM((2, width, LANES), f32), pltpu.SemaphoreType.DMA],
+        in_specs=[ANY] + [WHOLE] * 9,
+        out_specs=WHOLE,
+        out_shape=jax.ShapeDtypeStruct((width // LANES, 3 * rows + 8, LANES), f32),
+        scratch_shapes=[pltpu.VMEM((2, width, LANES), f32)],
         compiler_params=pltpu.CompilerParams(vmem_limit_bytes=4 * 2**20),
         cost_estimate=pl.CostEstimate(
             flops=60000 * rows * width, bytes_accessed=30 * rows * width, transcendentals=0
         ),
         name="dense_before",
-    )(order, *in_hbm([moment]), *operands)
-
-
-def dense_after(received, sent, operands):
+    )(order, *operands)
+
+
+def dense_after(received, sent, operands, moment):
     _, rows, width = operands[2].shape
     outs = [matrix.shape[1:] for matrix in operands[:4]]
     outs += [operands[4].shape, operands[6].shape[1:], operands[7].shape]
     return pl.pallas_call(
         after_kernel,
-        in_specs=[WHOLE] * 11,
-        out_specs=[ANY] * 7,
-        out_shape=[jax.ShapeDtypeStruct(shape, f32) for shape in outs],
+        in_specs=[WHOLE] * 11 + [ANY],
+        out_specs=[ANY] * 7 + [WHOLE],
+        out_shape=[jax.ShapeDtypeStruct(shape, f32) for shape in (*outs, moment.shape)],
         scratch_shapes=[pltpu.VMEM(shape, f32) for shape in outs]
         + [
             pltpu.VMEM((width // LANES, rows, LANES), f32),
             pltpu.VMEM((2, width, LANES), f32),
-            pltpu.SemaphoreType.DMA((7,)),
+            pltpu.SemaphoreType.DMA((8,)),
         ],
         compiler_params=pltpu.CompilerParams(vmem_limit_bytes=8 * 2**20),
         cost_estimate=pl.CostEstimate(
             flops=60000 * rows * width, bytes_accessed=40 * rows * width, transcendentals=0
         ),
         name="dense_after",
-    )(received, sent, *operands)
+    )(received, sent, *operands, *in_hbm([moment]))
 
 
 def paired(
@@ -660,13 +652,13 @@
     )
     totals = [add(*pair, flops=10**4) for pair in zip(mine, theirs)]
     moving = [lax.ppermute(total, axes, first) for total in totals]
-    sent, moment = dense_before(totals[0], coeff_momentum, operands)
+    sent = dense_before(totals[0], operands)
     received = lax.ppermute(sent, "group", swap)
     totals = [
         add(*pair, flops=flops) for *pair, flops in zip(totals, moving, (10**4, 2 * 10**10))
     ]
     moving = [lax.ppermute(total, axes, second) for total in totals]
-    dense = list(dense_after(received, sent, operands))
+    *dense, moment = dense_after(received, sent, operands, coeff_momentum)
     moving[0], dense[-1] = lax.optimization_barrier((moving[0], dense[-1]))
     own = [add(totals[0], moving[0], scale=0.5)]
     rest = [lax.ppermute(own[0], "group", swap)]

time: 18.6 us -> 18.5 us (level)
  Pallas kernels: 7.4 us -> 6.7 us
  waiting for transfers between devices: 1.39 us -> 1.93 us
    pallas_call x2, Pallas kernels: 2.85 us -> 2.21 us  [the longest x1 1.81 us: dense_after(): pl.pallas_call(after_kernel, in_specs=[WHOLE] * 11 + [ANY], out_specs=[AN...]
    ppermute x2, waiting for transfers between devices: 0.44 us -> 0.99 us  [paired(): moving = [lax.ppermute(total, axes, first) for total in totals]]
  transfers between devices with their start and end apart: 9 -> 9, of which waited for: 4 -> 4; matrix products, arithmetic and copies ran while one was open for 0% -> 0% of each run, Pallas kernels for 26% -> 23%
where the time goes in v7:
time: 18.5 us; the launch traced here: 18.3 us
  starting transfers between devices  8.74 us (47%)
  Pallas kernels  6.7 us (36%)
  waiting for transfers between devices  1.93 us (10%)
  between operations  0.87 us (5%)
    ppermute x2, starting transfers between devices, paired(): moving = [lax.ppermute(total, axes, first) for total in totals]  3.49 us
    ppermute x2, starting transfers between devices, paired(): moving = [lax.ppermute(total, axes, second) for total in totals]  3.36 us
    pallas_call x2, Pallas kernels, embed_pieces(): pl.pallas_call(functools.partial(embed_kernel, pieces, ready), in_specs=[...  2.24 us
    pallas_call x1, Pallas kernels, dense_after(): pl.pallas_call(after_kernel, in_specs=[WHOLE] * 11 + [ANY], out_specs=[AN...  1.81 us
    pallas_call x1, Pallas kernels, first_part(): pl.pallas_call(first_kernel, in_specs=[ANY] * 3, out_specs=WHOLE, out_sha...  1.53 us
    ppermute x2, waiting for transfers between devices, paired(): moving = [lax.ppermute(total, axes, first) for total in totals]  0.99 us
    ppermute x1, starting transfers between devices, paired(): rest = [lax.ppermute(own[0], 'group', swap)]  0.66 us
    ppermute x1, starting transfers between devices, paired(): theirs = [lax.ppermute(first_part(*embed), 'group', swap)]  0.52 us
  transfers between devices with their start and end apart: 9, of which 4 were waited for; matrix products, arithmetic and copies ran while one was open for 0% of the time, Pallas kernels for 23%

profile of v7, /device:TPU:0, one launch (start us, length us, event | category | flops | bytes accessed | tf_op | source)
XLA Modules:
  0.0 18.3 jit_solution(10959361428053493108)
XLA Ops:
  0.7 1.5 %first_part.1 = f32[64,512]{1,0:T(8,128)S(1)} custom-call(f32[64,192]{1,0:T(8,128)} %bitcast.12, bf16[192,2048]{1,0:T(8,128)(2,1)} %bitcast.10, f32[192,2048]{1,0:T(8,128)} %old_ref.7), custom_call_target="tpu_custom_call" | custom-call | flops 37748736 | bytes 589824 | tf_op jit(solution)/shard_map/first_part/pallas_call | solution.py:147
  2.2 0.0 copy-start.3
  2.2 0.0 copy-start.4
  2.2 0.0 copy-start.5
  2.2 0.0 copy-start.6
  2.3 0.0 copy-start.7
  2.3 0.0 copy-start.8
  2.3 0.0 copy-start.9
  2.3 0.0 copy-start.10
  2.3 0.0 copy-start.11
  2.3 0.5 %collective-permute-start = (f32[64,512]{1,0:T(8,128)S(1)}, f32[64,512]{1,0:T(8,128)S(1)}, u32[]{:S(2)}, u32[]{:S(2)}) collective-permute-start(f32[64,512]{1,0:T(8,128)S(1)} %first_part.1), channel_id=1, source_target_pairs={{0,16},{16,0},{1,17},{17,1},{2,18},{18,2},{3,19},{19,3},{4,20},{20... | collective-permute-start | bytes 393224 | tf_op jit(solution)/shard_map/ppermute | solution.py:638
  2.8 0.4 %other_parts.1 = (f32[64,512]{1,0:T(8,128)S(1)}, f32[64,512]{1,0:T(8,128)S(1)}, f32[64,512]{1,0:T(8,128)S(1)}, bf16[192,192]{1,0:T(8,128)(2,1)S(1)}) custom-call(f32[64,192]{1,0:T(8,128)S(1)} %bitcast.13, bf16[192,2048]{1,0:T(8,128)(2,1)S(1)} %bitcast.11, f32[192,2048]{1,0:T(8,128)S(1)} %copy-done), custom_call_target="tpu_custom_call" | custom-call | flops 10000000000 | bytes 1769472 | tf_op jit(solution)/shard_map/other_parts/pallas_call | solution.py:182
  3.3 0.2 %collective-permute-start.4 = (f32[64,512]{1,0:T(8,128)S(1)}, f32[64,512]{1,0:T(8,128)S(1)}, u32[]{:S(2)}, u32[]{:S(2)}) collective-permute-start(f32[64,512]{1,0:T(8,128)S(1)} %get-tuple-element.41), channel_id=1, source_target_pairs={{0,16},{16,0},{1,17},{17,1},{2,18},{18,2},{3,19},{19,3},{4,20},{20... | collective-permute-start | bytes 393224 | tf_op jit(solution)/shard_map/ppermute | solution.py:640
  3.4 0.4 %collective-permute-done.second_ref = f32[64,512]{1,0:T(8,128)S(1)} collective-permute-done((f32[64,512]{1,0:T(8,128)S(1)}, f32[64,512]{1,0:T(8,128)S(1)}, u32[]{:S(2)}, u32[]{:S(2)}) %collective-permute-start) | collective-permute-done | bytes 131104 | tf_op jit(solution)/shard_map/ppermute | solution.py:638
  3.8 2.7 %collective-permute-start.2 = (f32[64,512]{1,0:T(8,128)S(1)}, f32[64,512]{1,0:T(8,128)S(1)}, u32[]{:S(2)}, u32[]{:S(2)}) collective-permute-start(f32[64,512]{1,0:T(8,128)S(1)} %add.6.order_ref.first_ref), channel_id=1, source_target_pairs={{0,20},{4,28},{8,16},{12,24},{16,8},{20,0},{24,12},{28,4},{1,21},{... | collective-permute-start | bytes 393224 | tf_op jit(solution)/shard_map/ppermute | solution.py:654
  6.5 0.0 collective-permute-done.4.second_ref
  6.5 0.8 %collective-permute-start.5 = (f32[64,512]{1,0:T(8,128)S(1)}, f32[64,512]{1,0:T(8,128)S(1)}, u32[]{:S(2)}, u32[]{:S(2)}) collective-permute-start(f32[64,512]{1,0:T(8,128)S(1)} %add.8.first_ref), channel_id=1, source_target_pairs={{0,20},{4,28},{8,16},{12,24},{16,8},{20,0},{24,12},{28,4},{1,21},{... | collective-permute-start | bytes 393224 | tf_op jit(solution)/shard_map/ppermute | solution.py:654
  7.4 0.4 %dense_before.1.send_ref = f32[6,584,128]{2,1,0:T(8,128)S(1)} custom-call(f32[64,512]{1,0:T(8,128)S(1)} %add.6.order_ref.first_ref, bf16[1,192,576]{2,1,0:T(8,128)(2,1)S(1)} %copy-done.7, bf16[1,192,192]{2,1,0:T(8,128)(2,1)S(1)} %copy-done.8, bf16[1,192,768]{2,1,0:T(8,128)(2,1)S(1)} %copy-done.5, bf16[1,192,768]{2,1,0:T(8,128)(2,1)S(1)} %bitcast.18, ...), custom_call_target="tpu_custom_call" | custom-call | flops 8847360000 | bytes 4423680 | tf_op jit(solution)/shard_map/dense_before/pallas_call | solution.py:572
  7.8 0.4 %collective-permute-start.1 = (f32[6,584,128]{2,1,0:T(8,128)S(1)}, f32[6,584,128]{2,1,0:T(8,128)S(1)}, u32[]{:S(2)}, u32[]{:S(2)}) collective-permute-start(f32[6,584,128]{2,1,0:T(8,128)S(1)} %dense_before.1.send_ref), channel_id=1, source_target_pairs={{0,16},{16,0},{1,17},{17,1},{2,18},{18,2},{3,19},{19,3},{4,20},{20... | collective-permute-start | bytes 5382152 | tf_op jit(solution)/shard_map/ppermute | solution.py:656
  8.2 1.0 %collective-permute-done.2.second_ref = f32[64,512]{1,0:T(8,128)S(1)} collective-permute-done((f32[64,512]{1,0:T(8,128)S(1)}, f32[64,512]{1,0:T(8,128)S(1)}, u32[]{:S(2)}, u32[]{:S(2)}) %collective-permute-start.2) | collective-permute-done | bytes 131104 | tf_op jit(solution)/shard_map/ppermute | solution.py:654
  9.2 2.1 %collective-permute-start.3 = (f32[64,512]{1,0:T(8,128)S(1)}, f32[64,512]{1,0:T(8,128)S(1)}, u32[]{:S(2)}, u32[]{:S(2)}) collective-permute-start(f32[64,512]{1,0:T(8,128)S(1)} %add.7.first_ref), channel_id=1, source_target_pairs={{0,24},{4,16},{8,28},{12,20},{16,4},{20,12},{24,0},{28,8},{1,25},{... | collective-permute-start | bytes 393224 | tf_op jit(solution)/shard_map/ppermute | solution.py:660
  11.3 0.0 collective-permute-done.5.second_ref
  11.3 1.2 %collective-permute-start.6 = (f32[64,512]{1,0:T(8,128)S(1)}, f32[64,512]{1,0:T(8,128)S(1)}, u32[]{:S(2)}, u32[]{:S(2)}) collective-permute-start(f32[64,512]{1,0:T(8,128)S(1)} %add.9.first_ref), channel_id=1, source_target_pairs={{0,24},{4,16},{8,28},{12,20},{16,4},{20,12},{24,0},{28,8},{1,25},{... | collective-permute-start | bytes 393224 | tf_op jit(solution)/shard_map/ppermute | solution.py:660
  12.6 0.0 collective-permute-done.1.recv_ref
  12.6 1.8 %dense_after.1 = (f32[192,576]{1,0:T(8,128)}, f32[192,192]{1,0:T(8,128)}, f32[192,768]{1,0:T(8,128)}, f32[192,768]{1,0:T(8,128)}, f32[1728,128]{1,0:T(8,128)}, /...) custom-call(f32[6,584,128]{2,1,0:T(8,128)S(1)} %collective-permute-done.1.recv_ref, ...), custom_call_target="tpu_custom_call" | custom-call | flops 8847360000 | bytes 5898240 | tf_op jit(solution)/shard_map/dense_after/pallas_call | solution.py:590
  14.4 0.7 %collective-permute-start.8 = (f32[64,512]{1,0:T(8,128)S(1)}, f32[64,512]{1,0:T(8,128)S(1)}, u32[]{:S(2)}, u32[]{:S(2)}) collective-permute-start(f32[64,512]{1,0:T(8,128)S(1)} %add.10.coeff_ref), channel_id=1, source_target_pairs={{0,16},{16,0},{1,17},{17,1},{2,18},{18,2},{3,19},{19,3},{4,20},{20... | collective-permute-start | bytes 393224 | tf_op jit(solution)/shard_map/ppermute | solution.py:664
  15.1 0.2 %embed_early.1 = (f32[192,512]{1,0:T(8,128)S(1)}, f32[64,512]{1,0:T(8,128)S(1)}) custom-call(bf16[192,192]{1,0:T(8,128)(2,1)S(1)} %get-tuple-element.38.stack_ref, f32[64,2048]{1,0:T(8,128)S(1)} %get-tuple-element.39.moment_ref, f32[192,2048]{1,0:T(8,128)S(1)} %copy-done, f32[64,512]{1,0:T(8,128)S(1)} %add.10.coeff_ref), custom_call_target="tpu_custom_call" | custom-call | flops 37748736 | bytes 786432 | tf_op jit(solution)/shard_map/embed_early/pallas_call | solution.py:233
  15.3 0.5 %collective-permute-done.6.second_ref = f32[64,512]{1,0:T(8,128)S(1)} collective-permute-done((f32[64,512]{1,0:T(8,128)S(1)}, f32[64,512]{1,0:T(8,128)S(1)}, u32[]{:S(2)}, u32[]{:S(2)}) %collective-permute-start.6) | collective-permute-done | bytes 131104 | tf_op jit(solution)/shard_map/ppermute | solution.py:660
  15.8 0.2 collective-permute-start.7
  16.0 0.1 collective-permute-done.8.refs_1_
  16.1 1.2 %embed_pieces.2 = (f32[192,2048]{1,0:T(8,128)}, f32[64,2048]{1,0:T(8,128)}) custom-call(bf16[192,192]{1,0:T(8,128)(2,1)S(1)} %get-tuple-element.38.stack_ref, f32[64,2048]{1,0:T(8,128)S(1)} %get-tuple-element.39.moment_ref, f32[192,2048]{1,0:T(8,128)S(1)} %copy-done, f32[64,512]{1,0:T(8,128)S(1)} %add.11.refs_0_, ...), custom_call_target="tpu_custom_call" | custom-call | flops 75497472 | bytes 1572864 | tf_op jit(solution)/shard_map/embed_pieces/pallas_call | solution.py:283
  17.3 1.0 %embed_pieces.3 = (f32[192,2048]{1,0:T(8,128)}, f32[64,2048]{1,0:T(8,128)}) custom-call(bf16[192,192]{1,0:T(8,128)(2,1)S(1)} %get-tuple-element.38.stack_ref, f32[64,2048]{1,0:T(8,128)S(1)} %get-tuple-element.39.moment_ref, f32[192,2048]{1,0:T(8,128)S(1)} %copy-done, ...), custom_call_target="tpu_custom_call", output_to_operand_aliasing={{0}: (4, {}), {1}: (5, {})} | custom-call | flops 37748736 | bytes 786432 | tf_op jit(solution)/shard_map/embed_pieces/pallas_call | solution.py:283
  (23 shorter events, 0.1 us)
Async XLA Ops:
  0.6 2.2 %copy-start = (f32[192,2048]{1,0:T(8,128)S(1)}, f32[192,2048]{1,0:T(8,128)}, u32[]{:S(2)}) copy-start(f32[192,2048]{1,0:T(8,128)} %old_ref.7) | copy-start | bytes 4718596
  0.7 2.2 %copy-start.2 = (f32[192,64]{0,1:T(8,128)S(1)}, f32[192,64]{0,1:T(8,128)}, u32[]{:S(2)}) copy-start(f32[192,64]{0,1:T(8,128)} %param.24) | copy-start | bytes 147460
  0.7 2.2 %copy-start.1 = (bf16[1,192,2048]{2,1,0:T(8,128)(2,1)S(1)}, bf16[1,192,2048]{2,1,0:T(8,128)(2,1)}, u32[]{:S(2)}) copy-start(bf16[1,192,2048]{2,1,0:T(8,128)(2,1)} %param.22) | copy-start | bytes 2359300
  2.2 5.1 %copy-start.3 = (f32[1,221184]{1,0:T(1,128)S(1)}, f32[1,221184]{1,0:T(1,128)}, u32[]{:S(2)}) copy-start(f32[1,221184]{1,0:T(1,128)} %param.18) | copy-start | bytes 2654212
  2.2 5.1 %copy-start.4 = (f32[1,221184]{1,0:T(1,128)S(1)}, f32[1,221184]{1,0:T(1,128)}, u32[]{:S(2)}) copy-start(f32[1,221184]{1,0:T(1,128)} %param.19) | copy-start | bytes 2654212
  2.2 5.1 %copy-start.5 = (bf16[1,192,768]{2,1,0:T(8,128)(2,1)S(1)}, bf16[1,192,768]{2,1,0:T(8,128)(2,1)}, u32[]{:S(2)}) copy-start(bf16[1,192,768]{2,1,0:T(8,128)(2,1)} %up_ref.3) | copy-start | bytes 884740
  2.2 5.1 %copy-start.6 = (bf16[1,768,192]{1,2,0:T(8,128)(2,1)S(1)}, bf16[1,768,192]{1,2,0:T(8,128)(2,1)}, u32[]{:S(2)}) copy-start(bf16[1,768,192]{1,2,0:T(8,128)(2,1)} %param.16) | copy-start | bytes 884740
  2.3 5.1 %copy-start.7 = (bf16[1,192,576]{2,1,0:T(8,128)(2,1)S(1)}, bf16[1,192,576]{2,1,0:T(8,128)(2,1)}, u32[]{:S(2)}) copy-start(bf16[1,192,576]{2,1,0:T(8,128)(2,1)} %in_ref.3) | copy-start | bytes 663556
  2.3 5.1 %copy-start.8 = (bf16[1,192,192]{2,1,0:T(8,128)(2,1)S(1)}, bf16[1,192,192]{2,1,0:T(8,128)(2,1)}, u32[]{:S(2)}) copy-start(bf16[1,192,192]{2,1,0:T(8,128)(2,1)} %out_ref.3) | copy-start | bytes 221188
  2.3 5.1 %copy-start.9 = (bf16[1,1920]{1,0:T(2,128)(2,1)S(1)}, bf16[1,1920]{1,0:T(2,128)(2,1)}, u32[]{:S(2)}) copy-start(bf16[1,1920]{1,0:T(2,128)(2,1)} %small_ref.3) | copy-start | bytes 11524
  2.3 5.1 %copy-start.10 = (f32[960]{0:T(1024)S(1)}, f32[960]{0:T(1024)}, u32[]{:S(2)}) copy-start(f32[960]{0:T(1024)} %param.20) | copy-start | bytes 11524
  2.3 5.1 %copy-start.11 = (f32[960]{0:T(1024)S(1)}, f32[960]{0:T(1024)}, u32[]{:S(2)}) copy-start(f32[960]{0:T(1024)} %param.21) | copy-start | bytes 11524
  2.3 1.5 %collective-permute-start = (f32[64,512]{1,0:T(8,128)S(1)}, f32[64,512]{1,0:T(8,128)S(1)}, u32[]{:S(2)}, u32[]{:S(2)}) collective-permute-start(f32[64,512]{1,0:T(8,128)S(1)} %first_part.1), channel_id=1, source_target_pairs={{0,16},{16,0},{1,17},{17,1},{2,18},{18,2},{3,19},{19,3},{4,20},{20... | collective-permute-start | bytes 393224 | tf_op jit(solution)/shard_map/ppermute | solution.py:638
  3.3 3.3 %collective-permute-start.4 = (f32[64,512]{1,0:T(8,128)S(1)}, f32[64,512]{1,0:T(8,128)S(1)}, u32[]{:S(2)}, u32[]{:S(2)}) collective-permute-start(f32[64,512]{1,0:T(8,128)S(1)} %get-tuple-element.41), channel_id=1, source_target_pairs={{0,16},{16,0},{1,17},{17,1},{2,18},{18,2},{3,19},{19,3},{4,20},{20... | collective-permute-start | bytes 393224 | tf_op jit(solution)/shard_map/ppermute | solution.py:640
  3.8 5.3 %collective-permute-start.2 = (f32[64,512]{1,0:T(8,128)S(1)}, f32[64,512]{1,0:T(8,128)S(1)}, u32[]{:S(2)}, u32[]{:S(2)}) collective-permute-start(f32[64,512]{1,0:T(8,128)S(1)} %add.6.order_ref.first_ref), channel_id=1, source_target_pairs={{0,20},{4,28},{8,16},{12,24},{16,8},{20,0},{24,12},{28,4},{1,21},{... | collective-permute-start | bytes 393224 | tf_op jit(solution)/shard_map/ppermute | solution.py:654
  6.5 4.8 %collective-permute-start.5 = (f32[64,512]{1,0:T(8,128)S(1)}, f32[64,512]{1,0:T(8,128)S(1)}, u32[]{:S(2)}, u32[]{:S(2)}) collective-permute-start(f32[64,512]{1,0:T(8,128)S(1)} %add.8.first_ref), channel_id=1, source_target_pairs={{0,20},{4,28},{8,16},{12,24},{16,8},{20,0},{24,12},{28,4},{1,21},{... | collective-permute-start | bytes 393224 | tf_op jit(solution)/shard_map/ppermute | solution.py:654
  7.8 4.7 %collective-permute-start.1 = (f32[6,584,128]{2,1,0:T(8,128)S(1)}, f32[6,584,128]{2,1,0:T(8,128)S(1)}, u32[]{:S(2)}, u32[]{:S(2)}) collective-permute-start(f32[6,584,128]{2,1,0:T(8,128)S(1)} %dense_before.1.send_ref), channel_id=1, source_target_pairs={{0,16},{16,0},{1,17},{17,1},{2,18},{18,2},{3,19},{19,3},{4,20},{20... | collective-permute-start | bytes 5382152 | tf_op jit(solution)/shard_map/ppermute | solution.py:656
  9.2 5.2 %collective-permute-start.3 = (f32[64,512]{1,0:T(8,128)S(1)}, f32[64,512]{1,0:T(8,128)S(1)}, u32[]{:S(2)}, u32[]{:S(2)}) collective-permute-start(f32[64,512]{1,0:T(8,128)S(1)} %add.7.first_ref), channel_id=1, source_target_pairs={{0,24},{4,16},{8,28},{12,20},{16,4},{20,12},{24,0},{28,8},{1,25},{... | collective-permute-start | bytes 393224 | tf_op jit(solution)/shard_map/ppermute | solution.py:660
  11.3 4.5 %collective-permute-start.6 = (f32[64,512]{1,0:T(8,128)S(1)}, f32[64,512]{1,0:T(8,128)S(1)}, u32[]{:S(2)}, u32[]{:S(2)}) collective-permute-start(f32[64,512]{1,0:T(8,128)S(1)} %add.9.first_ref), channel_id=1, source_target_pairs={{0,24},{4,16},{8,28},{12,20},{16,4},{20,12},{24,0},{28,8},{1,25},{... | collective-permute-start | bytes 393224 | tf_op jit(solution)/shard_map/ppermute | solution.py:660
  14.4 1.6 %collective-permute-start.8 = (f32[64,512]{1,0:T(8,128)S(1)}, f32[64,512]{1,0:T(8,128)S(1)}, u32[]{:S(2)}, u32[]{:S(2)}) collective-permute-start(f32[64,512]{1,0:T(8,128)S(1)} %add.10.coeff_ref), channel_id=1, source_target_pairs={{0,16},{16,0},{1,17},{17,1},{2,18},{18,2},{3,19},{19,3},{4,20},{20... | collective-permute-start | bytes 393224 | tf_op jit(solution)/shard_map/ppermute | solution.py:664
  15.8 1.5 %collective-permute-start.7 = (f32[64,512]{1,0:T(8,128)S(1)}, f32[64,512]{1,0:T(8,128)S(1)}, u32[]{:S(2)}, u32[]{:S(2)}) collective-permute-start(f32[64,512]{1,0:T(8,128)S(1)} %add.11.refs_0_), channel_id=1, source_target_pairs={{0,16},{16,0},{1,17},{17,1},{2,18},{18,2},{3,19},{19,3},{4,20},{20... | collective-permute-start | bytes 393224 | tf_op jit(solution)/shard_map/ppermute | solution.py:667

commit v8 on v7

--- a/solution.py
+++ b/solution.py
@@ -115,18 +115,28 @@
     return (1 - side if other else side) * columns
 
 
-def product(basis, local, old):
-    rank = basis.shape[0]
-    high, low = split(basis)
-    diff_high, diff_low = split(old - local.astype(f32))
-    first = jnp.dot(
-        jnp.concatenate([high, low], axis=0), diff_high, preferred_element_type=f32
-    )
-    return first[:rank] + first[rank:] + jnp.dot(high, diff_low, preferred_element_type=f32)
+def both_parts(basis):
+    return jnp.concatenate(split(basis), axis=0)
+
+
+def doubled_product(both, local, old):
+    rank = both.shape[0] // 2
+    diff_high, diff_low = split(2 * old - local.astype(f32))
+    first = jnp.dot(both, diff_high, preferred_element_type=f32)
+    second = jnp.dot(both[:rank], diff_low, preferred_element_type=f32)
+    return first[:rank] + first[rank:] + second
+
+
+def local_product(both, local):
+    rank = both.shape[0] // 2
+    first = jnp.dot(both, local, preferred_element_type=f32)
+    return -(first[:rank] + first[rank:])
 
 
 def first_kernel(basis_hbm, local_hbm, old_hbm, out_ref, *refs):
     *held, sems = refs
+    basis_ref, local_ref, old_ref = held
+    group = lax.axis_index("group")
     columns = out_ref.shape[1]
     there = pl.ds(pl.multiple_of(side_start(True, CHUNKS * columns), columns), columns)
     sources = (basis_hbm, local_hbm.at[:, there], old_hbm.at[:, there])
@@ -134,11 +144,22 @@
         pltpu.make_async_copy(source, target, sems.at[k])
         for k, (source, target) in enumerate(zip(sources, held))
     ]
-    for copy in copies:
-        copy.start()
-    for copy in copies:
-        copy.wait()
-    out_ref[...] = product(*(ref[...] for ref in held))
+
+    @pl.when(group == 0)
+    def _():
+        for copy in copies[:2]:
+            copy.start()
+        for copy in copies[:2]:
+            copy.wait()
+        out_ref[...] = local_product(both_parts(basis_ref[...]), local_ref[...])
+
+    @pl.when(group == 1)
+    def _():
+        for copy in copies:
+            copy.start()
+        for copy in copies:
+            copy.wait()
+        out_ref[...] = doubled_product(both_parts(basis_ref[...]), local_ref[...], old_ref[...])
 
 
 def first_part(basis_t, local, old):
@@ -166,12 +187,26 @@
 def other_kernel(basis_ref, local_ref, old_ref, rest_ref, *refs):
     *out_refs, stack_ref = refs
     basis = basis_ref[...]
+    both = both_parts(basis)
     block = rest_ref.shape[1]
     columns = CHUNKS * block
     places = [(True, k) for k in range(1, CHUNKS)] + [(False, k) for k in range(CHUNKS)]
-    for (other, k), out_ref in zip(places, (rest_ref, *out_refs)):
-        there = pl.ds(pl.multiple_of(side_start(other, columns) + k * block, block), block)
-        out_ref[...] = product(basis, local_ref[:, there], old_ref[:, there])
+    group = lax.axis_index("group")
+    parts = [
+        (pl.ds(pl.multiple_of(side_start(other, columns) + k * block, block), block), out_ref)
+        for (other, k), out_ref in zip(places, (rest_ref, *out_refs))
+    ]
+
+    @pl.when(group == 0)
+    def _():
+        for there, out_ref in parts:
+            out_ref[...] = local_product(both, local_ref[:, there])
+
+    @pl.when(group == 1)
+    def _():
+        for there, out_ref in parts:
+            out_ref[...] = doubled_product(both, local_ref[:, there], old_ref[:, there])
+
     high = basis.astype(bf16).astype(f32)
     stack_ref[...] = jnp.concatenate([high, basis - high, high], axis=0).T.astype(bf16)
 

time: 18.5 us -> 18.3 us (0.989)
  starting transfers between devices: 8.74 us -> 9.05 us
  waiting for transfers between devices: 1.93 us -> 1.63 us
  Pallas kernels: 6.7 us -> 6.5 us
    ppermute x1, starting transfers between devices: 0.52 us -> 0.75 us  [paired(): theirs = [lax.ppermute(first_part(*embed), 'group', swap)]]
    pallas_call x1, Pallas kernels: 1.53 us -> 1.33 us  [first_part(): pl.pallas_call(first_kernel, in_specs=[ANY] * 3, out_specs=WHOLE, out_sha...]
where the time goes in v8:
time: 18.3 us; the launch traced here: 18.1 us
  starting transfers between devices  9.05 us (49%)
  Pallas kernels  6.5 us (36%)
  waiting for transfers between devices  1.63 us (9%)
  between operations  0.88 us (5%)
    ppermute x2, starting transfers between devices, paired(): moving = [lax.ppermute(total, axes, first) for total in totals]  3.43 us
    ppermute x2, starting transfers between devices, paired(): moving = [lax.ppermute(total, axes, second) for total in totals]  3.36 us
    pallas_call x2, Pallas kernels, embed_pieces(): pl.pallas_call(functools.partial(embed_kernel, pieces, ready), in_specs=[...  2.24 us
    pallas_call x1, Pallas kernels, dense_after(): pl.pallas_call(after_kernel, in_specs=[WHOLE] * 11 + [ANY], out_specs=[AN...  1.81 us
    pallas_call x1, Pallas kernels, first_part(): pl.pallas_call(first_kernel, in_specs=[ANY] * 3, out_specs=WHOLE, out_sha...  1.33 us
    ppermute x2, waiting for transfers between devices, paired(): moving = [lax.ppermute(total, axes, first) for total in totals]  0.82 us
    ppermute x1, starting transfers between devices, paired(): theirs = [lax.ppermute(first_part(*embed), 'group', swap)]  0.75 us
    ppermute x1, starting transfers between devices, paired(): rest = [lax.ppermute(own[0], 'group', swap)]  0.66 us
  transfers between devices with their start and end apart: 9, of which 4 were waited for; matrix products, arithmetic and copies ran while one was open for 0% of the time, Pallas kernels for 23%

profile of v8, /device:TPU:0, one launch (start us, length us, event | category | flops | bytes accessed | tf_op | source)
XLA Modules:
  0.0 18.1 jit_solution(3482209138009055008)
XLA Ops:
  0.7 1.3 %first_part.1 = f32[64,512]{1,0:T(8,128)S(1)} custom-call(f32[64,192]{1,0:T(8,128)} %bitcast.12, bf16[192,2048]{1,0:T(8,128)(2,1)} %bitcast.10, f32[192,2048]{1,0:T(8,128)} %old_ref.7), custom_call_target="tpu_custom_call" | custom-call | flops 37748736 | bytes 589824 | tf_op jit(solution)/shard_map/first_part/pallas_call | solution.py:168
  2.0 0.0 copy-start.3
  2.0 0.0 copy-start.4
  2.0 0.0 copy-start.5
  2.0 0.0 copy-start.6
  2.1 0.0 copy-start.7
  2.1 0.0 copy-start.8
  2.1 0.0 copy-start.9
  2.1 0.0 copy-start.10
  2.1 0.0 copy-start.11
  2.1 0.7 %collective-permute-start = (f32[64,512]{1,0:T(8,128)S(1)}, f32[64,512]{1,0:T(8,128)S(1)}, u32[]{:S(2)}, u32[]{:S(2)}) collective-permute-start(f32[64,512]{1,0:T(8,128)S(1)} %first_part.1), channel_id=1, source_target_pairs={{0,16},{16,0},{1,17},{17,1},{2,18},{18,2},{3,19},{19,3},{4,20},{20... | collective-permute-start | bytes 393224 | tf_op jit(solution)/shard_map/ppermute | solution.py:673
  2.9 0.4 %other_parts.1 = (f32[64,512]{1,0:T(8,128)S(1)}, f32[64,512]{1,0:T(8,128)S(1)}, f32[64,512]{1,0:T(8,128)S(1)}, bf16[192,192]{1,0:T(8,128)(2,1)S(1)}) custom-call(f32[64,192]{1,0:T(8,128)S(1)} %bitcast.13, bf16[192,2048]{1,0:T(8,128)(2,1)S(1)} %bitcast.11, f32[192,2048]{1,0:T(8,128)S(1)} %copy-done), custom_call_target="tpu_custom_call" | custom-call | flops 10000000000 | bytes 1769472 | tf_op jit(solution)/shard_map/other_parts/pallas_call | solution.py:217
  3.3 0.3 %collective-permute-start.4 = (f32[64,512]{1,0:T(8,128)S(1)}, f32[64,512]{1,0:T(8,128)S(1)}, u32[]{:S(2)}, u32[]{:S(2)}) collective-permute-start(f32[64,512]{1,0:T(8,128)S(1)} %get-tuple-element.41), channel_id=1, source_target_pairs={{0,16},{16,0},{1,17},{17,1},{2,18},{18,2},{3,19},{19,3},{4,20},{20... | collective-permute-start | bytes 393224 | tf_op jit(solution)/shard_map/ppermute | solution.py:675
  3.6 0.2 %collective-permute-done.second_ref = f32[64,512]{1,0:T(8,128)S(1)} collective-permute-done((f32[64,512]{1,0:T(8,128)S(1)}, f32[64,512]{1,0:T(8,128)S(1)}, u32[]{:S(2)}, u32[]{:S(2)}) %collective-permute-start) | collective-permute-done | bytes 131104 | tf_op jit(solution)/shard_map/ppermute | solution.py:673
  3.9 2.4 %collective-permute-start.2 = (f32[64,512]{1,0:T(8,128)S(1)}, f32[64,512]{1,0:T(8,128)S(1)}, u32[]{:S(2)}, u32[]{:S(2)}) collective-permute-start(f32[64,512]{1,0:T(8,128)S(1)} %add.6.order_ref.first_ref), channel_id=1, source_target_pairs={{0,20},{4,28},{8,16},{12,24},{16,8},{20,0},{24,12},{28,4},{1,21},{... | collective-permute-start | bytes 393224 | tf_op jit(solution)/shard_map/ppermute | solution.py:689
  6.3 0.0 collective-permute-done.4.second_ref
  6.3 1.0 %collective-permute-start.5 = (f32[64,512]{1,0:T(8,128)S(1)}, f32[64,512]{1,0:T(8,128)S(1)}, u32[]{:S(2)}, u32[]{:S(2)}) collective-permute-start(f32[64,512]{1,0:T(8,128)S(1)} %add.8.first_ref), channel_id=1, source_target_pairs={{0,20},{4,28},{8,16},{12,24},{16,8},{20,0},{24,12},{28,4},{1,21},{... | collective-permute-start | bytes 393224 | tf_op jit(solution)/shard_map/ppermute | solution.py:689
  7.4 0.4 %dense_before.1.send_ref = f32[6,584,128]{2,1,0:T(8,128)S(1)} custom-call(f32[64,512]{1,0:T(8,128)S(1)} %add.6.order_ref.first_ref, bf16[1,192,576]{2,1,0:T(8,128)(2,1)S(1)} %copy-done.7, bf16[1,192,192]{2,1,0:T(8,128)(2,1)S(1)} %copy-done.8, bf16[1,192,768]{2,1,0:T(8,128)(2,1)S(1)} %copy-done.5, bf16[1,192,768]{2,1,0:T(8,128)(2,1)S(1)} %bitcast.18, ...), custom_call_target="tpu_custom_call" | custom-call | flops 8847360000 | bytes 4423680 | tf_op jit(solution)/shard_map/dense_before/pallas_call | solution.py:607
  7.8 0.4 %collective-permute-start.1 = (f32[6,584,128]{2,1,0:T(8,128)S(1)}, f32[6,584,128]{2,1,0:T(8,128)S(1)}, u32[]{:S(2)}, u32[]{:S(2)}) collective-permute-start(f32[6,584,128]{2,1,0:T(8,128)S(1)} %dense_before.1.send_ref), channel_id=1, source_target_pairs={{0,16},{16,0},{1,17},{17,1},{2,18},{18,2},{3,19},{19,3},{4,20},{20... | collective-permute-start | bytes 5382152 | tf_op jit(solution)/shard_map/ppermute | solution.py:691
  8.1 0.8 %collective-permute-done.2.second_ref = f32[64,512]{1,0:T(8,128)S(1)} collective-permute-done((f32[64,512]{1,0:T(8,128)S(1)}, f32[64,512]{1,0:T(8,128)S(1)}, u32[]{:S(2)}, u32[]{:S(2)}) %collective-permute-start.2) | collective-permute-done | bytes 131104 | tf_op jit(solution)/shard_map/ppermute | solution.py:689
  9.0 2.1 %collective-permute-start.3 = (f32[64,512]{1,0:T(8,128)S(1)}, f32[64,512]{1,0:T(8,128)S(1)}, u32[]{:S(2)}, u32[]{:S(2)}) collective-permute-start(f32[64,512]{1,0:T(8,128)S(1)} %add.7.first_ref), channel_id=1, source_target_pairs={{0,24},{4,16},{8,28},{12,20},{16,4},{20,12},{24,0},{28,8},{1,25},{... | collective-permute-start | bytes 393224 | tf_op jit(solution)/shard_map/ppermute | solution.py:695
  11.1 0.0 collective-permute-done.5.second_ref
  11.1 1.2 %collective-permute-start.6 = (f32[64,512]{1,0:T(8,128)S(1)}, f32[64,512]{1,0:T(8,128)S(1)}, u32[]{:S(2)}, u32[]{:S(2)}) collective-permute-start(f32[64,512]{1,0:T(8,128)S(1)} %add.9.first_ref), channel_id=1, source_target_pairs={{0,24},{4,16},{8,28},{12,20},{16,4},{20,12},{24,0},{28,8},{1,25},{... | collective-permute-start | bytes 393224 | tf_op jit(solution)/shard_map/ppermute | solution.py:695
  12.4 0.0 collective-permute-done.1.recv_ref
  12.4 1.8 %dense_after.1 = (f32[192,576]{1,0:T(8,128)}, f32[192,192]{1,0:T(8,128)}, f32[192,768]{1,0:T(8,128)}, f32[192,768]{1,0:T(8,128)}, f32[1728,128]{1,0:T(8,128)}, /...) custom-call(f32[6,584,128]{2,1,0:T(8,128)S(1)} %collective-permute-done.1.recv_ref, ...), custom_call_target="tpu_custom_call" | custom-call | flops 8847360000 | bytes 5898240 | tf_op jit(solution)/shard_map/dense_after/pallas_call | solution.py:625
  14.2 0.7 %collective-permute-start.8 = (f32[64,512]{1,0:T(8,128)S(1)}, f32[64,512]{1,0:T(8,128)S(1)}, u32[]{:S(2)}, u32[]{:S(2)}) collective-permute-start(f32[64,512]{1,0:T(8,128)S(1)} %add.10.coeff_ref), channel_id=1, source_target_pairs={{0,16},{16,0},{1,17},{17,1},{2,18},{18,2},{3,19},{19,3},{4,20},{20... | collective-permute-start | bytes 393224 | tf_op jit(solution)/shard_map/ppermute | solution.py:699
  14.9 0.2 %embed_early.1 = (f32[192,512]{1,0:T(8,128)S(1)}, f32[64,512]{1,0:T(8,128)S(1)}) custom-call(bf16[192,192]{1,0:T(8,128)(2,1)S(1)} %get-tuple-element.38.stack_ref, f32[64,2048]{1,0:T(8,128)S(1)} %get-tuple-element.39.moment_ref, f32[192,2048]{1,0:T(8,128)S(1)} %copy-done, f32[64,512]{1,0:T(8,128)S(1)} %add.10.coeff_ref), custom_call_target="tpu_custom_call" | custom-call | flops 37748736 | bytes 786432 | tf_op jit(solution)/shard_map/embed_early/pallas_call | solution.py:268
  15.1 0.5 %collective-permute-done.6.second_ref = f32[64,512]{1,0:T(8,128)S(1)} collective-permute-done((f32[64,512]{1,0:T(8,128)S(1)}, f32[64,512]{1,0:T(8,128)S(1)}, u32[]{:S(2)}, u32[]{:S(2)}) %collective-permute-start.6) | collective-permute-done | bytes 131104 | tf_op jit(solution)/shard_map/ppermute | solution.py:695
  15.6 0.2 collective-permute-start.7
  15.8 0.1 collective-permute-done.8.refs_1_
  15.9 1.2 %embed_pieces.2 = (f32[192,2048]{1,0:T(8,128)}, f32[64,2048]{1,0:T(8,128)}) custom-call(bf16[192,192]{1,0:T(8,128)(2,1)S(1)} %get-tuple-element.38.stack_ref, f32[64,2048]{1,0:T(8,128)S(1)} %get-tuple-element.39.moment_ref, f32[192,2048]{1,0:T(8,128)S(1)} %copy-done, f32[64,512]{1,0:T(8,128)S(1)} %add.11.refs_0_, ...), custom_call_target="tpu_custom_call" | custom-call | flops 75497472 | bytes 1572864 | tf_op jit(solution)/shard_map/embed_pieces/pallas_call | solution.py:318
  17.1 1.0 %embed_pieces.3 = (f32[192,2048]{1,0:T(8,128)}, f32[64,2048]{1,0:T(8,128)}) custom-call(bf16[192,192]{1,0:T(8,128)(2,1)S(1)} %get-tuple-element.38.stack_ref, f32[64,2048]{1,0:T(8,128)S(1)} %get-tuple-element.39.moment_ref, f32[192,2048]{1,0:T(8,128)S(1)} %copy-done, ...), custom_call_target="tpu_custom_call", output_to_operand_aliasing={{0}: (4, {}), {1}: (5, {})} | custom-call | flops 37748736 | bytes 786432 | tf_op jit(solution)/shard_map/embed_pieces/pallas_call | solution.py:318
  (23 shorter events, 0.1 us)
Async XLA Ops:
  0.6 2.2 %copy-start = (f32[192,2048]{1,0:T(8,128)S(1)}, f32[192,2048]{1,0:T(8,128)}, u32[]{:S(2)}) copy-start(f32[192,2048]{1,0:T(8,128)} %old_ref.7) | copy-start | bytes 4718596
  0.7 2.2 %copy-start.2 = (f32[192,64]{0,1:T(8,128)S(1)}, f32[192,64]{0,1:T(8,128)}, u32[]{:S(2)}) copy-start(f32[192,64]{0,1:T(8,128)} %param.24) | copy-start | bytes 147460
  0.7 2.2 %copy-start.1 = (bf16[1,192,2048]{2,1,0:T(8,128)(2,1)S(1)}, bf16[1,192,2048]{2,1,0:T(8,128)(2,1)}, u32[]{:S(2)}) copy-start(bf16[1,192,2048]{2,1,0:T(8,128)(2,1)} %param.22) | copy-start | bytes 2359300
  2.0 5.3 %copy-start.3 = (f32[1,221184]{1,0:T(1,128)S(1)}, f32[1,221184]{1,0:T(1,128)}, u32[]{:S(2)}) copy-start(f32[1,221184]{1,0:T(1,128)} %param.18) | copy-start | bytes 2654212
  2.0 5.3 %copy-start.4 = (f32[1,221184]{1,0:T(1,128)S(1)}, f32[1,221184]{1,0:T(1,128)}, u32[]{:S(2)}) copy-start(f32[1,221184]{1,0:T(1,128)} %param.19) | copy-start | bytes 2654212
  2.0 5.3 %copy-start.5 = (bf16[1,192,768]{2,1,0:T(8,128)(2,1)S(1)}, bf16[1,192,768]{2,1,0:T(8,128)(2,1)}, u32[]{:S(2)}) copy-start(bf16[1,192,768]{2,1,0:T(8,128)(2,1)} %up_ref.3) | copy-start | bytes 884740
  2.0 5.3 %copy-start.6 = (bf16[1,768,192]{1,2,0:T(8,128)(2,1)S(1)}, bf16[1,768,192]{1,2,0:T(8,128)(2,1)}, u32[]{:S(2)}) copy-start(bf16[1,768,192]{1,2,0:T(8,128)(2,1)} %param.16) | copy-start | bytes 884740
  2.1 5.3 %copy-start.7 = (bf16[1,192,576]{2,1,0:T(8,128)(2,1)S(1)}, bf16[1,192,576]{2,1,0:T(8,128)(2,1)}, u32[]{:S(2)}) copy-start(bf16[1,192,576]{2,1,0:T(8,128)(2,1)} %in_ref.3) | copy-start | bytes 663556
  2.1 5.3 %copy-start.8 = (bf16[1,192,192]{2,1,0:T(8,128)(2,1)S(1)}, bf16[1,192,192]{2,1,0:T(8,128)(2,1)}, u32[]{:S(2)}) copy-start(bf16[1,192,192]{2,1,0:T(8,128)(2,1)} %out_ref.3) | copy-start | bytes 221188
  2.1 5.3 %copy-start.9 = (bf16[1,1920]{1,0:T(2,128)(2,1)S(1)}, bf16[1,1920]{1,0:T(2,128)(2,1)}, u32[]{:S(2)}) copy-start(bf16[1,1920]{1,0:T(2,128)(2,1)} %small_ref.3) | copy-start | bytes 11524
  2.1 5.3 %copy-start.10 = (f32[960]{0:T(1024)S(1)}, f32[960]{0:T(1024)}, u32[]{:S(2)}) copy-start(f32[960]{0:T(1024)} %param.20) | copy-start | bytes 11524
  2.1 5.3 %copy-start.11 = (f32[960]{0:T(1024)S(1)}, f32[960]{0:T(1024)}, u32[]{:S(2)}) copy-start(f32[960]{0:T(1024)} %param.21) | copy-start | bytes 11524
  2.1 1.7 %collective-permute-start = (f32[64,512]{1,0:T(8,128)S(1)}, f32[64,512]{1,0:T(8,128)S(1)}, u32[]{:S(2)}, u32[]{:S(2)}) collective-permute-start(f32[64,512]{1,0:T(8,128)S(1)} %first_part.1), channel_id=1, source_target_pairs={{0,16},{16,0},{1,17},{17,1},{2,18},{18,2},{3,19},{19,3},{4,20},{20... | collective-permute-start | bytes 393224 | tf_op jit(solution)/shard_map/ppermute | solution.py:673
  3.3 3.0 %collective-permute-start.4 = (f32[64,512]{1,0:T(8,128)S(1)}, f32[64,512]{1,0:T(8,128)S(1)}, u32[]{:S(2)}, u32[]{:S(2)}) collective-permute-start(f32[64,512]{1,0:T(8,128)S(1)} %get-tuple-element.41), channel_id=1, source_target_pairs={{0,16},{16,0},{1,17},{17,1},{2,18},{18,2},{3,19},{19,3},{4,20},{20... | collective-permute-start | bytes 393224 | tf_op jit(solution)/shard_map/ppermute | solution.py:675
  3.9 5.1 %collective-permute-start.2 = (f32[64,512]{1,0:T(8,128)S(1)}, f32[64,512]{1,0:T(8,128)S(1)}, u32[]{:S(2)}, u32[]{:S(2)}) collective-permute-start(f32[64,512]{1,0:T(8,128)S(1)} %add.6.order_ref.first_ref), channel_id=1, source_target_pairs={{0,20},{4,28},{8,16},{12,24},{16,8},{20,0},{24,12},{28,4},{1,21},{... | collective-permute-start | bytes 393224 | tf_op jit(solution)/shard_map/ppermute | solution.py:689
  6.3 4.8 %collective-permute-start.5 = (f32[64,512]{1,0:T(8,128)S(1)}, f32[64,512]{1,0:T(8,128)S(1)}, u32[]{:S(2)}, u32[]{:S(2)}) collective-permute-start(f32[64,512]{1,0:T(8,128)S(1)} %add.8.first_ref), channel_id=1, source_target_pairs={{0,20},{4,28},{8,16},{12,24},{16,8},{20,0},{24,12},{28,4},{1,21},{... | collective-permute-start | bytes 393224 | tf_op jit(solution)/shard_map/ppermute | solution.py:689
  7.8 4.6 %collective-permute-start.1 = (f32[6,584,128]{2,1,0:T(8,128)S(1)}, f32[6,584,128]{2,1,0:T(8,128)S(1)}, u32[]{:S(2)}, u32[]{:S(2)}) collective-permute-start(f32[6,584,128]{2,1,0:T(8,128)S(1)} %dense_before.1.send_ref), channel_id=1, source_target_pairs={{0,16},{16,0},{1,17},{17,1},{2,18},{18,2},{3,19},{19,3},{4,20},{20... | collective-permute-start | bytes 5382152 | tf_op jit(solution)/shard_map/ppermute | solution.py:691
  9.0 5.2 %collective-permute-start.3 = (f32[64,512]{1,0:T(8,128)S(1)}, f32[64,512]{1,0:T(8,128)S(1)}, u32[]{:S(2)}, u32[]{:S(2)}) collective-permute-start(f32[64,512]{1,0:T(8,128)S(1)} %add.7.first_ref), channel_id=1, source_target_pairs={{0,24},{4,16},{8,28},{12,20},{16,4},{20,12},{24,0},{28,8},{1,25},{... | collective-permute-start | bytes 393224 | tf_op jit(solution)/shard_map/ppermute | solution.py:695
  11.1 4.5 %collective-permute-start.6 = (f32[64,512]{1,0:T(8,128)S(1)}, f32[64,512]{1,0:T(8,128)S(1)}, u32[]{:S(2)}, u32[]{:S(2)}) collective-permute-start(f32[64,512]{1,0:T(8,128)S(1)} %add.9.first_ref), channel_id=1, source_target_pairs={{0,24},{4,16},{8,28},{12,20},{16,4},{20,12},{24,0},{28,8},{1,25},{... | collective-permute-start | bytes 393224 | tf_op jit(solution)/shard_map/ppermute | solution.py:695
  14.2 1.6 %collective-permute-start.8 = (f32[64,512]{1,0:T(8,128)S(1)}, f32[64,512]{1,0:T(8,128)S(1)}, u32[]{:S(2)}, u32[]{:S(2)}) collective-permute-start(f32[64,512]{1,0:T(8,128)S(1)} %add.10.coeff_ref), channel_id=1, source_target_pairs={{0,16},{16,0},{1,17},{17,1},{2,18},{18,2},{3,19},{19,3},{4,20},{20... | collective-permute-start | bytes 393224 | tf_op jit(solution)/shard_map/ppermute | solution.py:699
  15.6 1.5 %collective-permute-start.7 = (f32[64,512]{1,0:T(8,128)S(1)}, f32[64,512]{1,0:T(8,128)S(1)}, u32[]{:S(2)}, u32[]{:S(2)}) collective-permute-start(f32[64,512]{1,0:T(8,128)S(1)} %add.11.refs_0_), channel_id=1, source_target_pairs={{0,16},{16,0},{1,17},{17,1},{2,18},{18,2},{3,19},{19,3},{4,20},{20... | collective-permute-start | bytes 393224 | tf_op jit(solution)/shard_map/ppermute | solution.py:702

commit v9 on v8

--- a/solution.py
+++ b/solution.py
@@ -184,31 +184,29 @@
     )(*in_hbm((basis_t, local, old)))
 
 
-def other_kernel(basis_ref, local_ref, old_ref, rest_ref, *refs):
-    *out_refs, stack_ref = refs
-    basis = basis_ref[...]
-    both = both_parts(basis)
+def other_kernel(basis_ref, local_ref, old_ref, rest_ref, *out_refs):
     block = rest_ref.shape[1]
     columns = CHUNKS * block
     places = [(True, k) for k in range(1, CHUNKS)] + [(False, k) for k in range(CHUNKS)]
-    group = lax.axis_index("group")
     parts = [
         (pl.ds(pl.multiple_of(side_start(other, columns) + k * block, block), block), out_ref)
         for (other, k), out_ref in zip(places, (rest_ref, *out_refs))
     ]
 
+    def run(multiply):
+        both = both_parts(basis_ref[...])
+        for there, out_ref in parts:
+            out_ref[...] = multiply(both, there)
+
+    group = lax.axis_index("group")
+
     @pl.when(group == 0)
     def _():
-        for there, out_ref in parts:
-            out_ref[...] = local_product(both, local_ref[:, there])
+        run(lambda both, there: local_product(both, local_ref[:, there]))
 
     @pl.when(group == 1)
     def _():
-        for there, out_ref in parts:
-            out_ref[...] = doubled_product(both, local_ref[:, there], old_ref[:, there])
-
-    high = basis.astype(bf16).astype(f32)
-    stack_ref[...] = jnp.concatenate([high, basis - high, high], axis=0).T.astype(bf16)
+        run(lambda both, there: doubled_product(both, local_ref[:, there], old_ref[:, there]))
 
 
 def other_parts(basis_t, local, old):
@@ -217,9 +215,8 @@
     return pl.pallas_call(
         other_kernel,
         in_specs=[WHOLE] * 3,
-        out_specs=[WHOLE] * (2 * CHUNKS),
-        out_shape=[jax.ShapeDtypeStruct((rank, block), f32)] * (2 * CHUNKS - 1)
-        + [jax.ShapeDtypeStruct((depth, 3 * rank), bf16)],
+        out_specs=[WHOLE] * (2 * CHUNKS - 1),
+        out_shape=[jax.ShapeDtypeStruct((rank, block), f32)] * (2 * CHUNKS - 1),
         compiler_params=pltpu.CompilerParams(vmem_limit_bytes=4 * 2**20),
         cost_estimate=pl.CostEstimate(
             flops=10**10, bytes_accessed=18 * depth * block, transcendentals=0
@@ -393,10 +390,13 @@
 
 
 def before_kernel(
-    order_ref, in_ref, out_ref, up_ref, down_ref, old_ref, mom_ref, small_ref, small_old_ref,
-    small_mom_ref, send_ref, wide_ref,
+    order_ref, basis_ref, in_ref, out_ref, up_ref, down_ref, old_ref, mom_ref, small_ref,
+    small_old_ref, small_mom_ref, send_ref, stack_ref, wide_ref,
 ):
     del order_ref
+    basis = basis_ref[...]
+    high = basis.astype(bf16).astype(f32)
+    stack_ref[...] = jnp.concatenate([high, basis - high, high], axis=0).T.astype(bf16)
     group = lax.axis_index("group")
     rows = up_ref.shape[1]
     mid = rows // 2
@@ -602,20 +602,24 @@
             copy.wait()
 
 
-def dense_before(order, operands):
+def dense_before(order, basis_t, operands):
     _, rows, width = operands[2].shape
+    rank, depth = basis_t.shape
     return pl.pallas_call(
         before_kernel,
-        in_specs=[ANY] + [WHOLE] * 9,
-        out_specs=WHOLE,
-        out_shape=jax.ShapeDtypeStruct((width // LANES, 3 * rows + 8, LANES), f32),
+        in_specs=[ANY] + [WHOLE] * 10,
+        out_specs=[WHOLE] * 2,
+        out_shape=[
+            jax.ShapeDtypeStruct((width // LANES, 3 * rows + 8, LANES), f32),
+            jax.ShapeDtypeStruct((depth, 3 * rank), bf16),
+        ],
         scratch_shapes=[pltpu.VMEM((2, width, LANES), f32)],
         compiler_params=pltpu.CompilerParams(vmem_limit_bytes=4 * 2**20),
         cost_estimate=pl.CostEstimate(
             flops=60000 * rows * width, bytes_accessed=30 * rows * width, transcendentals=0
         ),
         name="dense_before",
-    )(order, *operands)
+    )(order, basis_t, *operands)
 
 
 def dense_after(received, sent, operands, moment):
@@ -671,7 +675,7 @@
 
     embed = (basis.T, embed_local[0], embed_old)
     theirs = [lax.ppermute(first_part(*embed), "group", swap)]
-    late, *mine, stack = other_parts(*embed)
+    late, *mine = other_parts(*embed)
     theirs.append(lax.ppermute(late, "group", swap))
 
     operands = (
@@ -687,7 +691,7 @@
     )
     totals = [add(*pair, flops=10**4) for pair in zip(mine, theirs)]
     moving = [lax.ppermute(total, axes, first) for total in totals]
-    sent = dense_before(totals[0], operands)
+    sent, stack = dense_before(totals[0], embed[0], operands)
     received = lax.ppermute(sent, "group", swap)
     totals = [
         add(*pair, flops=flops) for *pair, flops in zip(totals, moving, (10**4, 2 * 10**10))

time: 18.3 us -> 18.3 us (level)
  no operation moved by 1% of the time
where the time goes in v9:
time: 18.3 us; the launch traced here: 18.1 us
  starting transfers between devices  8.93 us (49%)
  Pallas kernels  6.49 us (35%)
  waiting for transfers between devices  1.75 us (10%)
  between operations  0.88 us (5%)
    ppermute x2, starting transfers between devices, paired(): moving = [lax.ppermute(total, axes, second) for total in totals]  3.36 us
    ppermute x2, starting transfers between devices, paired(): moving = [lax.ppermute(total, axes, first) for total in totals]  3.32 us
    pallas_call x2, Pallas kernels, embed_pieces(): pl.pallas_call(functools.partial(embed_kernel, pieces, ready), in_specs=[...  2.24 us
    pallas_call x1, Pallas kernels, dense_after(): pl.pallas_call(after_kernel, in_specs=[WHOLE] * 11 + [ANY], out_specs=[AN...  1.81 us
    pallas_call x1, Pallas kernels, first_part(): pl.pallas_call(first_kernel, in_specs=[ANY] * 3, out_specs=WHOLE, out_sha...  1.33 us
    ppermute x2, waiting for transfers between devices, paired(): moving = [lax.ppermute(total, axes, first) for total in totals]  0.81 us
    ppermute x1, starting transfers between devices, paired(): theirs = [lax.ppermute(first_part(*embed), 'group', swap)]  0.75 us
    ppermute x1, starting transfers between devices, paired(): rest = [lax.ppermute(own[0], 'group', swap)]  0.66 us
  transfers between devices with their start and end apart: 9, of which 4 were waited for; matrix products, arithmetic and copies ran while one was open for 0% of the time, Pallas kernels for 23%

profile of v9, /device:TPU:0, one launch (start us, length us, event | category | flops | bytes accessed | tf_op | source)
XLA Modules:
  0.0 18.1 jit_solution(7761736739673825989)
XLA Ops:
  0.7 1.3 %first_part.1 = f32[64,512]{1,0:T(8,128)S(1)} custom-call(f32[64,192]{1,0:T(8,128)} %bitcast.12, bf16[192,2048]{1,0:T(8,128)(2,1)} %bitcast.10, f32[192,2048]{1,0:T(8,128)} %old_ref.7), custom_call_target="tpu_custom_call" | custom-call | flops 37748736 | bytes 589824 | tf_op jit(solution)/shard_map/first_part/pallas_call | solution.py:168
  2.0 0.0 copy-start.3
  2.0 0.0 copy-start.4
  2.0 0.0 copy-start.5
  2.0 0.0 copy-start.6
  2.1 0.0 copy-start.7
  2.1 0.0 copy-start.8
  2.1 0.0 copy-start.9
  2.1 0.0 copy-start.10
  2.1 0.0 copy-start.11
  2.1 0.7 %collective-permute-start = (f32[64,512]{1,0:T(8,128)S(1)}, f32[64,512]{1,0:T(8,128)S(1)}, u32[]{:S(2)}, u32[]{:S(2)}) collective-permute-start(f32[64,512]{1,0:T(8,128)S(1)} %first_part.1), channel_id=1, source_target_pairs={{0,16},{16,0},{1,17},{17,1},{2,18},{18,2},{3,19},{19,3},{4,20},{20... | collective-permute-start | bytes 393224 | tf_op jit(solution)/shard_map/ppermute | solution.py:677
  2.9 0.3 %other_parts.1 = (f32[64,512]{1,0:T(8,128)S(1)}, f32[64,512]{1,0:T(8,128)S(1)}, f32[64,512]{1,0:T(8,128)S(1)}) custom-call(f32[64,192]{1,0:T(8,128)S(1)} %bitcast.13, bf16[192,2048]{1,0:T(8,128)(2,1)S(1)} %bitcast.11, f32[192,2048]{1,0:T(8,128)S(1)} %copy-done), custom_call_target="tpu_custom_call" | custom-call | flops 10000000000 | bytes 1769472 | tf_op jit(solution)/shard_map/other_parts/pallas_call | solution.py:215
  3.2 0.3 %collective-permute-start.4 = (f32[64,512]{1,0:T(8,128)S(1)}, f32[64,512]{1,0:T(8,128)S(1)}, u32[]{:S(2)}, u32[]{:S(2)}) collective-permute-start(f32[64,512]{1,0:T(8,128)S(1)} %get-tuple-element.43), channel_id=1, source_target_pairs={{0,16},{16,0},{1,17},{17,1},{2,18},{18,2},{3,19},{19,3},{4,20},{20... | collective-permute-start | bytes 393224 | tf_op jit(solution)/shard_map/ppermute | solution.py:679
  3.5 0.4 %collective-permute-done.second_ref = f32[64,512]{1,0:T(8,128)S(1)} collective-permute-done((f32[64,512]{1,0:T(8,128)S(1)}, f32[64,512]{1,0:T(8,128)S(1)}, u32[]{:S(2)}, u32[]{:S(2)}) %collective-permute-start) | collective-permute-done | bytes 131104 | tf_op jit(solution)/shard_map/ppermute | solution.py:677
  3.9 2.4 %collective-permute-start.2 = (f32[64,512]{1,0:T(8,128)S(1)}, f32[64,512]{1,0:T(8,128)S(1)}, u32[]{:S(2)}, u32[]{:S(2)}) collective-permute-start(f32[64,512]{1,0:T(8,128)S(1)} %add.6.order_ref.first_ref), channel_id=1, source_target_pairs={{0,20},{4,28},{8,16},{12,24},{16,8},{20,0},{24,12},{28,4},{1,21},{... | collective-permute-start | bytes 393224 | tf_op jit(solution)/shard_map/ppermute | solution.py:693
  6.3 0.0 collective-permute-done.4.second_ref
  6.3 0.9 %collective-permute-start.5 = (f32[64,512]{1,0:T(8,128)S(1)}, f32[64,512]{1,0:T(8,128)S(1)}, u32[]{:S(2)}, u32[]{:S(2)}) collective-permute-start(f32[64,512]{1,0:T(8,128)S(1)} %add.8.first_ref), channel_id=1, source_target_pairs={{0,20},{4,28},{8,16},{12,24},{16,8},{20,0},{24,12},{28,4},{1,21},{... | collective-permute-start | bytes 393224 | tf_op jit(solution)/shard_map/ppermute | solution.py:693
  7.3 0.5 %dense_before.1 = (f32[6,584,128]{2,1,0:T(8,128)S(1)}, bf16[192,192]{1,0:T(8,128)(2,1)S(1)}) custom-call(f32[64,512]{1,0:T(8,128)S(1)} %add.6.order_ref.first_ref, f32[64,192]{1,0:T(8,128)S(1)} %bitcast.14, bf16[1,192,576]{2,1,0:T(8,128)(2,1)S(1)} %copy-done.7, bf16[1,192,192]{2,1,0:T(8,128)(2,1)S(1)} %copy-done.8, bf16[1,192,768]{2,1,0:T(8,128)(2,1)S(1)} %copy-done.5, ...), custom_call_target="tpu_custom_call" | custom-call | flops 8847360000 | bytes 4423680 | tf_op jit(solution)/shard_map/dense_before/pallas_call | solution.py:608
  7.8 0.4 %collective-permute-start.1 = (f32[6,584,128]{2,1,0:T(8,128)S(1)}, f32[6,584,128]{2,1,0:T(8,128)S(1)}, u32[]{:S(2)}, u32[]{:S(2)}) collective-permute-start(f32[6,584,128]{2,1,0:T(8,128)S(1)} %get-tuple-element.31.send_ref), channel_id=1, source_target_pairs={{0,16},{16,0},{1,17},{17,1},{2,18},{18,2},{3,19},{19,3},{4,20},{20... | collective-permute-start | bytes 5382152 | tf_op jit(solution)/shard_map/ppermute | solution.py:695
  8.2 0.8 %collective-permute-done.2.second_ref = f32[64,512]{1,0:T(8,128)S(1)} collective-permute-done((f32[64,512]{1,0:T(8,128)S(1)}, f32[64,512]{1,0:T(8,128)S(1)}, u32[]{:S(2)}, u32[]{:S(2)}) %collective-permute-start.2) | collective-permute-done | bytes 131104 | tf_op jit(solution)/shard_map/ppermute | solution.py:693
  9.0 2.1 %collective-permute-start.3 = (f32[64,512]{1,0:T(8,128)S(1)}, f32[64,512]{1,0:T(8,128)S(1)}, u32[]{:S(2)}, u32[]{:S(2)}) collective-permute-start(f32[64,512]{1,0:T(8,128)S(1)} %add.7.first_ref), channel_id=1, source_target_pairs={{0,24},{4,16},{8,28},{12,20},{16,4},{20,12},{24,0},{28,8},{1,25},{... | collective-permute-start | bytes 393224 | tf_op jit(solution)/shard_map/ppermute | solution.py:699
  11.1 0.0 collective-permute-done.5.second_ref
  11.1 1.2 %collective-permute-start.6 = (f32[64,512]{1,0:T(8,128)S(1)}, f32[64,512]{1,0:T(8,128)S(1)}, u32[]{:S(2)}, u32[]{:S(2)}) collective-permute-start(f32[64,512]{1,0:T(8,128)S(1)} %add.9.first_ref), channel_id=1, source_target_pairs={{0,24},{4,16},{8,28},{12,20},{16,4},{20,12},{24,0},{28,8},{1,25},{... | collective-permute-start | bytes 393224 | tf_op jit(solution)/shard_map/ppermute | solution.py:699
  12.4 0.0 collective-permute-done.1.recv_ref
  12.4 1.8 %dense_after.1 = (f32[192,576]{1,0:T(8,128)}, f32[192,192]{1,0:T(8,128)}, f32[192,768]{1,0:T(8,128)}, f32[192,768]{1,0:T(8,128)}, f32[1728,128]{1,0:T(8,128)}, /...) custom-call(f32[6,584,128]{2,1,0:T(8,128)S(1)} %collective-permute-done.1.recv_ref, ...), custom_call_target="tpu_custom_call" | custom-call | flops 8847360000 | bytes 5898240 | tf_op jit(solution)/shard_map/dense_after/pallas_call | solution.py:629
  14.2 0.7 %collective-permute-start.8 = (f32[64,512]{1,0:T(8,128)S(1)}, f32[64,512]{1,0:T(8,128)S(1)}, u32[]{:S(2)}, u32[]{:S(2)}) collective-permute-start(f32[64,512]{1,0:T(8,128)S(1)} %add.10.coeff_ref), channel_id=1, source_target_pairs={{0,16},{16,0},{1,17},{17,1},{2,18},{18,2},{3,19},{19,3},{4,20},{20... | collective-permute-start | bytes 393224 | tf_op jit(solution)/shard_map/ppermute | solution.py:703
  14.9 0.2 %embed_early.1 = (f32[192,512]{1,0:T(8,128)S(1)}, f32[64,512]{1,0:T(8,128)S(1)}) custom-call(bf16[192,192]{1,0:T(8,128)(2,1)S(1)} %get-tuple-element.40.stack_ref, f32[64,2048]{1,0:T(8,128)S(1)} %get-tuple-element.41.moment_ref, f32[192,2048]{1,0:T(8,128)S(1)} %copy-done, f32[64,512]{1,0:T(8,128)S(1)} %add.10.coeff_ref), custom_call_target="tpu_custom_call" | custom-call | flops 37748736 | bytes 786432 | tf_op jit(solution)/shard_map/embed_early/pallas_call | solution.py:265
  15.1 0.5 %collective-permute-done.6.second_ref = f32[64,512]{1,0:T(8,128)S(1)} collective-permute-done((f32[64,512]{1,0:T(8,128)S(1)}, f32[64,512]{1,0:T(8,128)S(1)}, u32[]{:S(2)}, u32[]{:S(2)}) %collective-permute-start.6) | collective-permute-done | bytes 131104 | tf_op jit(solution)/shard_map/ppermute | solution.py:699
  15.6 0.2 collective-permute-start.7
  15.8 0.1 collective-permute-done.8.refs_1_
  15.9 1.2 %embed_pieces.2 = (f32[192,2048]{1,0:T(8,128)}, f32[64,2048]{1,0:T(8,128)}) custom-call(bf16[192,192]{1,0:T(8,128)(2,1)S(1)} %get-tuple-element.40.stack_ref, f32[64,2048]{1,0:T(8,128)S(1)} %get-tuple-element.41.moment_ref, f32[192,2048]{1,0:T(8,128)S(1)} %copy-done, f32[64,512]{1,0:T(8,128)S(1)} %add.11.refs_0_, ...), custom_call_target="tpu_custom_call" | custom-call | flops 75497472 | bytes 1572864 | tf_op jit(solution)/shard_map/embed_pieces/pallas_call | solution.py:315
  17.1 1.0 %embed_pieces.3 = (f32[192,2048]{1,0:T(8,128)}, f32[64,2048]{1,0:T(8,128)}) custom-call(bf16[192,192]{1,0:T(8,128)(2,1)S(1)} %get-tuple-element.40.stack_ref, f32[64,2048]{1,0:T(8,128)S(1)} %get-tuple-element.41.moment_ref, f32[192,2048]{1,0:T(8,128)S(1)} %copy-done, ...), custom_call_target="tpu_custom_call", output_to_operand_aliasing={{0}: (4, {}), {1}: (5, {})} | custom-call | flops 37748736 | bytes 786432 | tf_op jit(solution)/shard_map/embed_pieces/pallas_call | solution.py:315
  (23 shorter events, 0.1 us)
Async XLA Ops:
  0.6 2.2 %copy-start = (f32[192,2048]{1,0:T(8,128)S(1)}, f32[192,2048]{1,0:T(8,128)}, u32[]{:S(2)}) copy-start(f32[192,2048]{1,0:T(8,128)} %old_ref.7) | copy-start | bytes 4718596
  0.7 2.2 %copy-start.2 = (f32[192,64]{0,1:T(8,128)S(1)}, f32[192,64]{0,1:T(8,128)}, u32[]{:S(2)}) copy-start(f32[192,64]{0,1:T(8,128)} %param.24) | copy-start | bytes 147460
  0.7 2.2 %copy-start.1 = (bf16[1,192,2048]{2,1,0:T(8,128)(2,1)S(1)}, bf16[1,192,2048]{2,1,0:T(8,128)(2,1)}, u32[]{:S(2)}) copy-start(bf16[1,192,2048]{2,1,0:T(8,128)(2,1)} %param.22) | copy-start | bytes 2359300
  2.0 5.2 %copy-start.3 = (f32[1,221184]{1,0:T(1,128)S(1)}, f32[1,221184]{1,0:T(1,128)}, u32[]{:S(2)}) copy-start(f32[1,221184]{1,0:T(1,128)} %param.18) | copy-start | bytes 2654212
  2.0 5.2 %copy-start.4 = (f32[1,221184]{1,0:T(1,128)S(1)}, f32[1,221184]{1,0:T(1,128)}, u32[]{:S(2)}) copy-start(f32[1,221184]{1,0:T(1,128)} %param.19) | copy-start | bytes 2654212
  2.0 5.2 %copy-start.5 = (bf16[1,192,768]{2,1,0:T(8,128)(2,1)S(1)}, bf16[1,192,768]{2,1,0:T(8,128)(2,1)}, u32[]{:S(2)}) copy-start(bf16[1,192,768]{2,1,0:T(8,128)(2,1)} %up_ref.3) | copy-start | bytes 884740
  2.0 5.2 %copy-start.6 = (bf16[1,768,192]{1,2,0:T(8,128)(2,1)S(1)}, bf16[1,768,192]{1,2,0:T(8,128)(2,1)}, u32[]{:S(2)}) copy-start(bf16[1,768,192]{1,2,0:T(8,128)(2,1)} %param.16) | copy-start | bytes 884740
  2.1 5.2 %copy-start.7 = (bf16[1,192,576]{2,1,0:T(8,128)(2,1)S(1)}, bf16[1,192,576]{2,1,0:T(8,128)(2,1)}, u32[]{:S(2)}) copy-start(bf16[1,192,576]{2,1,0:T(8,128)(2,1)} %in_ref.3) | copy-start | bytes 663556
  2.1 5.2 %copy-start.8 = (bf16[1,192,192]{2,1,0:T(8,128)(2,1)S(1)}, bf16[1,192,192]{2,1,0:T(8,128)(2,1)}, u32[]{:S(2)}) copy-start(bf16[1,192,192]{2,1,0:T(8,128)(2,1)} %out_ref.3) | copy-start | bytes 221188
  2.1 5.2 %copy-start.9 = (bf16[1,1920]{1,0:T(2,128)(2,1)S(1)}, bf16[1,1920]{1,0:T(2,128)(2,1)}, u32[]{:S(2)}) copy-start(bf16[1,1920]{1,0:T(2,128)(2,1)} %small_ref.3) | copy-start | bytes 11524
  2.1 5.2 %copy-start.10 = (f32[960]{0:T(1024)S(1)}, f32[960]{0:T(1024)}, u32[]{:S(2)}) copy-start(f32[960]{0:T(1024)} %param.20) | copy-start | bytes 11524
  2.1 5.2 %copy-start.11 = (f32[960]{0:T(1024)S(1)}, f32[960]{0:T(1024)}, u32[]{:S(2)}) copy-start(f32[960]{0:T(1024)} %param.21) | copy-start | bytes 11524
  2.1 1.7 %collective-permute-start = (f32[64,512]{1,0:T(8,128)S(1)}, f32[64,512]{1,0:T(8,128)S(1)}, u32[]{:S(2)}, u32[]{:S(2)}) collective-permute-start(f32[64,512]{1,0:T(8,128)S(1)} %first_part.1), channel_id=1, source_target_pairs={{0,16},{16,0},{1,17},{17,1},{2,18},{18,2},{3,19},{19,3},{4,20},{20... | collective-permute-start | bytes 393224 | tf_op jit(solution)/shard_map/ppermute | solution.py:677
  3.2 3.2 %collective-permute-start.4 = (f32[64,512]{1,0:T(8,128)S(1)}, f32[64,512]{1,0:T(8,128)S(1)}, u32[]{:S(2)}, u32[]{:S(2)}) collective-permute-start(f32[64,512]{1,0:T(8,128)S(1)} %get-tuple-element.43), channel_id=1, source_target_pairs={{0,16},{16,0},{1,17},{17,1},{2,18},{18,2},{3,19},{19,3},{4,20},{20... | collective-permute-start | bytes 393224 | tf_op jit(solution)/shard_map/ppermute | solution.py:679
  3.9 5.1 %collective-permute-start.2 = (f32[64,512]{1,0:T(8,128)S(1)}, f32[64,512]{1,0:T(8,128)S(1)}, u32[]{:S(2)}, u32[]{:S(2)}) collective-permute-start(f32[64,512]{1,0:T(8,128)S(1)} %add.6.order_ref.first_ref), channel_id=1, source_target_pairs={{0,20},{4,28},{8,16},{12,24},{16,8},{20,0},{24,12},{28,4},{1,21},{... | collective-permute-start | bytes 393224 | tf_op jit(solution)/shard_map/ppermute | solution.py:693
  6.3 4.8 %collective-permute-start.5 = (f32[64,512]{1,0:T(8,128)S(1)}, f32[64,512]{1,0:T(8,128)S(1)}, u32[]{:S(2)}, u32[]{:S(2)}) collective-permute-start(f32[64,512]{1,0:T(8,128)S(1)} %add.8.first_ref), channel_id=1, source_target_pairs={{0,20},{4,28},{8,16},{12,24},{16,8},{20,0},{24,12},{28,4},{1,21},{... | collective-permute-start | bytes 393224 | tf_op jit(solution)/shard_map/ppermute | solution.py:693
  7.8 4.6 %collective-permute-start.1 = (f32[6,584,128]{2,1,0:T(8,128)S(1)}, f32[6,584,128]{2,1,0:T(8,128)S(1)}, u32[]{:S(2)}, u32[]{:S(2)}) collective-permute-start(f32[6,584,128]{2,1,0:T(8,128)S(1)} %get-tuple-element.31.send_ref), channel_id=1, source_target_pairs={{0,16},{16,0},{1,17},{17,1},{2,18},{18,2},{3,19},{19,3},{4,20},{20... | collective-permute-start | bytes 5382152 | tf_op jit(solution)/shard_map/ppermute | solution.py:695
  9.0 5.2 %collective-permute-start.3 = (f32[64,512]{1,0:T(8,128)S(1)}, f32[64,512]{1,0:T(8,128)S(1)}, u32[]{:S(2)}, u32[]{:S(2)}) collective-permute-start(f32[64,512]{1,0:T(8,128)S(1)} %add.7.first_ref), channel_id=1, source_target_pairs={{0,24},{4,16},{8,28},{12,20},{16,4},{20,12},{24,0},{28,8},{1,25},{... | collective-permute-start | bytes 393224 | tf_op jit(solution)/shard_map/ppermute | solution.py:699
  11.1 4.5 %collective-permute-start.6 = (f32[64,512]{1,0:T(8,128)S(1)}, f32[64,512]{1,0:T(8,128)S(1)}, u32[]{:S(2)}, u32[]{:S(2)}) collective-permute-start(f32[64,512]{1,0:T(8,128)S(1)} %add.9.first_ref), channel_id=1, source_target_pairs={{0,24},{4,16},{8,28},{12,20},{16,4},{20,12},{24,0},{28,8},{1,25},{... | collective-permute-start | bytes 393224 | tf_op jit(solution)/shard_map/ppermute | solution.py:699
  14.2 1.6 %collective-permute-start.8 = (f32[64,512]{1,0:T(8,128)S(1)}, f32[64,512]{1,0:T(8,128)S(1)}, u32[]{:S(2)}, u32[]{:S(2)}) collective-permute-start(f32[64,512]{1,0:T(8,128)S(1)} %add.10.coeff_ref), channel_id=1, source_target_pairs={{0,16},{16,0},{1,17},{17,1},{2,18},{18,2},{3,19},{19,3},{4,20},{20... | collective-permute-start | bytes 393224 | tf_op jit(solution)/shard_map/ppermute | solution.py:703
  15.6 1.5 %collective-permute-start.7 = (f32[64,512]{1,0:T(8,128)S(1)}, f32[64,512]{1,0:T(8,128)S(1)}, u32[]{:S(2)}, u32[]{:S(2)}) collective-permute-start(f32[64,512]{1,0:T(8,128)S(1)} %add.11.refs_0_), channel_id=1, source_target_pairs={{0,16},{16,0},{1,17},{17,1},{2,18},{18,2},{3,19},{19,3},{4,20},{20... | collective-permute-start | bytes 393224 | tf_op jit(solution)/shard_map/ppermute | solution.py:706

commit v10 on v9

--- a/solution.py
+++ b/solution.py
@@ -133,80 +133,56 @@
     return -(first[:rank] + first[rank:])
 
 
-def first_kernel(basis_hbm, local_hbm, old_hbm, out_ref, *refs):
+def first_kernel(basis_hbm, local_hbm, out_ref, *refs):
     *held, sems = refs
-    basis_ref, local_ref, old_ref = held
-    group = lax.axis_index("group")
     columns = out_ref.shape[1]
     there = pl.ds(pl.multiple_of(side_start(True, CHUNKS * columns), columns), columns)
-    sources = (basis_hbm, local_hbm.at[:, there], old_hbm.at[:, there])
     copies = [
         pltpu.make_async_copy(source, target, sems.at[k])
-        for k, (source, target) in enumerate(zip(sources, held))
+        for k, (source, target) in enumerate(zip((basis_hbm, local_hbm.at[:, there]), held))
     ]
-
-    @pl.when(group == 0)
-    def _():
-        for copy in copies[:2]:
-            copy.start()
-        for copy in copies[:2]:
-            copy.wait()
-        out_ref[...] = local_product(both_parts(basis_ref[...]), local_ref[...])
-
-    @pl.when(group == 1)
-    def _():
-        for copy in copies:
-            copy.start()
-        for copy in copies:
-            copy.wait()
-        out_ref[...] = doubled_product(both_parts(basis_ref[...]), local_ref[...], old_ref[...])
-
-
-def first_part(basis_t, local, old):
+    for copy in copies:
+        copy.start()
+    for copy in copies:
+        copy.wait()
+    basis_ref, local_ref = held
+    out_ref[...] = local_product(both_parts(basis_ref[...]), local_ref[...])
+
+
+def first_part(basis_t, local):
     rank, depth = basis_t.shape
-    block = old.shape[1] // (2 * CHUNKS)
+    block = local.shape[1] // (2 * CHUNKS)
     return pl.pallas_call(
         first_kernel,
-        in_specs=[ANY] * 3,
+        in_specs=[ANY] * 2,
         out_specs=WHOLE,
         out_shape=jax.ShapeDtypeStruct((rank, block), f32),
         scratch_shapes=[
             pltpu.VMEM((rank, depth), f32),
             pltpu.VMEM((depth, block), bf16),
-            pltpu.VMEM((depth, block), f32),
-            pltpu.SemaphoreType.DMA((3,)),
+            pltpu.SemaphoreType.DMA((2,)),
         ],
         compiler_params=pltpu.CompilerParams(vmem_limit_bytes=4 * 2**20),
         cost_estimate=pl.CostEstimate(
-            flops=6 * rank * depth * block, bytes_accessed=6 * depth * block, transcendentals=0
+            flops=2 * 10**9, bytes_accessed=2 * depth * block, transcendentals=0
         ),
         name="first_part",
-    )(*in_hbm((basis_t, local, old)))
+    )(*in_hbm((basis_t, local)))
 
 
 def other_kernel(basis_ref, local_ref, old_ref, rest_ref, *out_refs):
     block = rest_ref.shape[1]
     columns = CHUNKS * block
-    places = [(True, k) for k in range(1, CHUNKS)] + [(False, k) for k in range(CHUNKS)]
-    parts = [
-        (pl.ds(pl.multiple_of(side_start(other, columns) + k * block, block), block), out_ref)
-        for (other, k), out_ref in zip(places, (rest_ref, *out_refs))
-    ]
-
-    def run(multiply):
-        both = both_parts(basis_ref[...])
-        for there, out_ref in parts:
-            out_ref[...] = multiply(both, there)
-
-    group = lax.axis_index("group")
-
-    @pl.when(group == 0)
-    def _():
-        run(lambda both, there: local_product(both, local_ref[:, there]))
-
-    @pl.when(group == 1)
-    def _():
-        run(lambda both, there: doubled_product(both, local_ref[:, there], old_ref[:, there]))
+    both = both_parts(basis_ref[...])
+
+    def there(other, part):
+        start = side_start(other, columns) + part * block
+        return pl.ds(pl.multiple_of(start, block), block)
+
+    rest_ref[...] = local_product(both, local_ref[:, there(True, 1)])
+    for k, out_ref in enumerate(out_refs):
+        here = there(False, k)
+        out_ref[...] = doubled_product(both, local_ref[:, here], old_ref[:, here])
 
 
 def other_parts(basis_t, local, old):
@@ -215,8 +191,8 @@
     return pl.pallas_call(
         other_kernel,
         in_specs=[WHOLE] * 3,
-        out_specs=[WHOLE] * (2 * CHUNKS - 1),
-        out_shape=[jax.ShapeDtypeStruct((rank, block), f32)] * (2 * CHUNKS - 1),
+        out_specs=[WHOLE] * (CHUNKS + 1),
+        out_shape=[jax.ShapeDtypeStruct((rank, block), f32)] * (CHUNKS + 1),
         compiler_params=pltpu.CompilerParams(vmem_limit_bytes=4 * 2**20),
         cost_estimate=pl.CostEstimate(
             flops=10**10, bytes_accessed=18 * depth * block, transcendentals=0
@@ -674,7 +650,7 @@
     axes = ("group", "shard")
 
     embed = (basis.T, embed_local[0], embed_old)
-    theirs = [lax.ppermute(first_part(*embed), "group", swap)]
+    theirs = [lax.ppermute(first_part(*embed[:2]), "group", swap)]
     late, *mine = other_parts(*embed)
     theirs.append(lax.ppermute(late, "group", swap))
 

time: 18.3 us -> 18.3 us (level)
    ppermute x1, starting transfers between devices: 0.75 us -> 0.52 us  [paired(): theirs = [lax.ppermute(first_part(*embed[:2]), 'group', swap)]]
where the time goes in v10:
time: 18.3 us; the launch traced here: 18.1 us
  starting transfers between devices  8.84 us (48%)
  Pallas kernels  6.56 us (36%)
  waiting for transfers between devices  1.76 us (10%)
  between operations  0.87 us (5%)
    ppermute x2, starting transfers between devices, paired(): moving = [lax.ppermute(total, axes, first) for total in totals]  3.44 us
    ppermute x2, starting transfers between devices, paired(): moving = [lax.ppermute(total, axes, second) for total in totals]  3.36 us
    pallas_call x2, Pallas kernels, embed_pieces(): pl.pallas_call(functools.partial(embed_kernel, pieces, ready), in_specs=[...  2.24 us
    pallas_call x1, Pallas kernels, dense_after(): pl.pallas_call(after_kernel, in_specs=[WHOLE] * 11 + [ANY], out_specs=[AN...  1.81 us
    pallas_call x1, Pallas kernels, first_part(): pl.pallas_call(first_kernel, in_specs=[ANY] * 2, out_specs=WHOLE, out_sha...  1.31 us
    ppermute x2, waiting for transfers between devices, paired(): moving = [lax.ppermute(total, axes, first) for total in totals]  0.85 us
    ppermute x1, starting transfers between devices, paired(): rest = [lax.ppermute(own[0], 'group', swap)]  0.66 us
    pallas_call x1, Pallas kernels, dense_before(): pl.pallas_call(before_kernel, in_specs=[ANY] + [WHOLE] * 10, out_specs=[W...  0.53 us
  transfers between devices with their start and end apart: 9, of which 4 were waited for; matrix products, arithmetic and copies ran while one was open for 0% of the time, Pallas kernels for 23%

profile of v10, /device:TPU:0, one launch (start us, length us, event | category | flops | bytes accessed | tf_op | source)
XLA Modules:
  0.0 18.1 jit_solution(9266849804686602197)
XLA Ops:
  0.7 1.3 %first_part.1 = f32[64,512]{1,0:T(8,128)S(1)} custom-call(f32[64,192]{1,0:T(8,128)} %bitcast.18, bf16[192,2048]{1,0:T(8,128)(2,1)} %bitcast.14), custom_call_target="tpu_custom_call" | custom-call | flops 2000000000 | bytes 196608 | tf_op jit(solution)/shard_map/first_part/pallas_call | solution.py:155
  2.0 0.0 copy-start.1
  2.0 0.0 copy-start.2
  2.0 0.0 copy-start.4
  2.0 0.0 copy-start.5
  2.0 0.0 copy-start.6
  2.0 0.0 copy-start.7
  2.1 0.0 copy-start.9
  2.1 0.0 copy-start.10
  2.1 0.0 copy-start.11
  2.1 0.5 %collective-permute-start = (f32[64,512]{1,0:T(8,128)S(1)}, f32[64,512]{1,0:T(8,128)S(1)}, u32[]{:S(2)}, u32[]{:S(2)}) collective-permute-start(f32[64,512]{1,0:T(8,128)S(1)} %first_part.1), channel_id=1, source_target_pairs={{0,16},{16,0},{1,17},{17,1},{2,18},{18,2},{3,19},{19,3},{4,20},{20... | collective-permute-start | bytes 393224 | tf_op jit(solution)/shard_map/ppermute | solution.py:653
  2.6 0.4 %other_parts.1 = (f32[64,512]{1,0:T(8,128)S(1)}, f32[64,512]{1,0:T(8,128)S(1)}, f32[64,512]{1,0:T(8,128)S(1)}) custom-call(f32[64,192]{1,0:T(8,128)S(1)} %bitcast.19, bf16[192,2048]{1,0:T(8,128)(2,1)S(1)} %bitcast.15, f32[192,2048]{1,0:T(8,128)S(1)} %copy-done), custom_call_target="tpu_custom_call" | custom-call | flops 10000000000 | bytes 1769472 | tf_op jit(solution)/shard_map/other_parts/pallas_call | solution.py:191
  3.0 0.3 %collective-permute-start.4 = (f32[64,512]{1,0:T(8,128)S(1)}, f32[64,512]{1,0:T(8,128)S(1)}, u32[]{:S(2)}, u32[]{:S(2)}) collective-permute-start(f32[64,512]{1,0:T(8,128)S(1)} %get-tuple-element.43), channel_id=1, source_target_pairs={{0,16},{16,0},{1,17},{17,1},{2,18},{18,2},{3,19},{19,3},{4,20},{20... | collective-permute-start | bytes 393224 | tf_op jit(solution)/shard_map/ppermute | solution.py:655
  3.3 0.3 %collective-permute-done.second_ref = f32[64,512]{1,0:T(8,128)S(1)} collective-permute-done((f32[64,512]{1,0:T(8,128)S(1)}, f32[64,512]{1,0:T(8,128)S(1)}, u32[]{:S(2)}, u32[]{:S(2)}) %collective-permute-start) | collective-permute-done | bytes 131104 | tf_op jit(solution)/shard_map/ppermute | solution.py:653
  3.6 2.7 %collective-permute-start.2 = (f32[64,512]{1,0:T(8,128)S(1)}, f32[64,512]{1,0:T(8,128)S(1)}, u32[]{:S(2)}, u32[]{:S(2)}) collective-permute-start(f32[64,512]{1,0:T(8,128)S(1)} %add.6.order_ref.first_ref), channel_id=1, source_target_pairs={{0,20},{4,28},{8,16},{12,24},{16,8},{20,0},{24,12},{28,4},{1,21},{... | collective-permute-start | bytes 393224 | tf_op jit(solution)/shard_map/ppermute | solution.py:669
  6.3 0.0 collective-permute-done.4.second_ref
  6.3 0.8 %collective-permute-start.5 = (f32[64,512]{1,0:T(8,128)S(1)}, f32[64,512]{1,0:T(8,128)S(1)}, u32[]{:S(2)}, u32[]{:S(2)}) collective-permute-start(f32[64,512]{1,0:T(8,128)S(1)} %add.8.first_ref), channel_id=1, source_target_pairs={{0,20},{4,28},{8,16},{12,24},{16,8},{20,0},{24,12},{28,4},{1,21},{... | collective-permute-start | bytes 393224 | tf_op jit(solution)/shard_map/ppermute | solution.py:669
  7.1 0.5 %dense_before.1 = (f32[6,584,128]{2,1,0:T(8,128)S(1)}, bf16[192,192]{1,0:T(8,128)(2,1)S(1)}) custom-call(f32[64,512]{1,0:T(8,128)S(1)} %add.6.order_ref.first_ref, f32[64,192]{1,0:T(8,128)S(1)} %bitcast.20, bf16[1,192,576]{2,1,0:T(8,128)(2,1)S(1)} %copy-done.6, bf16[1,192,192]{2,1,0:T(8,128)(2,1)S(1)} %copy-done.7, bf16[1,192,768]{2,1,0:T(8,128)(2,1)S(1)} %copy-done.4, ...), custom_call_target="tpu_custom_call" | custom-call | flops 8847360000 | bytes 4423680 | tf_op jit(solution)/shard_map/dense_before/pallas_call | solution.py:584
  7.7 0.4 %collective-permute-start.1 = (f32[6,584,128]{2,1,0:T(8,128)S(1)}, f32[6,584,128]{2,1,0:T(8,128)S(1)}, u32[]{:S(2)}, u32[]{:S(2)}) collective-permute-start(f32[6,584,128]{2,1,0:T(8,128)S(1)} %get-tuple-element.31.send_ref), channel_id=1, source_target_pairs={{0,16},{16,0},{1,17},{17,1},{2,18},{18,2},{3,19},{19,3},{4,20},{20... | collective-permute-start | bytes 5382152 | tf_op jit(solution)/shard_map/ppermute | solution.py:671
  8.1 0.8 %collective-permute-done.2.second_ref = f32[64,512]{1,0:T(8,128)S(1)} collective-permute-done((f32[64,512]{1,0:T(8,128)S(1)}, f32[64,512]{1,0:T(8,128)S(1)}, u32[]{:S(2)}, u32[]{:S(2)}) %collective-permute-start.2) | collective-permute-done | bytes 131104 | tf_op jit(solution)/shard_map/ppermute | solution.py:669
  9.0 2.1 %collective-permute-start.3 = (f32[64,512]{1,0:T(8,128)S(1)}, f32[64,512]{1,0:T(8,128)S(1)}, u32[]{:S(2)}, u32[]{:S(2)}) collective-permute-start(f32[64,512]{1,0:T(8,128)S(1)} %add.7.first_ref), channel_id=1, source_target_pairs={{0,24},{4,16},{8,28},{12,20},{16,4},{20,12},{24,0},{28,8},{1,25},{... | collective-permute-start | bytes 393224 | tf_op jit(solution)/shard_map/ppermute | solution.py:675
  11.1 1.2 %collective-permute-start.6 = (f32[64,512]{1,0:T(8,128)S(1)}, f32[64,512]{1,0:T(8,128)S(1)}, u32[]{:S(2)}, u32[]{:S(2)}) collective-permute-start(f32[64,512]{1,0:T(8,128)S(1)} %add.9.first_ref), channel_id=1, source_target_pairs={{0,24},{4,16},{8,28},{12,20},{16,4},{20,12},{24,0},{28,8},{1,25},{... | collective-permute-start | bytes 393224 | tf_op jit(solution)/shard_map/ppermute | solution.py:675
  12.3 0.0 collective-permute-done.1.recv_ref
  12.3 1.8 %dense_after.1 = (f32[192,576]{1,0:T(8,128)}, f32[192,192]{1,0:T(8,128)}, f32[192,768]{1,0:T(8,128)}, f32[192,768]{1,0:T(8,128)}, f32[1728,128]{1,0:T(8,128)}, /...) custom-call(f32[6,584,128]{2,1,0:T(8,128)S(1)} %collective-permute-done.1.recv_ref, ...), custom_call_target="tpu_custom_call" | custom-call | flops 8847360000 | bytes 5898240 | tf_op jit(solution)/shard_map/dense_after/pallas_call | solution.py:605
  14.2 0.0 collective-permute-done.3.second_ref
  14.2 0.7 %collective-permute-start.8 = (f32[64,512]{1,0:T(8,128)S(1)}, f32[64,512]{1,0:T(8,128)S(1)}, u32[]{:S(2)}, u32[]{:S(2)}) collective-permute-start(f32[64,512]{1,0:T(8,128)S(1)} %add.10.coeff_ref), channel_id=1, source_target_pairs={{0,16},{16,0},{1,17},{17,1},{2,18},{18,2},{3,19},{19,3},{4,20},{20... | collective-permute-start | bytes 393224 | tf_op jit(solution)/shard_map/ppermute | solution.py:679
  14.9 0.2 %embed_early.1 = (f32[192,512]{1,0:T(8,128)S(1)}, f32[64,512]{1,0:T(8,128)S(1)}) custom-call(bf16[192,192]{1,0:T(8,128)(2,1)S(1)} %get-tuple-element.40.stack_ref, f32[64,2048]{1,0:T(8,128)S(1)} %get-tuple-element.41.moment_ref, f32[192,2048]{1,0:T(8,128)S(1)} %copy-done, f32[64,512]{1,0:T(8,128)S(1)} %add.10.coeff_ref), custom_call_target="tpu_custom_call" | custom-call | flops 37748736 | bytes 786432 | tf_op jit(solution)/shard_map/embed_early/pallas_call | solution.py:241
  15.1 0.5 %collective-permute-done.6.second_ref = f32[64,512]{1,0:T(8,128)S(1)} collective-permute-done((f32[64,512]{1,0:T(8,128)S(1)}, f32[64,512]{1,0:T(8,128)S(1)}, u32[]{:S(2)}, u32[]{:S(2)}) %collective-permute-start.6) | collective-permute-done | bytes 131104 | tf_op jit(solution)/shard_map/ppermute | solution.py:675
  15.6 0.2 collective-permute-start.7
  15.8 0.1 collective-permute-done.8.refs_1_
  15.8 1.2 %embed_pieces.2 = (f32[192,2048]{1,0:T(8,128)}, f32[64,2048]{1,0:T(8,128)}) custom-call(bf16[192,192]{1,0:T(8,128)(2,1)S(1)} %get-tuple-element.40.stack_ref, f32[64,2048]{1,0:T(8,128)S(1)} %get-tuple-element.41.moment_ref, f32[192,2048]{1,0:T(8,128)S(1)} %copy-done, f32[64,512]{1,0:T(8,128)S(1)} %add.11.refs_0_, ...), custom_call_target="tpu_custom_call" | custom-call | flops 75497472 | bytes 1572864 | tf_op jit(solution)/shard_map/embed_pieces/pallas_call | solution.py:291
  17.1 1.0 %embed_pieces.3 = (f32[192,2048]{1,0:T(8,128)}, f32[64,2048]{1,0:T(8,128)}) custom-call(bf16[192,192]{1,0:T(8,128)(2,1)S(1)} %get-tuple-element.40.stack_ref, f32[64,2048]{1,0:T(8,128)S(1)} %get-tuple-element.41.moment_ref, f32[192,2048]{1,0:T(8,128)S(1)} %copy-done, ...), custom_call_target="tpu_custom_call", output_to_operand_aliasing={{0}: (4, {}), {1}: (5, {})} | custom-call | flops 37748736 | bytes 786432 | tf_op jit(solution)/shard_map/embed_pieces/pallas_call | solution.py:291
  (23 shorter events, 0.1 us)
Async XLA Ops:
  0.6 2.0 %copy-start = (f32[192,2048]{1,0:T(8,128)S(1)}, f32[192,2048]{1,0:T(8,128)}, u32[]{:S(2)}) copy-start(f32[192,2048]{1,0:T(8,128)} %old_ref.7) | copy-start | bytes 4718596
  0.7 2.0 %copy-start.3 = (bf16[1,192,2048]{2,1,0:T(8,128)(2,1)S(1)}, bf16[1,192,2048]{2,1,0:T(8,128)(2,1)}, u32[]{:S(2)}) copy-start(bf16[1,192,2048]{2,1,0:T(8,128)(2,1)} %param.22) | copy-start | bytes 2359300
  0.7 2.0 %copy-start.8 = (f32[192,64]{0,1:T(8,128)S(1)}, f32[192,64]{0,1:T(8,128)}, u32[]{:S(2)}) copy-start(f32[192,64]{0,1:T(8,128)} %param.24) | copy-start | bytes 147460
  2.0 5.1 %copy-start.1 = (f32[1,221184]{1,0:T(1,128)S(1)}, f32[1,221184]{1,0:T(1,128)}, u32[]{:S(2)}) copy-start(f32[1,221184]{1,0:T(1,128)} %param.18) | copy-start | bytes 2654212
  2.0 5.1 %copy-start.2 = (f32[1,221184]{1,0:T(1,128)S(1)}, f32[1,221184]{1,0:T(1,128)}, u32[]{:S(2)}) copy-start(f32[1,221184]{1,0:T(1,128)} %param.19) | copy-start | bytes 2654212
  2.0 5.1 %copy-start.4 = (bf16[1,192,768]{2,1,0:T(8,128)(2,1)S(1)}, bf16[1,192,768]{2,1,0:T(8,128)(2,1)}, u32[]{:S(2)}) copy-start(bf16[1,192,768]{2,1,0:T(8,128)(2,1)} %up_ref.3) | copy-start | bytes 884740
  2.0 5.1 %copy-start.5 = (bf16[1,768,192]{1,2,0:T(8,128)(2,1)S(1)}, bf16[1,768,192]{1,2,0:T(8,128)(2,1)}, u32[]{:S(2)}) copy-start(bf16[1,768,192]{1,2,0:T(8,128)(2,1)} %param.16) | copy-start | bytes 884740
  2.0 5.1 %copy-start.6 = (bf16[1,192,576]{2,1,0:T(8,128)(2,1)S(1)}, bf16[1,192,576]{2,1,0:T(8,128)(2,1)}, u32[]{:S(2)}) copy-start(bf16[1,192,576]{2,1,0:T(8,128)(2,1)} %in_ref.3) | copy-start | bytes 663556
  2.0 5.1 %copy-start.7 = (bf16[1,192,192]{2,1,0:T(8,128)(2,1)S(1)}, bf16[1,192,192]{2,1,0:T(8,128)(2,1)}, u32[]{:S(2)}) copy-start(bf16[1,192,192]{2,1,0:T(8,128)(2,1)} %out_ref.3) | copy-start | bytes 221188
  2.1 5.1 %copy-start.9 = (bf16[1,1920]{1,0:T(2,128)(2,1)S(1)}, bf16[1,1920]{1,0:T(2,128)(2,1)}, u32[]{:S(2)}) copy-start(bf16[1,1920]{1,0:T(2,128)(2,1)} %small_ref.3) | copy-start | bytes 11524
  2.1 5.1 %copy-start.10 = (f32[960]{0:T(1024)S(1)}, f32[960]{0:T(1024)}, u32[]{:S(2)}) copy-start(f32[960]{0:T(1024)} %param.20) | copy-start | bytes 11524
  2.1 5.1 %copy-start.11 = (f32[960]{0:T(1024)S(1)}, f32[960]{0:T(1024)}, u32[]{:S(2)}) copy-start(f32[960]{0:T(1024)} %param.21) | copy-start | bytes 11524
  2.1 1.5 %collective-permute-start = (f32[64,512]{1,0:T(8,128)S(1)}, f32[64,512]{1,0:T(8,128)S(1)}, u32[]{:S(2)}, u32[]{:S(2)}) collective-permute-start(f32[64,512]{1,0:T(8,128)S(1)} %first_part.1), channel_id=1, source_target_pairs={{0,16},{16,0},{1,17},{17,1},{2,18},{18,2},{3,19},{19,3},{4,20},{20... | collective-permute-start | bytes 393224 | tf_op jit(solution)/shard_map/ppermute | solution.py:653
  3.0 3.3 %collective-permute-start.4 = (f32[64,512]{1,0:T(8,128)S(1)}, f32[64,512]{1,0:T(8,128)S(1)}, u32[]{:S(2)}, u32[]{:S(2)}) collective-permute-start(f32[64,512]{1,0:T(8,128)S(1)} %get-tuple-element.43), channel_id=1, source_target_pairs={{0,16},{16,0},{1,17},{17,1},{2,18},{18,2},{3,19},{19,3},{4,20},{20... | collective-permute-start | bytes 393224 | tf_op jit(solution)/shard_map/ppermute | solution.py:655
  3.6 5.3 %collective-permute-start.2 = (f32[64,512]{1,0:T(8,128)S(1)}, f32[64,512]{1,0:T(8,128)S(1)}, u32[]{:S(2)}, u32[]{:S(2)}) collective-permute-start(f32[64,512]{1,0:T(8,128)S(1)} %add.6.order_ref.first_ref), channel_id=1, source_target_pairs={{0,20},{4,28},{8,16},{12,24},{16,8},{20,0},{24,12},{28,4},{1,21},{... | collective-permute-start | bytes 393224 | tf_op jit(solution)/shard_map/ppermute | solution.py:669
  6.3 4.8 %collective-permute-start.5 = (f32[64,512]{1,0:T(8,128)S(1)}, f32[64,512]{1,0:T(8,128)S(1)}, u32[]{:S(2)}, u32[]{:S(2)}) collective-permute-start(f32[64,512]{1,0:T(8,128)S(1)} %add.8.first_ref), channel_id=1, source_target_pairs={{0,20},{4,28},{8,16},{12,24},{16,8},{20,0},{24,12},{28,4},{1,21},{... | collective-permute-start | bytes 393224 | tf_op jit(solution)/shard_map/ppermute | solution.py:669
  7.7 4.7 %collective-permute-start.1 = (f32[6,584,128]{2,1,0:T(8,128)S(1)}, f32[6,584,128]{2,1,0:T(8,128)S(1)}, u32[]{:S(2)}, u32[]{:S(2)}) collective-permute-start(f32[6,584,128]{2,1,0:T(8,128)S(1)} %get-tuple-element.31.send_ref), channel_id=1, source_target_pairs={{0,16},{16,0},{1,17},{17,1},{2,18},{18,2},{3,19},{19,3},{4,20},{20... | collective-permute-start | bytes 5382152 | tf_op jit(solution)/shard_map/ppermute | solution.py:671
  9.0 5.2 %collective-permute-start.3 = (f32[64,512]{1,0:T(8,128)S(1)}, f32[64,512]{1,0:T(8,128)S(1)}, u32[]{:S(2)}, u32[]{:S(2)}) collective-permute-start(f32[64,512]{1,0:T(8,128)S(1)} %add.7.first_ref), channel_id=1, source_target_pairs={{0,24},{4,16},{8,28},{12,20},{16,4},{20,12},{24,0},{28,8},{1,25},{... | collective-permute-start | bytes 393224 | tf_op jit(solution)/shard_map/ppermute | solution.py:675
  11.1 4.5 %collective-permute-start.6 = (f32[64,512]{1,0:T(8,128)S(1)}, f32[64,512]{1,0:T(8,128)S(1)}, u32[]{:S(2)}, u32[]{:S(2)}) collective-permute-start(f32[64,512]{1,0:T(8,128)S(1)} %add.9.first_ref), channel_id=1, source_target_pairs={{0,24},{4,16},{8,28},{12,20},{16,4},{20,12},{24,0},{28,8},{1,25},{... | collective-permute-start | bytes 393224 | tf_op jit(solution)/shard_map/ppermute | solution.py:675
  14.2 1.6 %collective-permute-start.8 = (f32[64,512]{1,0:T(8,128)S(1)}, f32[64,512]{1,0:T(8,128)S(1)}, u32[]{:S(2)}, u32[]{:S(2)}) collective-permute-start(f32[64,512]{1,0:T(8,128)S(1)} %add.10.coeff_ref), channel_id=1, source_target_pairs={{0,16},{16,0},{1,17},{17,1},{2,18},{18,2},{3,19},{19,3},{4,20},{20... | collective-permute-start | bytes 393224 | tf_op jit(solution)/shard_map/ppermute | solution.py:679
  15.6 1.5 %collective-permute-start.7 = (f32[64,512]{1,0:T(8,128)S(1)}, f32[64,512]{1,0:T(8,128)S(1)}, u32[]{:S(2)}, u32[]{:S(2)}) collective-permute-start(f32[64,512]{1,0:T(8,128)S(1)} %add.11.refs_0_), channel_id=1, source_target_pairs={{0,16},{16,0},{1,17},{17,1},{2,18},{18,2},{3,19},{19,3},{4,20},{20... | collective-permute-start | bytes 393224 | tf_op jit(solution)/shard_map/ppermute | solution.py:682

commit v11 on v10

--- a/solution.py
+++ b/solution.py
@@ -217,23 +217,28 @@
     )(first, second, *after)
 
 
-def embed_piece(start, width, coeff, stack_ref, moment_ref, old_ref):
-    there = pl.ds(pl.multiple_of(start, width), width)
-    moved = momentum_coef * moment_ref[:, there] + coeff
+def moved_piece(there, coeff, moment_ref):
+    return momentum_coef * moment_ref[:, there] + coeff
+
+
+def embed_piece(there, coeff, moved, stack_ref, old_ref):
     up_high, up_low = split(coeff + momentum_coef * moved)
     change = jnp.dot(
         stack_ref[...],
         jnp.concatenate([up_high, up_high, up_low], axis=0),
         preferred_element_type=f32,
     )
-    return old_ref[:, there] - outer_rate * change, moved
+    return old_ref[:, there] - outer_rate * change
 
 
 def early_kernel(stack_ref, moment_ref, old_ref, coeff_ref, embed_ref, moved_ref):
+    width = coeff_ref.shape[1]
     start = side_start(False, old_ref.shape[1] // 2)
-    embed_ref[...], moved_ref[...] = embed_piece(
-        start, coeff_ref.shape[1], coeff_ref[...], stack_ref, moment_ref, old_ref
-    )
+    there = pl.ds(pl.multiple_of(start, width), width)
+    coeff = coeff_ref[...]
+    moved = moved_piece(there, coeff, moment_ref)
+    moved_ref[...] = moved
+    embed_ref[...] = embed_piece(there, coeff, moved, stack_ref, old_ref)
 
 
 def embed_early(stack, moment, old, coeff):
@@ -261,25 +266,26 @@
     width = coeffs[0].shape[1]
     copies = []
 
-    def start_of(other, part):
-        return side_start(other, old_ref.shape[1] // 2) + part * width
-
-    def send(start, embed, moved):
-        there = pl.ds(pl.multiple_of(start, width), width)
-        for source, target in ((moved, moved_hbm), (embed, embed_hbm)):
-            copies.append(
-                pltpu.make_async_copy(source, target.at[:, there], sems.at[len(copies)])
-            )
-            copies[-1].start()
+    def place(other, part):
+        start = side_start(other, old_ref.shape[1] // 2) + part * width
+        return pl.ds(pl.multiple_of(start, width), width)
+
+    def send(source, target, there):
+        copies.append(pltpu.make_async_copy(source, target.at[:, there], sems.at[len(copies)]))
+        copies[-1].start()
 
     if ready:
-        send(start_of(*ready), refs[0], refs[1])
+        there = place(*ready)
+        send(refs[0], embed_hbm, there)
+        send(refs[1], moved_hbm, there)
     for k, piece in enumerate(pieces):
-        start = start_of(*piece)
-        embed_ref[k], moved_ref[k] = embed_piece(
-            start, width, coeffs[k][...], stack_ref, moment_ref, old_ref
-        )
-        send(start, embed_ref.at[k], moved_ref.at[k])
+        there = place(*piece)
+        coeff = coeffs[k][...]
+        moved = moved_piece(there, coeff, moment_ref)
+        moved_ref[k] = moved
+        send(moved_ref.at[k], moved_hbm, there)
+        embed_ref[k] = embed_piece(there, coeff, moved, stack_ref, old_ref)
+        send(embed_ref.at[k], embed_hbm, there)
     for copy in copies:
         copy.wait()
 

time: 18.3 us -> 18.3 us (level)
  no operation moved by 1% of the time
where the time goes in v11:
time: 18.3 us; the launch traced here: 18.1 us
  starting transfers between devices  8.84 us (48%)
  Pallas kernels  6.56 us (36%)
  waiting for transfers between devices  1.76 us (10%)
  between operations  0.87 us (5%)
    ppermute x2, starting transfers between devices, paired(): moving = [lax.ppermute(total, axes, first) for total in totals]  3.44 us
    ppermute x2, starting transfers between devices, paired(): moving = [lax.ppermute(total, axes, second) for total in totals]  3.36 us
    pallas_call x2, Pallas kernels, embed_pieces(): pl.pallas_call(functools.partial(embed_kernel, pieces, ready), in_specs=[...  2.24 us
    pallas_call x1, Pallas kernels, dense_after(): pl.pallas_call(after_kernel, in_specs=[WHOLE] * 11 + [ANY], out_specs=[AN...  1.81 us
    pallas_call x1, Pallas kernels, first_part(): pl.pallas_call(first_kernel, in_specs=[ANY] * 2, out_specs=WHOLE, out_sha...  1.31 us
    ppermute x2, waiting for transfers between devices, paired(): moving = [lax.ppermute(total, axes, first) for total in totals]  0.85 us
    ppermute x1, starting transfers between devices, paired(): rest = [lax.ppermute(own[0], 'group', swap)]  0.66 us
    pallas_call x1, Pallas kernels, dense_before(): pl.pallas_call(before_kernel, in_specs=[ANY] + [WHOLE] * 10, out_specs=[W...  0.53 us
  transfers between devices with their start and end apart: 9, of which 4 were waited for; matrix products, arithmetic and copies ran while one was open for 0% of the time, Pallas kernels for 23%

profile of v11, /device:TPU:0, one launch (start us, length us, event | category | flops | bytes accessed | tf_op | source)
XLA Modules:
  0.0 18.1 jit_solution(8261573493912335712)
XLA Ops:
  0.7 1.3 %first_part.1 = f32[64,512]{1,0:T(8,128)S(1)} custom-call(f32[64,192]{1,0:T(8,128)} %bitcast.18, bf16[192,2048]{1,0:T(8,128)(2,1)} %bitcast.14), custom_call_target="tpu_custom_call" | custom-call | flops 2000000000 | bytes 196608 | tf_op jit(solution)/shard_map/first_part/pallas_call | solution.py:155
  2.0 0.0 copy-start.1
  2.0 0.0 copy-start.2
  2.0 0.0 copy-start.4
  2.0 0.0 copy-start.5
  2.0 0.0 copy-start.6
  2.0 0.0 copy-start.7
  2.1 0.0 copy-start.9
  2.1 0.0 copy-start.10
  2.1 0.0 copy-start.11
  2.1 0.5 %collective-permute-start = (f32[64,512]{1,0:T(8,128)S(1)}, f32[64,512]{1,0:T(8,128)S(1)}, u32[]{:S(2)}, u32[]{:S(2)}) collective-permute-start(f32[64,512]{1,0:T(8,128)S(1)} %first_part.1), channel_id=1, source_target_pairs={{0,16},{16,0},{1,17},{17,1},{2,18},{18,2},{3,19},{19,3},{4,20},{20... | collective-permute-start | bytes 393224 | tf_op jit(solution)/shard_map/ppermute | solution.py:659
  2.6 0.4 %other_parts.1 = (f32[64,512]{1,0:T(8,128)S(1)}, f32[64,512]{1,0:T(8,128)S(1)}, f32[64,512]{1,0:T(8,128)S(1)}) custom-call(f32[64,192]{1,0:T(8,128)S(1)} %bitcast.19, bf16[192,2048]{1,0:T(8,128)(2,1)S(1)} %bitcast.15, f32[192,2048]{1,0:T(8,128)S(1)} %copy-done), custom_call_target="tpu_custom_call" | custom-call | flops 10000000000 | bytes 1769472 | tf_op jit(solution)/shard_map/other_parts/pallas_call | solution.py:191
  3.0 0.3 %collective-permute-start.4 = (f32[64,512]{1,0:T(8,128)S(1)}, f32[64,512]{1,0:T(8,128)S(1)}, u32[]{:S(2)}, u32[]{:S(2)}) collective-permute-start(f32[64,512]{1,0:T(8,128)S(1)} %get-tuple-element.43), channel_id=1, source_target_pairs={{0,16},{16,0},{1,17},{17,1},{2,18},{18,2},{3,19},{19,3},{4,20},{20... | collective-permute-start | bytes 393224 | tf_op jit(solution)/shard_map/ppermute | solution.py:661
  3.3 0.3 %collective-permute-done.second_ref = f32[64,512]{1,0:T(8,128)S(1)} collective-permute-done((f32[64,512]{1,0:T(8,128)S(1)}, f32[64,512]{1,0:T(8,128)S(1)}, u32[]{:S(2)}, u32[]{:S(2)}) %collective-permute-start) | collective-permute-done | bytes 131104 | tf_op jit(solution)/shard_map/ppermute | solution.py:659
  3.6 2.7 %collective-permute-start.2 = (f32[64,512]{1,0:T(8,128)S(1)}, f32[64,512]{1,0:T(8,128)S(1)}, u32[]{:S(2)}, u32[]{:S(2)}) collective-permute-start(f32[64,512]{1,0:T(8,128)S(1)} %add.6.order_ref.first_ref), channel_id=1, source_target_pairs={{0,20},{4,28},{8,16},{12,24},{16,8},{20,0},{24,12},{28,4},{1,21},{... | collective-permute-start | bytes 393224 | tf_op jit(solution)/shard_map/ppermute | solution.py:675
  6.3 0.0 collective-permute-done.4.second_ref
  6.3 0.8 %collective-permute-start.5 = (f32[64,512]{1,0:T(8,128)S(1)}, f32[64,512]{1,0:T(8,128)S(1)}, u32[]{:S(2)}, u32[]{:S(2)}) collective-permute-start(f32[64,512]{1,0:T(8,128)S(1)} %add.8.first_ref), channel_id=1, source_target_pairs={{0,20},{4,28},{8,16},{12,24},{16,8},{20,0},{24,12},{28,4},{1,21},{... | collective-permute-start | bytes 393224 | tf_op jit(solution)/shard_map/ppermute | solution.py:675
  7.1 0.5 %dense_before.1 = (f32[6,584,128]{2,1,0:T(8,128)S(1)}, bf16[192,192]{1,0:T(8,128)(2,1)S(1)}) custom-call(f32[64,512]{1,0:T(8,128)S(1)} %add.6.order_ref.first_ref, f32[64,192]{1,0:T(8,128)S(1)} %bitcast.20, bf16[1,192,576]{2,1,0:T(8,128)(2,1)S(1)} %copy-done.6, bf16[1,192,192]{2,1,0:T(8,128)(2,1)S(1)} %copy-done.7, bf16[1,192,768]{2,1,0:T(8,128)(2,1)S(1)} %copy-done.4, ...), custom_call_target="tpu_custom_call" | custom-call | flops 8847360000 | bytes 4423680 | tf_op jit(solution)/shard_map/dense_before/pallas_call | solution.py:590
  7.7 0.4 %collective-permute-start.1 = (f32[6,584,128]{2,1,0:T(8,128)S(1)}, f32[6,584,128]{2,1,0:T(8,128)S(1)}, u32[]{:S(2)}, u32[]{:S(2)}) collective-permute-start(f32[6,584,128]{2,1,0:T(8,128)S(1)} %get-tuple-element.31.send_ref), channel_id=1, source_target_pairs={{0,16},{16,0},{1,17},{17,1},{2,18},{18,2},{3,19},{19,3},{4,20},{20... | collective-permute-start | bytes 5382152 | tf_op jit(solution)/shard_map/ppermute | solution.py:677
  8.1 0.8 %collective-permute-done.2.second_ref = f32[64,512]{1,0:T(8,128)S(1)} collective-permute-done((f32[64,512]{1,0:T(8,128)S(1)}, f32[64,512]{1,0:T(8,128)S(1)}, u32[]{:S(2)}, u32[]{:S(2)}) %collective-permute-start.2) | collective-permute-done | bytes 131104 | tf_op jit(solution)/shard_map/ppermute | solution.py:675
  9.0 2.1 %collective-permute-start.3 = (f32[64,512]{1,0:T(8,128)S(1)}, f32[64,512]{1,0:T(8,128)S(1)}, u32[]{:S(2)}, u32[]{:S(2)}) collective-permute-start(f32[64,512]{1,0:T(8,128)S(1)} %add.7.first_ref), channel_id=1, source_target_pairs={{0,24},{4,16},{8,28},{12,20},{16,4},{20,12},{24,0},{28,8},{1,25},{... | collective-permute-start | bytes 393224 | tf_op jit(solution)/shard_map/ppermute | solution.py:681
  11.1 1.2 %collective-permute-start.6 = (f32[64,512]{1,0:T(8,128)S(1)}, f32[64,512]{1,0:T(8,128)S(1)}, u32[]{:S(2)}, u32[]{:S(2)}) collective-permute-start(f32[64,512]{1,0:T(8,128)S(1)} %add.9.first_ref), channel_id=1, source_target_pairs={{0,24},{4,16},{8,28},{12,20},{16,4},{20,12},{24,0},{28,8},{1,25},{... | collective-permute-start | bytes 393224 | tf_op jit(solution)/shard_map/ppermute | solution.py:681
  12.3 0.0 collective-permute-done.1.recv_ref
  12.3 1.8 %dense_after.1 = (f32[192,576]{1,0:T(8,128)}, f32[192,192]{1,0:T(8,128)}, f32[192,768]{1,0:T(8,128)}, f32[192,768]{1,0:T(8,128)}, f32[1728,128]{1,0:T(8,128)}, /...) custom-call(f32[6,584,128]{2,1,0:T(8,128)S(1)} %collective-permute-done.1.recv_ref, ...), custom_call_target="tpu_custom_call" | custom-call | flops 8847360000 | bytes 5898240 | tf_op jit(solution)/shard_map/dense_after/pallas_call | solution.py:611
  14.2 0.0 collective-permute-done.3.second_ref
  14.2 0.7 %collective-permute-start.8 = (f32[64,512]{1,0:T(8,128)S(1)}, f32[64,512]{1,0:T(8,128)S(1)}, u32[]{:S(2)}, u32[]{:S(2)}) collective-permute-start(f32[64,512]{1,0:T(8,128)S(1)} %add.10.coeff_ref), channel_id=1, source_target_pairs={{0,16},{16,0},{1,17},{17,1},{2,18},{18,2},{3,19},{19,3},{4,20},{20... | collective-permute-start | bytes 393224 | tf_op jit(solution)/shard_map/ppermute | solution.py:685
  14.9 0.2 %embed_early.1 = (f32[192,512]{1,0:T(8,128)S(1)}, f32[64,512]{1,0:T(8,128)S(1)}) custom-call(bf16[192,192]{1,0:T(8,128)(2,1)S(1)} %get-tuple-element.40.stack_ref, f32[64,2048]{1,0:T(8,128)S(1)} %get-tuple-element.41.moment_ref, f32[192,2048]{1,0:T(8,128)S(1)} %copy-done, f32[64,512]{1,0:T(8,128)S(1)} %add.10.coeff_ref), custom_call_target="tpu_custom_call" | custom-call | flops 37748736 | bytes 786432 | tf_op jit(solution)/shard_map/embed_early/pallas_call | solution.py:246
  15.1 0.5 %collective-permute-done.6.second_ref = f32[64,512]{1,0:T(8,128)S(1)} collective-permute-done((f32[64,512]{1,0:T(8,128)S(1)}, f32[64,512]{1,0:T(8,128)S(1)}, u32[]{:S(2)}, u32[]{:S(2)}) %collective-permute-start.6) | collective-permute-done | bytes 131104 | tf_op jit(solution)/shard_map/ppermute | solution.py:681
  15.6 0.2 collective-permute-start.7
  15.8 0.1 collective-permute-done.8.refs_1_
  15.8 1.2 %embed_pieces.2 = (f32[192,2048]{1,0:T(8,128)}, f32[64,2048]{1,0:T(8,128)}) custom-call(bf16[192,192]{1,0:T(8,128)(2,1)S(1)} %get-tuple-element.40.stack_ref, f32[64,2048]{1,0:T(8,128)S(1)} %get-tuple-element.41.moment_ref, f32[192,2048]{1,0:T(8,128)S(1)} %copy-done, f32[64,512]{1,0:T(8,128)S(1)} %add.11.refs_0_, ...), custom_call_target="tpu_custom_call" | custom-call | flops 75497472 | bytes 1572864 | tf_op jit(solution)/shard_map/embed_pieces/pallas_call | solution.py:297
  17.1 1.0 %embed_pieces.3 = (f32[192,2048]{1,0:T(8,128)}, f32[64,2048]{1,0:T(8,128)}) custom-call(bf16[192,192]{1,0:T(8,128)(2,1)S(1)} %get-tuple-element.40.stack_ref, f32[64,2048]{1,0:T(8,128)S(1)} %get-tuple-element.41.moment_ref, f32[192,2048]{1,0:T(8,128)S(1)} %copy-done, ...), custom_call_target="tpu_custom_call", output_to_operand_aliasing={{0}: (4, {}), {1}: (5, {})} | custom-call | flops 37748736 | bytes 786432 | tf_op jit(solution)/shard_map/embed_pieces/pallas_call | solution.py:297
  (23 shorter events, 0.1 us)
Async XLA Ops:
  0.6 2.0 %copy-start = (f32[192,2048]{1,0:T(8,128)S(1)}, f32[192,2048]{1,0:T(8,128)}, u32[]{:S(2)}) copy-start(f32[192,2048]{1,0:T(8,128)} %old_ref.7) | copy-start | bytes 4718596
  0.7 2.0 %copy-start.3 = (bf16[1,192,2048]{2,1,0:T(8,128)(2,1)S(1)}, bf16[1,192,2048]{2,1,0:T(8,128)(2,1)}, u32[]{:S(2)}) copy-start(bf16[1,192,2048]{2,1,0:T(8,128)(2,1)} %param.22) | copy-start | bytes 2359300
  0.7 2.0 %copy-start.8 = (f32[192,64]{0,1:T(8,128)S(1)}, f32[192,64]{0,1:T(8,128)}, u32[]{:S(2)}) copy-start(f32[192,64]{0,1:T(8,128)} %param.24) | copy-start | bytes 147460
  2.0 5.1 %copy-start.1 = (f32[1,221184]{1,0:T(1,128)S(1)}, f32[1,221184]{1,0:T(1,128)}, u32[]{:S(2)}) copy-start(f32[1,221184]{1,0:T(1,128)} %param.18) | copy-start | bytes 2654212
  2.0 5.1 %copy-start.2 = (f32[1,221184]{1,0:T(1,128)S(1)}, f32[1,221184]{1,0:T(1,128)}, u32[]{:S(2)}) copy-start(f32[1,221184]{1,0:T(1,128)} %param.19) | copy-start | bytes 2654212
  2.0 5.1 %copy-start.4 = (bf16[1,192,768]{2,1,0:T(8,128)(2,1)S(1)}, bf16[1,192,768]{2,1,0:T(8,128)(2,1)}, u32[]{:S(2)}) copy-start(bf16[1,192,768]{2,1,0:T(8,128)(2,1)} %up_ref.3) | copy-start | bytes 884740
  2.0 5.1 %copy-start.5 = (bf16[1,768,192]{1,2,0:T(8,128)(2,1)S(1)}, bf16[1,768,192]{1,2,0:T(8,128)(2,1)}, u32[]{:S(2)}) copy-start(bf16[1,768,192]{1,2,0:T(8,128)(2,1)} %param.16) | copy-start | bytes 884740
  2.0 5.1 %copy-start.6 = (bf16[1,192,576]{2,1,0:T(8,128)(2,1)S(1)}, bf16[1,192,576]{2,1,0:T(8,128)(2,1)}, u32[]{:S(2)}) copy-start(bf16[1,192,576]{2,1,0:T(8,128)(2,1)} %in_ref.3) | copy-start | bytes 663556
  2.0 5.1 %copy-start.7 = (bf16[1,192,192]{2,1,0:T(8,128)(2,1)S(1)}, bf16[1,192,192]{2,1,0:T(8,128)(2,1)}, u32[]{:S(2)}) copy-start(bf16[1,192,192]{2,1,0:T(8,128)(2,1)} %out_ref.3) | copy-start | bytes 221188
  2.1 5.1 %copy-start.9 = (bf16[1,1920]{1,0:T(2,128)(2,1)S(1)}, bf16[1,1920]{1,0:T(2,128)(2,1)}, u32[]{:S(2)}) copy-start(bf16[1,1920]{1,0:T(2,128)(2,1)} %small_ref.3) | copy-start | bytes 11524
  2.1 5.1 %copy-start.10 = (f32[960]{0:T(1024)S(1)}, f32[960]{0:T(1024)}, u32[]{:S(2)}) copy-start(f32[960]{0:T(1024)} %param.20) | copy-start | bytes 11524
  2.1 5.1 %copy-start.11 = (f32[960]{0:T(1024)S(1)}, f32[960]{0:T(1024)}, u32[]{:S(2)}) copy-start(f32[960]{0:T(1024)} %param.21) | copy-start | bytes 11524
  2.1 1.5 %collective-permute-start = (f32[64,512]{1,0:T(8,128)S(1)}, f32[64,512]{1,0:T(8,128)S(1)}, u32[]{:S(2)}, u32[]{:S(2)}) collective-permute-start(f32[64,512]{1,0:T(8,128)S(1)} %first_part.1), channel_id=1, source_target_pairs={{0,16},{16,0},{1,17},{17,1},{2,18},{18,2},{3,19},{19,3},{4,20},{20... | collective-permute-start | bytes 393224 | tf_op jit(solution)/shard_map/ppermute | solution.py:659
  3.0 3.3 %collective-permute-start.4 = (f32[64,512]{1,0:T(8,128)S(1)}, f32[64,512]{1,0:T(8,128)S(1)}, u32[]{:S(2)}, u32[]{:S(2)}) collective-permute-start(f32[64,512]{1,0:T(8,128)S(1)} %get-tuple-element.43), channel_id=1, source_target_pairs={{0,16},{16,0},{1,17},{17,1},{2,18},{18,2},{3,19},{19,3},{4,20},{20... | collective-permute-start | bytes 393224 | tf_op jit(solution)/shard_map/ppermute | solution.py:661
  3.6 5.3 %collective-permute-start.2 = (f32[64,512]{1,0:T(8,128)S(1)}, f32[64,512]{1,0:T(8,128)S(1)}, u32[]{:S(2)}, u32[]{:S(2)}) collective-permute-start(f32[64,512]{1,0:T(8,128)S(1)} %add.6.order_ref.first_ref), channel_id=1, source_target_pairs={{0,20},{4,28},{8,16},{12,24},{16,8},{20,0},{24,12},{28,4},{1,21},{... | collective-permute-start | bytes 393224 | tf_op jit(solution)/shard_map/ppermute | solution.py:675
  6.3 4.8 %collective-permute-start.5 = (f32[64,512]{1,0:T(8,128)S(1)}, f32[64,512]{1,0:T(8,128)S(1)}, u32[]{:S(2)}, u32[]{:S(2)}) collective-permute-start(f32[64,512]{1,0:T(8,128)S(1)} %add.8.first_ref), channel_id=1, source_target_pairs={{0,20},{4,28},{8,16},{12,24},{16,8},{20,0},{24,12},{28,4},{1,21},{... | collective-permute-start | bytes 393224 | tf_op jit(solution)/shard_map/ppermute | solution.py:675
  7.7 4.7 %collective-permute-start.1 = (f32[6,584,128]{2,1,0:T(8,128)S(1)}, f32[6,584,128]{2,1,0:T(8,128)S(1)}, u32[]{:S(2)}, u32[]{:S(2)}) collective-permute-start(f32[6,584,128]{2,1,0:T(8,128)S(1)} %get-tuple-element.31.send_ref), channel_id=1, source_target_pairs={{0,16},{16,0},{1,17},{17,1},{2,18},{18,2},{3,19},{19,3},{4,20},{20... | collective-permute-start | bytes 5382152 | tf_op jit(solution)/shard_map/ppermute | solution.py:677
  9.0 5.2 %collective-permute-start.3 = (f32[64,512]{1,0:T(8,128)S(1)}, f32[64,512]{1,0:T(8,128)S(1)}, u32[]{:S(2)}, u32[]{:S(2)}) collective-permute-start(f32[64,512]{1,0:T(8,128)S(1)} %add.7.first_ref), channel_id=1, source_target_pairs={{0,24},{4,16},{8,28},{12,20},{16,4},{20,12},{24,0},{28,8},{1,25},{... | collective-permute-start | bytes 393224 | tf_op jit(solution)/shard_map/ppermute | solution.py:681
  11.1 4.5 %collective-permute-start.6 = (f32[64,512]{1,0:T(8,128)S(1)}, f32[64,512]{1,0:T(8,128)S(1)}, u32[]{:S(2)}, u32[]{:S(2)}) collective-permute-start(f32[64,512]{1,0:T(8,128)S(1)} %add.9.first_ref), channel_id=1, source_target_pairs={{0,24},{4,16},{8,28},{12,20},{16,4},{20,12},{24,0},{28,8},{1,25},{... | collective-permute-start | bytes 393224 | tf_op jit(solution)/shard_map/ppermute | solution.py:681
  14.2 1.6 %collective-permute-start.8 = (f32[64,512]{1,0:T(8,128)S(1)}, f32[64,512]{1,0:T(8,128)S(1)}, u32[]{:S(2)}, u32[]{:S(2)}) collective-permute-start(f32[64,512]{1,0:T(8,128)S(1)} %add.10.coeff_ref), channel_id=1, source_target_pairs={{0,16},{16,0},{1,17},{17,1},{2,18},{18,2},{3,19},{19,3},{4,20},{20... | collective-permute-start | bytes 393224 | tf_op jit(solution)/shard_map/ppermute | solution.py:685
  15.6 1.5 %collective-permute-start.7 = (f32[64,512]{1,0:T(8,128)S(1)}, f32[64,512]{1,0:T(8,128)S(1)}, u32[]{:S(2)}, u32[]{:S(2)}) collective-permute-start(f32[64,512]{1,0:T(8,128)S(1)} %add.11.refs_0_), channel_id=1, source_target_pairs={{0,16},{16,0},{1,17},{17,1},{2,18},{18,2},{3,19},{19,3},{4,20},{20... | collective-permute-start | bytes 393224 | tf_op jit(solution)/shard_map/ppermute | solution.py:688
